TPU v7x, 256 devices: a whole 4x4x8 slice. The times are simulated.
256 devices in a mesh: azim: 64 (over z, x_hi, y), span: 4 (over x_lo, core).
Axes of the slice: x: 4 (x_hi: 2, x_lo: 2; x = x_hi * 2 + x_lo), y: 4, z: 8, core: 2. Of those that a mesh axis runs over, the one named last changes fastest.
Arguments:
- field: float32 [2, 8, 64, 8192], P(None, None, 'span', 'azim'), may hold values from -6 to 6
- positions: float32 [3, 64, 8192], P(None, 'span', 'azim'), may hold values from -1366 to 1366, as said below
- normals: float32 [3, 64, 8192], P(None, 'span', 'azim'), may hold values from -2 to 2, as said below
- areas: float32 [64, 8192], P('span', 'azim'), may hold values from 0.5 to 2
- col_cluster: int32 [64, 4, 64, 2], P('azim', 'span'), may hold values from 0 to 15
- block_count: int32 [64, 4, 64], P('azim', 'span'), may hold values from 0 to 2, as said below
- row_cluster: int32 [64, 4, 64, 2], P('azim', 'span'), may hold values from 0 to 63
- v_factors: float32 [64, 4, 64, 2, 2, 24, 128], P('azim', 'span'), may hold values from -0.5 to 0.5
- u_factors: float32 [64, 4, 64, 2, 2, 24, 128], P('azim', 'span'), may hold values from -0.4375 to 0.4375
Outputs:
- result: float32 [2, 8, 64, 8192], P(None, None, 'span', 'azim')
Inputs may be any that keep to these rules, and one draw needn't show every extreme that they name: `positions`: angles follow the azimuth column and heights the axial row, so that distinct panels lie 0.5 or more apart. `normals`: tangential and axial components lie within half of the radial one. `block_count`: slot k of a sender and receiving sector holds a block when k < the count; the count of a sector with itself is 0, and every sender fills all 2 slots to some sector.
All inputs are finite; a program needn't handle non-finite values.
Results may differ from a plain program's by a relative error of at most 0.0003.
Values sent between devices are 32-bit elements; how exact they have to be, the bound alone decides.
No kernel may reach another device: no remote copies, remote signals or barrier semaphores. Data moves between devices by JAX's collectives and lax.ppermute only.
A program may use at most 64 MiB of HBM per device.

v0:
```python
import functools
import math

import jax
import jax.numpy as jnp
from jax import lax
from jax.experimental import pallas as pl
from jax.experimental.pallas import tpu as pltpu
from jax.sharding import PartitionSpec as P

wavenumber = 0.9
coupling = 1.1
f32 = jnp.float32
bf16 = jnp.bfloat16

SEG = 8
SIN_POLY = (4.44286798, -7.30744541, 3.59480208, -0.78440355)
COS_POLY = (1.41420408, -6.97764206, 5.71523842, -1.72834866)


def split_two(value):
    high = value.astype(bf16)
    return high, (value - high.astype(f32)).astype(bf16)


def dot_nt(left, right):
    return lax.dot_general(left, right, (((1,), (1,)), ((), ())), preferred_element_type=f32)


def segment_swap(value):
    rows = value.shape[1]
    row = lax.broadcasted_iota(jnp.int32, value.shape, 1)
    seg = lax.broadcasted_iota(jnp.int32, value.shape, 2) // SEG
    bit = 1
    while bit < rows:
        row_bit = (row // bit) % 2
        seg_bit = (seg // bit) % 2
        up = jnp.roll(jnp.roll(value, -bit, 1), SEG * bit, 2)
        down = jnp.roll(jnp.roll(value, bit, 1), -SEG * bit, 2)
        value = jnp.where(row_bit == seg_bit, value, jnp.where(row_bit == 0, up, down))
        bit *= 2
    return value


def pack_kernel(field_ref, pos_ref, nrm_ref, area_ref, out_ref, low_ref, high_ref):
    rhs = field_ref.shape[1]
    weight = area_ref[...] * (wavenumber / (2.0 * math.pi) / (4.0 * math.pi))
    parts = [field_ref[c, u] * weight for c in range(2) for u in range(rhs)]
    parts += [pos_ref[i] for i in range(3)] + [nrm_ref[i] for i in range(3)]
    packed = segment_swap(jnp.stack(parts, 0))
    blocks = out_ref.shape[0]
    for q in range(len(parts)):
        out_ref[:, q, :] = packed[q]
        low_ref[:, q, :] = packed[q, : low_ref.shape[0]]
        high_ref[:, q, :] = packed[q, blocks - high_ref.shape[0] :]


def send_kernel(chosen_ref, count_ref, field_ref, v_ref, out_ref, table_ref):
    step = pl.program_id(0)
    peers = out_ref.shape[0]
    rank = v_ref.shape[3]
    cap = v_ref.shape[1]
    width = field_ref.shape[3]

    @pl.when(step == 0)
    def _():
        for row in range(field_ref.shape[2]):
            pair = jnp.concatenate([field_ref[0, :, row, :], field_ref[1, :, row, :]], 1)
            high, low = split_two(pair)
            table_ref[row] = jnp.concatenate([high.astype(f32), low.astype(f32)], 0).astype(bf16)

    lane = lax.broadcasted_iota(jnp.int32, (8, 2 * rank * cap), 1)
    for i in range(peers):
        peer = step * peers + i
        wide = []
        for k in range(cap):
            re, im = v_ref[i, k, 0], v_ref[i, k, 1]
            wide += [jnp.concatenate([re, -im], 1), jnp.concatenate([im, re], 1)]
        high, low = split_two(jnp.concatenate(wide, 0))
        left = jnp.concatenate([table_ref[chosen_ref[peer * cap + k]] for k in range(cap)], 0)
        first = dot_nt(left, high)
        second = dot_nt(left, low)
        total = jnp.zeros((8, 2 * rank * cap), f32)
        for k in range(cap):
            part = first[16 * k : 16 * k + 8] + (first[16 * k + 8 : 16 * k + 16] + second[16 * k : 16 * k + 8])
            here = (lane // (2 * rank) == k) & (k < count_ref[peer])
            total = jnp.where(here, part, total)
        out_ref[i, :, : 2 * rank * cap] = total
        out_ref[i, :, 2 * rank * cap :] = jnp.zeros((8, width - 2 * rank * cap), f32)


def receive_kernel(target_ref, coef_ref, u_ref, out_ref):
    step = pl.program_id(0)
    peers = coef_ref.shape[0]
    cap, rank, width = u_ref.shape[1], u_ref.shape[3], u_ref.shape[4]
    used = 2 * rank * cap

    @pl.when(step == 0)
    def _():
        out_ref[...] = jnp.zeros_like(out_ref)

    coef = coef_ref[...].reshape(peers * 8, width)
    lane = lax.broadcasted_iota(jnp.int32, coef.shape, 1)
    is_im = (lane // rank) % 2 == 1
    real_row = jnp.where(is_im, -coef, coef)
    imag_row = jnp.where(is_im, jnp.roll(coef, rank, 1), jnp.roll(coef, -rank, 1))
    zero = jnp.zeros_like(coef)
    rows = []
    for k in range(cap):
        here = lane // (2 * rank) == k
        rows += [jnp.where(here, real_row, zero), jnp.where(here, imag_row, zero)]
    for i in range(peers):
        left = jnp.concatenate([r[8 * i : 8 * i + 8, :used] for r in rows], 0)
        left_high, left_low = split_two(left)
        high, low = split_two(u_ref[i].reshape(used, width))
        one = jnp.dot(jnp.concatenate([left_high, left_low], 0), high, preferred_element_type=f32)
        two = jnp.dot(left_high, low, preferred_element_type=f32)
        count = left.shape[0]
        total = one[:count] + (one[count:] + two)
        for k in range(cap):
            w = target_ref[(step * peers + i) * cap + k]
            out_ref[w] += total[16 * k : 16 * k + 16]


def near_kernel(left_ref, mid_ref, right_ref, field_ref, out_ref, pos_ref, wide_ref, kern_ref, acc_ref):
    blocks = mid_ref.shape[0]
    halo = left_ref.shape[0]
    window = 2 * halo + 1
    width = mid_ref.shape[2]
    turn = wavenumber / (2.0 * math.pi)

    def block_in(index):
        if index < halo:
            return left_ref.at[index]
        if index < halo + blocks:
            return mid_ref.at[index - halo]
        return right_ref.at[index - halo - blocks]

    origin = mid_ref[blocks // 2, 16:19, 0:1]
    for b in range(blocks + 2 * halo):
        ref = block_in(b)
        pos_ref[b, 0:3, :] = (ref[16:19, :] - origin) * turn
        pos_ref[b, 3:6, :] = ref[19:22, :]
        re, im = ref[0:8, :], ref[8:16, :]
        rows = jnp.concatenate(
            [jnp.concatenate([re, -im], 1), jnp.concatenate([im, re], 1)], 0
        )
        high, low = split_two(rows)
        wide_ref[:, 2 * width * b : 2 * width * (b + 1)] = jnp.concatenate([high, low], 0)

    chunk = 16
    sub = lax.broadcasted_iota(jnp.int32, (chunk, width), 0)
    lane = lax.broadcasted_iota(jnp.int32, (chunk, width), 1)

    def one_block(tb, carry):
        target = jnp.transpose(pos_ref[tb + halo])
        for ch in range(width // chunk):
            rows = slice(ch * chunk, (ch + 1) * chunk)
            tx, ty, tz = (
                jnp.broadcast_to(target[rows, i : i + 1], (chunk, width)) for i in range(3)
            )
            for d in range(window):
                src = pos_ref.at[tb + d]
                dx, dy, dz = tx - src[0:1, :], ty - src[1:2, :], tz - src[2:3, :]
                squared = dx * dx + dy * dy + dz * dz
                if d == halo:
                    self_pair = (sub + ch * chunk) == lane
                    squared = jnp.where(self_pair, 1.0, squared)
                inv = lax.rsqrt(squared)
                turns = squared * inv
                frac = turns - jnp.round(turns)
                z = frac * frac
                s = frac * (SIN_POLY[0] + z * (SIN_POLY[1] + z * (SIN_POLY[2] + z * SIN_POLY[3])))
                c = COS_POLY[0] + z * (COS_POLY[1] + z * (COS_POLY[2] + z * COS_POLY[3]))
                sine = s * c
                cosine = 1.0 - s * s
                if d == halo:
                    inv = jnp.where(self_pair, 0.0, inv)
                if d == 0:
                    inv = jnp.where(lane % SEG >= sub % SEG, inv, 0.0)
                if d == window - 1:
                    inv = jnp.where(lane % SEG <= sub % SEG, inv, 0.0)
                slant = (dx * src[3:4, :] + dy * src[4:5, :] + dz * src[5:6, :]) * inv
                first = (slant * turn) * inv
                second = wavenumber * slant + coupling
                pc, ps = inv * cosine, inv * sine
                k_re = first * pc + second * ps
                k_im = first * ps - second * pc
                for kern, at in ((k_re, 0), (k_im, width)):
                    high, low = split_two(kern)
                    cols = slice(2 * width * d + at, 2 * width * d + at + width)
                    kern_ref[ch * chunk : (ch + 1) * chunk, cols] = high
                    kern_ref[width + ch * chunk : width + (ch + 1) * chunk, cols] = low
        start = pl.multiple_of(tb * (2 * width), 2 * width)
        rhs = wide_ref[:, pl.ds(start, 2 * width * window)]
        prod = dot_nt(kern_ref[...], rhs)
        prod = prod[:width] + prod[width:]
        prod = jnp.transpose(prod)
        acc_ref[:, pl.ds(tb, 1), :] = (prod[:16] + prod[16:])[:, None, :]
        return carry

    lax.fori_loop(0, blocks, one_block, 0)
    swapped = segment_swap(acc_ref[...])
    rhs_count = field_ref.shape[1]
    for c in range(2):
        for u in range(rhs_count):
            out_ref[c, u] = swapped[c * rhs_count + u] + 0.5 * field_ref[c, u]


def whole(shape):
    return pl.BlockSpec(shape, lambda *_: (0,) * len(shape))


def run_pack(field, positions, normals, areas):
    rows, width = areas.shape
    blocks = width // SEG
    halo = blocks // 4
    shapes = [(blocks, 24, width), (halo, 24, width), (halo, 24, width)]
    return pl.pallas_call(
        pack_kernel,
        out_shape=[jax.ShapeDtypeStruct(s, f32) for s in shapes],
        name="pack",
    )(field, positions, normals, areas)


def run_send(chosen, counts, field, v):
    peers, cap, _, rank, width = v.shape
    step = 8
    grid_spec = pltpu.PrefetchScalarGridSpec(
        num_scalar_prefetch=2,
        grid=(peers // step,),
        in_specs=[
            pl.BlockSpec(field.shape, lambda i, *_: (0, 0, 0, 0)),
            pl.BlockSpec((step, cap, 2, rank, width), lambda i, *_: (i, 0, 0, 0, 0)),
        ],
        out_specs=pl.BlockSpec((step, 8, width), lambda i, *_: (i, 0, 0)),
        scratch_shapes=[pltpu.VMEM((field.shape[2], 16, 2 * width), bf16)],
    )
    return pl.pallas_call(
        send_kernel,
        grid_spec=grid_spec,
        out_shape=jax.ShapeDtypeStruct((peers, 8, width), f32),
        name="send",
    )(chosen, counts, field, v)


def run_receive(targets, coef, u, span_rows):
    peers, cap, _, rank, width = u.shape
    step = 8
    grid_spec = pltpu.PrefetchScalarGridSpec(
        num_scalar_prefetch=1,
        grid=(peers // step,),
        in_specs=[
            pl.BlockSpec((step, 8, width), lambda i, *_: (i, 0, 0)),
            pl.BlockSpec((step, cap, 2, rank, width), lambda i, *_: (i, 0, 0, 0, 0)),
        ],
        out_specs=pl.BlockSpec((span_rows, 16, width), lambda i, *_: (0, 0, 0)),
    )
    return pl.pallas_call(
        receive_kernel,
        grid_spec=grid_spec,
        out_shape=jax.ShapeDtypeStruct((span_rows, 16, width), f32),
        name="receive",
    )(targets, coef, u)


def run_near(left, mid, right, field):
    blocks, _, width = mid.shape
    halo = left.shape[0]
    count = blocks + 2 * halo
    return pl.pallas_call(
        near_kernel,
        out_shape=jax.ShapeDtypeStruct(field.shape, f32),
        scratch_shapes=[
            pltpu.VMEM((count, 8, width), f32),
            pltpu.VMEM((32, 2 * width * count), bf16),
            pltpu.VMEM((2 * width, 2 * width * (2 * halo + 1)), bf16),
            pltpu.VMEM((16, blocks, width), f32),
        ],
        compiler_params=pltpu.CompilerParams(vmem_limit_bytes=40 * 1024 * 1024),
        name="near",
    )(left, mid, right, field)


def shards(
    field, positions, normals, areas, col_cluster, block_count, row_cluster, v_factors, u_factors
):
    azim = lax.axis_size("azim")
    span = lax.axis_size("span")
    span_rows = field.shape[2]
    mid, low, high = run_pack(field, positions, normals, areas)
    forward = [(i, (i + 1) % azim) for i in range(azim)]
    backward = [(b, a) for a, b in forward]
    left = lax.ppermute(high, "azim", forward)
    right = lax.ppermute(low, "azim", backward)
    outgoing = run_send(
        col_cluster.reshape(-1), block_count.reshape(-1), field, v_factors.reshape(v_factors.shape[2:])
    )
    incoming = lax.all_to_all(outgoing, "azim", split_axis=0, concat_axis=0, tiled=True)
    near = run_near(left, mid, right, field)
    rows = run_receive(
        row_cluster.reshape(-1), incoming, u_factors.reshape(u_factors.shape[2:]), span * span_rows
    )
    me = lax.axis_index("span")
    total = lax.dynamic_slice_in_dim(rows, me * span_rows, span_rows, 0)
    for k in range(1, span):
        ring = [(i, (i + k) % span) for i in range(span)]
        other = ((me + k) % span) * span_rows
        piece = lax.dynamic_slice_in_dim(rows, other, span_rows, 0)
        total = total + lax.ppermute(piece, "span", ring)
    return near + total.transpose(1, 0, 2).reshape(near.shape)


def solution(mesh):
    placed = (
        P(None, None, "span", "azim"),
        P(None, "span", "azim"),
        P(None, "span", "azim"),
        P("span", "azim"),
        P("azim", "span", None, None),
        P("azim", "span", None),
        P("azim", "span", None, None),
        P("azim", "span", None, None, None, None, None),
        P("azim", "span", None, None, None, None, None),
    )
    return jax.shard_map(
        shards, mesh=mesh, in_specs=placed, out_specs=P(None, None, "span", "azim"), check_vma=False
    )
```

profile of v0, /device:TPU:1, one launch (start us, length us, event | category | flops | bytes accessed | tf_op | source)
XLA Modules:
  0.0 89.6 jit_solution(2838189536630716815)
XLA Ops:
  0.0 0.0 copy-start.3
  0.0 0.8 copy.14
  0.8 0.7 reshape.19.chosen_ref
  1.4 7.7 %send.1 = f32[64,8,128]{2,1,0:T(8,128)} custom-call(s32[128]{0:T(128)} %reshape.19.chosen_ref, s32[64]{0:T(128)} %bitcast.13, f32[2,8,16,128]{3,2,1,0:T(8,128)} %field_ref.5, f32[64,2,2,24,128]{4,3,2,1,0:T(8,128)} %bitcast.11), custom_call_target="tpu_custom_call" | custom-call | tf_op jit(solution)/shard_map/send/pallas_call | solution.py:239
  9.1 0.0 copy-start
  9.1 15.2 %all-to-all-start = ((f32[64,8,128]{2,1,0:T(8,128)}), f32[64,8,128]{2,1,0:T(8,128)S(1)}, u32[]{:S(2)}, u32[]{:S(2)}) async-start(f32[64,8,128]{2,1,0:T(8,128)} %send.1), calls=%async_computation | async-start | bytes 524288 | tf_op jit(solution)/shard_map/all_to_all | solution.py:299
  24.4 0.0 copy-done.3
  24.4 0.1 copy.13
  24.5 0.7 reshape.18.target_ref
  25.2 11.1 %all-to-all-done.coef_ref = f32[64,8,128]{2,1,0:T(8,128)S(1)} async-done(((f32[64,8,128]{2,1,0:T(8,128)}), f32[64,8,128]{2,1,0:T(8,128)S(1)}, u32[]{:S(2)}, u32[]{:S(2)}) %all-to-all-start) | async-done | bytes 262176 | tf_op jit(solution)/shard_map/all_to_all | solution.py:299
  36.3 0.0 copy-start.2
  36.3 0.7 copy-done.2
  37.0 7.2 %receive.1 = f32[64,16,128]{2,1,0:T(8,128)} custom-call(s32[128]{0:T(128)} %reshape.18.target_ref, f32[64,8,128]{2,1,0:T(8,128)} %copy-done.2, f32[64,2,2,24,128]{4,3,2,1,0:T(8,128)} %bitcast.12), custom_call_target="tpu_custom_call" | custom-call | tf_op jit(solution)/shard_map/receive/pallas_call | solution.py:259
  44.1 1.1 %constant_dynamic-slice_fusion.2 = (f32[16,16,128]{2,1,0:T(8,128)S(1)}, f32[16,16,128]{2,1,0:T(8,128)S(1)}, f32[16,16,128]{2,1,0:T(8,128)S(1)}) fusion(f32[64,16,128]{2,1,0:T(8,128)} %receive.1, s32[]{:T(128)S(6)} %select_n.29, s32[]{:T(128)S(6)} %select_n.33, s32[]{:T(128)S(6)} %select_n.31), kind=kLoop, calls=%fused_computation.4 | loop fusion | bytes 786444 | tf_op jit(solution)/shard_map/dynamic_slice | solution.py:309
  45.2 3.5 %collective-permute-start.2 = (f32[16,16,128]{2,1,0:T(8,128)S(1)}, f32[16,16,128]{2,1,0:T(8,128)S(1)}, u32[]{:S(2)}, u32[]{:S(2)}) collective-permute-start(f32[16,16,128]{2,1,0:T(8,128)S(1)} %get-tuple-element.11), channel_id=1, source_target_pairs={{0,1},{1,2},{2,3},{3,0},{4,5},{5,6},{6,7},{7,4},{8,9},{9,10},{10,1... | collective-permute-start | bytes 393224 | tf_op jit(solution)/shard_map/ppermute | solution.py:310
  48.7 1.2 %collective-permute-start.3 = (f32[16,16,128]{2,1,0:T(8,128)S(1)}, f32[16,16,128]{2,1,0:T(8,128)S(1)}, u32[]{:S(2)}, u32[]{:S(2)}) collective-permute-start(f32[16,16,128]{2,1,0:T(8,128)S(1)} %get-tuple-element.13), channel_id=1, source_target_pairs={{0,2},{1,3},{2,0},{3,1},{4,6},{5,7},{6,4},{7,5},{8,10},{9,11},{10,... | collective-permute-start | bytes 393224 | tf_op jit(solution)/shard_map/ppermute | solution.py:310
  49.9 0.0 collective-permute-start.4
  49.9 2.2 %pack.1 = (f32[16,24,128]{2,1,0:T(8,128)}, f32[4,24,128]{2,1,0:T(8,128)}, f32[4,24,128]{2,1,0:T(8,128)}) custom-call(f32[2,8,16,128]{3,2,1,0:T(8,128)} %field_ref.5, f32[3,16,128]{2,1,0:T(8,128)} %pos_ref.1, f32[3,16,128]{2,1,0:T(8,128)} %nrm_ref.1, f32[16,128]{1,0:T(8,128)} %area_ref.1), custom_call_target="tpu_custom_call" | custom-call | tf_op jit(solution)/shard_map/pack/pallas_call | solution.py:219
  52.1 0.1 collective-permute-start
  52.2 7.1 %collective-permute-start.1 = (f32[4,24,128]{2,1,0:T(8,128)}, f32[4,24,128]{2,1,0:T(8,128)S(1)}, u32[]{:S(2)}, u32[]{:S(2)}) collective-permute-start(f32[4,24,128]{2,1,0:T(8,128)} %get-tuple-element.10), channel_id=1, source_target_pairs={{4,0},{8,4},{12,8},{16,12},{20,16},{24,20},{28,24},{32,28},{36,32}... | collective-permute-start | bytes 147464 | tf_op jit(solution)/shard_map/ppermute | solution.py:295
  59.3 1.7 %collective-permute-done.left_ref = f32[4,24,128]{2,1,0:T(8,128)S(1)} collective-permute-done((f32[4,24,128]{2,1,0:T(8,128)}, f32[4,24,128]{2,1,0:T(8,128)S(1)}, u32[]{:S(2)}, u32[]{:S(2)}) %collective-permute-start) | collective-permute-done | bytes 49184 | tf_op jit(solution)/shard_map/ppermute | solution.py:294
  61.0 0.0 collective-permute-done.1.right_ref
  61.0 0.0 copy-done
  61.0 0.0 copy-start.1
  61.0 0.9 %copy-done.1 = f32[16,24,128]{2,1,0:T(8,128)S(1)} copy-done((f32[16,24,128]{2,1,0:T(8,128)S(1)}, f32[16,24,128]{2,1,0:T(8,128)}, u32[]{:S(2)}) %copy-start.1) | copy-done | bytes 196632
  61.9 26.0 %near.1 = f32[2,8,16,128]{3,2,1,0:T(8,128)S(1)} custom-call(f32[4,24,128]{2,1,0:T(8,128)S(1)} %collective-permute-done.left_ref, f32[16,24,128]{2,1,0:T(8,128)S(1)} %copy-done.1, f32[4,24,128]{2,1,0:T(8,128)S(1)} %collective-permute-done.1.right_ref, f32[2,8,16,128]{3,2,1,0:T(8,128)S(1)} %copy-done), custom_call_target="tpu_custom_call" | custom-call | tf_op jit(solution)/shard_map/near/pallas_call | solution.py:271
  87.9 0.0 collective-permute-done.2
  87.9 0.0 collective-permute-done.3
  87.9 0.0 collective-permute-done.4
  87.9 0.9 %add_bitcast_fusion = f32[2,8,16,128]{3,1,0,2:T(8,128)S(1)} fusion(f32[16,16,128]{2,1,0:T(8,128)S(1)} %collective-permute-done.4, f32[16,16,128]{2,1,0:T(8,128)S(1)} %collective-permute-done.3, f32[16,16,128]{2,1,0:T(8,128)S(1)} %collective-permute-done.2, f32[64,16,128]{2,1,0:T(8,128)} %receive.1, s32[]{:T(128)S(6)} %select_n.27), kind=kLoop, calls=%fused_computation.1 | loop fusion | flops 98304 | bytes 655364 | tf_op jit(solution)/shard_map/reshape | solution.py:311
  88.9 0.7 copy_add_fusion
Async XLA Ops:
  0.0 24.4 %copy-start.3 = (s32[1,1,64,2]{2,3,1,0:T(2,128)S(1)}, s32[1,1,64,2]{2,3,1,0:T(2,128)}, u32[]{:S(2)}) copy-start(s32[1,1,64,2]{2,3,1,0:T(2,128)} %param.15) | copy-start | bytes 1540
  9.1 51.9 %copy-start = (f32[2,8,16,128]{3,2,1,0:T(8,128)S(1)}, f32[2,8,16,128]{3,2,1,0:T(8,128)}, u32[]{:S(2)}) copy-start(f32[2,8,16,128]{3,2,1,0:T(8,128)} %field_ref.5) | copy-start | bytes 393220
  9.1 27.1 %all-to-all-start = ((f32[64,8,128]{2,1,0:T(8,128)}), f32[64,8,128]{2,1,0:T(8,128)S(1)}, u32[]{:S(2)}, u32[]{:S(2)}) async-start(f32[64,8,128]{2,1,0:T(8,128)} %send.1), calls=%async_computation | async-start | bytes 524288 | tf_op jit(solution)/shard_map/all_to_all | solution.py:299
  36.3 0.7 copy-start.2
  45.2 42.7 %collective-permute-start.2 = (f32[16,16,128]{2,1,0:T(8,128)S(1)}, f32[16,16,128]{2,1,0:T(8,128)S(1)}, u32[]{:S(2)}, u32[]{:S(2)}) collective-permute-start(f32[16,16,128]{2,1,0:T(8,128)S(1)} %get-tuple-element.11), channel_id=1, source_target_pairs={{0,1},{1,2},{2,3},{3,0},{4,5},{5,6},{6,7},{7,4},{8,9},{9,10},{10,1... | collective-permute-start | bytes 393224 | tf_op jit(solution)/shard_map/ppermute | solution.py:310
  48.7 39.2 %collective-permute-start.3 = (f32[16,16,128]{2,1,0:T(8,128)S(1)}, f32[16,16,128]{2,1,0:T(8,128)S(1)}, u32[]{:S(2)}, u32[]{:S(2)}) collective-permute-start(f32[16,16,128]{2,1,0:T(8,128)S(1)} %get-tuple-element.13), channel_id=1, source_target_pairs={{0,2},{1,3},{2,0},{3,1},{4,6},{5,7},{6,4},{7,5},{8,10},{9,11},{10,... | collective-permute-start | bytes 393224 | tf_op jit(solution)/shard_map/ppermute | solution.py:310
  49.9 38.0 %collective-permute-start.4 = (f32[16,16,128]{2,1,0:T(8,128)S(1)}, f32[16,16,128]{2,1,0:T(8,128)S(1)}, u32[]{:S(2)}, u32[]{:S(2)}) collective-permute-start(f32[16,16,128]{2,1,0:T(8,128)S(1)} %get-tuple-element.12), channel_id=1, source_target_pairs={{0,3},{1,0},{2,1},{3,2},{4,7},{5,4},{6,5},{7,6},{8,11},{9,8},{10,9... | collective-permute-start | bytes 393224 | tf_op jit(solution)/shard_map/ppermute | solution.py:310
  52.1 8.9 %collective-permute-start = (f32[4,24,128]{2,1,0:T(8,128)}, f32[4,24,128]{2,1,0:T(8,128)S(1)}, u32[]{:S(2)}, u32[]{:S(2)}) collective-permute-start(f32[4,24,128]{2,1,0:T(8,128)} %get-tuple-element.8), channel_id=1, source_target_pairs={{0,4},{4,8},{8,12},{12,16},{16,20},{20,24},{24,28},{28,32},{32,36}... | collective-permute-start | bytes 147464 | tf_op jit(solution)/shard_map/ppermute | solution.py:294
  52.2 8.8 %collective-permute-start.1 = (f32[4,24,128]{2,1,0:T(8,128)}, f32[4,24,128]{2,1,0:T(8,128)S(1)}, u32[]{:S(2)}, u32[]{:S(2)}) collective-permute-start(f32[4,24,128]{2,1,0:T(8,128)} %get-tuple-element.10), channel_id=1, source_target_pairs={{4,0},{8,4},{12,8},{16,12},{20,16},{24,20},{28,24},{32,28},{36,32}... | collective-permute-start | bytes 147464 | tf_op jit(solution)/shard_map/ppermute | solution.py:295
  61.0 0.9 %copy-start.1 = (f32[16,24,128]{2,1,0:T(8,128)S(1)}, f32[16,24,128]{2,1,0:T(8,128)}, u32[]{:S(2)}) copy-start(f32[16,24,128]{2,1,0:T(8,128)} %get-tuple-element.9.mid_ref) | copy-start | bytes 589828
where the time goes:
time: 90.6 us; the launch traced here: 89.6 us
  Pallas kernels  43.1 us (48%)
  starting transfers between devices  27.1 us (30%)
  waiting for transfers between devices  12.8 us (14%)
  local copies, waits for them, and re-layouts  4.86 us (5%)
  other arithmetic  1.65 us (2%)
    pallas_call x1, Pallas kernels, run_near(): pl.pallas_call(near_kernel, out_shape=jax.ShapeDtypeStruct(field.shape, f...  26 us
    all_to_all x1, starting transfers between devices, shards(): lax.all_to_all(outgoing, 'azim', split_axis=0, concat_axis=0, tiled=True)  15.2 us
    all_to_all x1, waiting for transfers between devices, shards(): lax.all_to_all(outgoing, 'azim', split_axis=0, concat_axis=0, tiled=True)  11.1 us
    pallas_call x1, Pallas kernels, run_send(): pl.pallas_call(send_kernel, grid_spec=grid_spec, out_shape=jax.ShapeDtype...  7.68 us
    pallas_call x1, Pallas kernels, run_receive(): pl.pallas_call(receive_kernel, grid_spec=grid_spec, out_shape=jax.ShapeDt...  7.19 us
    ppermute x1, starting transfers between devices, shards(): right = lax.ppermute(low, 'azim', backward)  7.1 us
    ppermute x3, starting transfers between devices, shards(): total = total + lax.ppermute(piece, 'span', ring)  4.7 us
    unnamed x10, local copies, waits for them, and re-layouts  2.5 us
  transfers between devices with their start and end apart: 6, of which 2 were waited for; matrix products, arithmetic and copies ran while one was open for 1% of the time, Pallas kernels for 31%

commit v1 on v0

v1 whole, which is shorter than its diff:
```python
import functools
import math

import jax
import jax.numpy as jnp
from jax import lax
from jax.experimental import pallas as pl
from jax.experimental.pallas import tpu as pltpu
from jax.sharding import PartitionSpec as P

wavenumber = 0.9
coupling = 1.1
f32 = jnp.float32
bf16 = jnp.bfloat16

SEG = 8
SIN_POLY = (4.44286798, -7.30744541, 3.59480208, -0.78440355)
COS_POLY = (1.41420408, -6.97764206, 5.71523842, -1.72834866)


def split_two(value):
    high = value.astype(bf16)
    return high, (value - high.astype(f32)).astype(bf16)


def dot_nt(left, right):
    return lax.dot_general(left, right, (((1,), (1,)), ((), ())), preferred_element_type=f32)


def segment_swap(value):
    rows = value.shape[1]
    row = lax.broadcasted_iota(jnp.int32, value.shape, 1)
    seg = lax.broadcasted_iota(jnp.int32, value.shape, 2) // SEG
    bit = 1
    while bit < rows:
        row_bit = (row // bit) % 2
        seg_bit = (seg // bit) % 2
        up = jnp.roll(jnp.roll(value, -bit, 1), SEG * bit, 2)
        down = jnp.roll(jnp.roll(value, bit, 1), -SEG * bit, 2)
        value = jnp.where(row_bit == seg_bit, value, jnp.where(row_bit == 0, up, down))
        bit *= 2
    return value


def pack_kernel(field_ref, pos_ref, nrm_ref, area_ref, out_ref, low_ref, high_ref):
    rhs = field_ref.shape[1]
    weight = area_ref[...] * (wavenumber / (2.0 * math.pi) / (4.0 * math.pi))
    parts = [field_ref[c, u] * weight for c in range(2) for u in range(rhs)]
    parts += [pos_ref[i] for i in range(3)] + [nrm_ref[i] for i in range(3)]
    packed = segment_swap(jnp.stack(parts, 0))
    blocks = out_ref.shape[0]
    for q in range(len(parts)):
        out_ref[:, q, :] = packed[q]
        low_ref[:, q, :] = packed[q, : low_ref.shape[0]]
        high_ref[:, q, :] = packed[q, blocks - high_ref.shape[0] :]


def send_kernel(chosen_ref, count_ref, field_ref, v_hbm, out_ref, v_ref, table_ref, sems):
    chunks = sems.shape[0]
    peers = out_ref.shape[0] // chunks
    rank = v_ref.shape[3]
    cap = v_ref.shape[1]
    width = out_ref.shape[2]
    span_rows = table_ref.shape[0]

    def fetch(index):
        rows = pl.ds(index * peers, peers)
        return pltpu.make_async_copy(v_hbm.at[rows], v_ref.at[rows], sems.at[index])

    for index in range(chunks):
        fetch(index).start()

    half = field_ref.shape[0] // 2
    for row in range(span_rows):
        pair = jnp.concatenate(
            [field_ref[pl.ds(c * half + row, 8, stride=span_rows), :] for c in range(2)], 1
        )
        high, low = split_two(pair)
        table_ref[row] = jnp.concatenate([high.astype(f32), low.astype(f32)], 0).astype(bf16)

    lane = lax.broadcasted_iota(jnp.int32, (8, 2 * rank * cap), 1)

    def one_chunk(index, carry):
        fetch(index).wait()
        for i in range(peers):
            peer = index * peers + i
            wide = []
            for k in range(cap):
                re, im = v_ref[peer, k, 0], v_ref[peer, k, 1]
                wide += [jnp.concatenate([re, -im], 1), jnp.concatenate([im, re], 1)]
            high, low = split_two(jnp.concatenate(wide, 0))
            left = jnp.concatenate([table_ref[chosen_ref[k, peer]] for k in range(cap)], 0)
            first = dot_nt(left, high)
            second = dot_nt(left, low)
            total = jnp.zeros((8, 2 * rank * cap), f32)
            for k in range(cap):
                at = 16 * k
                part = first[at : at + 8] + (first[at + 8 : at + 16] + second[at : at + 8])
                here = (lane // (2 * rank) == k) & (k < count_ref[0, peer])
                total = jnp.where(here, part, total)
            out_ref[peer, :, : 2 * rank * cap] = total
            out_ref[peer, :, 2 * rank * cap :] = jnp.zeros((8, width - 2 * rank * cap), f32)
        return carry

    lax.fori_loop(0, chunks, one_chunk, 0)


def receive_kernel(target_ref, me_ref, coef_ref, u_ref, *rest):
    outs, acc_ref = rest[:-1], rest[-1]
    span = len(outs)
    count, cap, rank, width = u_ref.shape[0], u_ref.shape[1], u_ref.shape[3], u_ref.shape[4]
    span_rows = outs[0].shape[1]
    used = 2 * rank * cap
    piece = acc_ref.shape[0] // span
    peers = 8
    acc_ref[...] = jnp.zeros_like(acc_ref)
    me = me_ref[0]
    lane = lax.broadcasted_iota(jnp.int32, (peers * 8, width), 1)

    def one_chunk(index, carry):
        coef = coef_ref[pl.ds(index * peers, peers)].reshape(peers * 8, width)
        is_im = (lane // rank) % 2 == 1
        real_row = jnp.where(is_im, -coef, coef)
        imag_row = jnp.where(is_im, jnp.roll(coef, rank, 1), jnp.roll(coef, -rank, 1))
        zero = jnp.zeros_like(coef)
        rows = []
        for k in range(cap):
            here = lane // (2 * rank) == k
            rows += [jnp.where(here, real_row, zero), jnp.where(here, imag_row, zero)]
        for i in range(peers):
            peer = index * peers + i
            left = jnp.concatenate([r[8 * i : 8 * i + 8, :used] for r in rows], 0)
            left_high, left_low = split_two(left)
            high, low = split_two(u_ref[peer].reshape(used, width))
            one = jnp.dot(
                jnp.concatenate([left_high, left_low], 0), high, preferred_element_type=f32
            )
            two = jnp.dot(left_high, low, preferred_element_type=f32)
            many = left.shape[0]
            total = one[:many] + (one[many:] + two)
            for k in range(cap):
                w = target_ref[k, peer]
                place = ((w // span_rows - me + span) % span) * piece + w % span_rows
                at = pl.ds(place, 16, stride=span_rows)
                acc_ref[at, :] += total[16 * k : 16 * k + 16]
        return carry

    lax.fori_loop(0, count // peers, one_chunk, 0)
    for k in range(span):
        outs[k][...] = acc_ref[k * piece : (k + 1) * piece, :].reshape(outs[k].shape)


def near_kernel(begin, count, skip, edge, *refs):
    if edge:
        left_ref, mid_ref, right_ref, done_ref, field_ref = refs[:5]
        out_ref, pos_ref, wide_ref, kern_ref, acc_ref = refs[5:]
    else:
        mid_ref, acc_ref, pos_ref, wide_ref, kern_ref = refs
    blocks = mid_ref.shape[0]
    halo = blocks // 4
    window = 2 * halo + 1
    width = mid_ref.shape[2]
    turn = wavenumber / (2.0 * math.pi)

    def block_in(index):
        if index < halo:
            return left_ref.at[index]
        if index < halo + blocks:
            return mid_ref.at[index - halo]
        return right_ref.at[index - halo - blocks]

    origin = mid_ref[blocks // 2, 16:19, 0:1]
    for b in range(0 if edge else halo, blocks + (2 if edge else 1) * halo):
        ref = block_in(b)
        pos_ref[b, 0:3, :] = (ref[16:19, :] - origin) * turn
        pos_ref[b, 3:6, :] = ref[19:22, :]
        re, im = ref[0:8, :], ref[8:16, :]
        rows = jnp.concatenate(
            [jnp.concatenate([re, -im], 1), jnp.concatenate([im, re], 1)], 0
        )
        high, low = split_two(rows)
        wide_ref[:, 2 * width * b : 2 * width * (b + 1)] = jnp.concatenate([high, low], 0)

    chunk = 16
    sub = lax.broadcasted_iota(jnp.int32, (chunk, width), 0)
    lane = lax.broadcasted_iota(jnp.int32, (chunk, width), 1)

    def one_block(step, carry):
        tb = jnp.where(step < count, step, step + skip) + begin
        target = jnp.transpose(pos_ref[tb + halo])
        for ch in range(width // chunk):
            rows = slice(ch * chunk, (ch + 1) * chunk)
            tx, ty, tz = (
                jnp.broadcast_to(target[rows, i : i + 1], (chunk, width)) for i in range(3)
            )
            for d in range(window):
                src = pos_ref.at[tb + d]
                dx, dy, dz = tx - src[0:1, :], ty - src[1:2, :], tz - src[2:3, :]
                squared = dx * dx + dy * dy + dz * dz
                if d == halo:
                    self_pair = (sub + ch * chunk) == lane
                    squared = jnp.where(self_pair, 1.0, squared)
                inv = lax.rsqrt(squared)
                turns = squared * inv
                frac = turns - jnp.round(turns)
                z = frac * frac
                s = frac * (SIN_POLY[0] + z * (SIN_POLY[1] + z * (SIN_POLY[2] + z * SIN_POLY[3])))
                c = COS_POLY[0] + z * (COS_POLY[1] + z * (COS_POLY[2] + z * COS_POLY[3]))
                sine = s * c
                cosine = 1.0 - s * s
                if d == halo:
                    inv = jnp.where(self_pair, 0.0, inv)
                if d == 0:
                    inv = jnp.where(lane % SEG >= sub % SEG, inv, 0.0)
                if d == window - 1:
                    inv = jnp.where(lane % SEG <= sub % SEG, inv, 0.0)
                slant = (dx * src[3:4, :] + dy * src[4:5, :] + dz * src[5:6, :]) * inv
                first = (slant * turn) * inv
                second = wavenumber * slant + coupling
                pc, ps = inv * cosine, inv * sine
                k_re = first * pc + second * ps
                k_im = first * ps - second * pc
                for kern, at in ((k_re, 0), (k_im, width)):
                    high, low = split_two(kern)
                    cols = slice(2 * width * d + at, 2 * width * d + at + width)
                    kern_ref[ch * chunk : (ch + 1) * chunk, cols] = high
                    kern_ref[width + ch * chunk : width + (ch + 1) * chunk, cols] = low
        start = pl.multiple_of(tb * (2 * width), 2 * width)
        rhs = wide_ref[:, pl.ds(start, 2 * width * window)]
        prod = dot_nt(kern_ref[...], rhs)
        prod = prod[:width] + prod[width:]
        prod = jnp.transpose(prod)
        at = tb if edge else step
        acc_ref[:, pl.ds(at, 1), :] = (prod[:16] + prod[16:])[:, None, :]
        return carry

    lax.fori_loop(0, 2 * count if edge else count, one_block, 0)
    if edge:
        acc_ref[:, count : count + skip, :] = done_ref[...]
        swapped = segment_swap(acc_ref[...])
        rhs_count = field_ref.shape[1]
        for c in range(2):
            for u in range(rhs_count):
                out_ref[c, u] = swapped[c * rhs_count + u] + 0.5 * field_ref[c, u]


def run_pack(field, positions, normals, areas):
    rows, width = areas.shape
    blocks = width // SEG
    halo = blocks // 4
    shapes = [(blocks, 24, width), (halo, 24, width), (halo, 24, width)]
    return pl.pallas_call(
        pack_kernel,
        out_shape=[jax.ShapeDtypeStruct(s, f32) for s in shapes],
        cost_estimate=cost(10**8, 10**6),
        name="pack",
    )(field, positions, normals, areas)


def vmem(count=1):
    return [pl.BlockSpec(memory_space=pltpu.VMEM)] * count


def smem(count=1):
    return [pl.BlockSpec(memory_space=pltpu.SMEM)] * count


def cost(flops, size):
    return pl.CostEstimate(flops=flops, bytes_accessed=size, transcendentals=0)


def run_send(chosen, counts, field, v):
    peers, cap, _, rank, width = v.shape
    rhs, span_rows = field.shape[1:3]
    chunks = 8
    return pl.pallas_call(
        send_kernel,
        in_specs=smem(2) + vmem(1) + [pl.BlockSpec(memory_space=pl.ANY)],
        out_specs=vmem()[0],
        out_shape=jax.ShapeDtypeStruct((peers, 8, width), f32),
        scratch_shapes=[
            pltpu.VMEM(v.shape, f32),
            pltpu.VMEM((span_rows, 16, 2 * width), bf16),
            pltpu.SemaphoreType.DMA((chunks,)),
        ],
        cost_estimate=cost(3 * 10**9, 4 * v.size),
        name="send",
    )(chosen, counts, field.reshape(2 * rhs * span_rows, width), v)


def run_receive(targets, me, coef, u, span, span_rows):
    width = u.shape[4]
    shape = (16, span_rows, width)
    return pl.pallas_call(
        receive_kernel,
        in_specs=smem(2) + vmem(2),
        out_specs=vmem(span),
        out_shape=[jax.ShapeDtypeStruct(shape, f32)] * span,
        scratch_shapes=[pltpu.VMEM((span * 16 * span_rows, width), f32)],
        cost_estimate=cost(3 * 10**9, 4 * u.size),
        name="receive",
    )(targets, me, coef, u)


def near_scratch(blocks, width):
    halo = blocks // 4
    count = blocks + 2 * halo
    return [
        pltpu.VMEM((count, 8, width), f32),
        pltpu.VMEM((32, 2 * width * count), bf16),
        pltpu.VMEM((2 * width, 2 * width * (2 * halo + 1)), bf16),
    ]


def run_near_inner(mid):
    blocks, _, width = mid.shape
    halo = blocks // 4
    count = blocks - 2 * halo
    return pl.pallas_call(
        functools.partial(near_kernel, halo, count, 0, False),
        in_specs=vmem(1),
        out_specs=vmem()[0],
        out_shape=jax.ShapeDtypeStruct((16, count, width), f32),
        scratch_shapes=near_scratch(blocks, width),
        cost_estimate=cost(10**10, 10**6),
        name="near_inner",
    )(mid)


def run_near_edge(left, mid, right, done, field):
    blocks, _, width = mid.shape
    halo = left.shape[0]
    return pl.pallas_call(
        functools.partial(near_kernel, 0, halo, blocks - 2 * halo, True),
        in_specs=vmem(5),
        out_specs=vmem()[0],
        out_shape=jax.ShapeDtypeStruct(field.shape, f32),
        scratch_shapes=near_scratch(blocks, width) + [pltpu.VMEM((16, blocks, width), f32)],
        cost_estimate=cost(10**10, 10**6),
        name="near_edge",
    )(left, mid, right, done, field)


def shards(
    field, positions, normals, areas, col_cluster, block_count, row_cluster, v_factors, u_factors
):
    azim = lax.axis_size("azim")
    span = lax.axis_size("span")
    span_rows = field.shape[2]
    hold = lax.optimization_barrier
    outgoing = run_send(
        col_cluster[0, 0].T, block_count[0], field, v_factors.reshape(v_factors.shape[2:])
    )
    outgoing, positions = hold((outgoing, positions))
    incoming = lax.all_to_all(outgoing, "azim", split_axis=0, concat_axis=0, tiled=True)
    mid, low, high = run_pack(field, positions, normals, areas)
    forward = [(i, (i + 1) % azim) for i in range(azim)]
    backward = [(b, a) for a, b in forward]
    left = lax.ppermute(high, "azim", forward)
    right = lax.ppermute(low, "azim", backward)
    inner = run_near_inner(mid)
    incoming, inner, left, right = hold((incoming, inner, left, right))
    me = lax.axis_index("span").astype(jnp.int32).reshape(1)
    pieces = run_receive(
        row_cluster[0, 0].T, me, incoming, u_factors.reshape(u_factors.shape[2:]), span, span_rows
    )
    mid, *pieces = hold((mid, *pieces))
    total = pieces[0]
    others = []
    for k in range(1, span):
        ring = [(i, (i + k) % span) for i in range(span)]
        others.append(lax.ppermute(pieces[k], "span", ring))
    near = run_near_edge(left, mid, right, inner, field)
    for other in others:
        total = total + other
    return near + total.reshape(near.shape)


def solution(mesh):
    placed = (
        P(None, None, "span", "azim"),
        P(None, "span", "azim"),
        P(None, "span", "azim"),
        P("span", "azim"),
        P("azim", "span", None, None),
        P("azim", "span", None),
        P("azim", "span", None, None),
        P("azim", "span", None, None, None, None, None),
        P("azim", "span", None, None, None, None, None),
    )
    return jax.shard_map(
        shards, mesh=mesh, in_specs=placed, out_specs=P(None, None, "span", "azim"), check_vma=False
    )
```

time: 90.6 us -> 71 us (0.78)
  waiting for transfers between devices: 12.8 us -> 0.02 us
  local copies, waits for them, and re-layouts: 4.86 us -> 0.72 us
  starting transfers between devices: 27.1 us -> 25.2 us
    all_to_all x1, waiting for transfers between devices: 11.1 us -> 0.01 us  [shards(): lax.all_to_all(outgoing, 'azim', split_axis=0, concat_axis=0, tiled=True)]
    ppermute x3, starting transfers between devices: 4.7 us -> 2.87 us  [shards(): others.append(lax.ppermute(pieces[k], 'span', ring))]
    unnamed x10 -> x8, local copies, waits for them, and re-layouts: 2.5 us -> 0.72 us
    ppermute x1, waiting for transfers between devices: 1.68 us -> 0.01 us  [shards(): left = lax.ppermute(high, 'azim', forward)]
    reshape x2 -> x0, local copies, waits for them, and re-layouts: 1.31 us -> none  [the longest x1 0.65 us: shards(): row_cluster.reshape(-1)]
    dynamic_slice x1 -> x0, local copies, waits for them, and re-layouts: 1.06 us -> none  [shards(): piece = lax.dynamic_slice_in_dim(rows, other, span_rows, 0)]
    reshape x1 -> x0, other arithmetic: 0.95 us -> none  [shards(): return near + total.transpose(1, 0, 2).reshape(near.shape)]
    ppermute x1, starting transfers between devices: 0.09 us -> 1.01 us  [shards(): left = lax.ppermute(high, 'azim', forward)]
  transfers between devices with their start and end apart: 6 -> 6, of which waited for: 2 -> 0; matrix products, arithmetic and copies ran while one was open for 1% -> 0% of each run, Pallas kernels for 31% -> 45%
where the time goes in v1:
time: 71 us; the launch traced here: 70.7 us
  Pallas kernels  43.1 us (61%)
  starting transfers between devices  25.2 us (35%)
  other arithmetic  1.62 us (2%)
  local copies, waits for them, and re-layouts  0.72 us (1%)
    all_to_all x1, starting transfers between devices, shards(): lax.all_to_all(outgoing, 'azim', split_axis=0, concat_axis=0, tiled=True)  15.1 us
    pallas_call x1, Pallas kernels, run_near_edge(): pl.pallas_call(functools.partial(near_kernel, 0, halo, blocks - 2 * halo,...  15 us
    pallas_call x1, Pallas kernels, run_near_inner(): pl.pallas_call(functools.partial(near_kernel, halo, count, 0, False), in_...  14.3 us
    ppermute x1, starting transfers between devices, shards(): right = lax.ppermute(low, 'azim', backward)  6.18 us
    pallas_call x1, Pallas kernels, run_receive(): pl.pallas_call(receive_kernel, in_specs=smem(2) + vmem(2), out_specs=vmem...  5.81 us
    pallas_call x1, Pallas kernels, run_send(): pl.pallas_call(send_kernel, in_specs=smem(2) + vmem(1) + [pl.BlockSpec(me...  5.79 us
    ppermute x3, starting transfers between devices, shards(): others.append(lax.ppermute(pieces[k], 'span', ring))  2.87 us
    pallas_call x1, Pallas kernels, run_pack(): pl.pallas_call(pack_kernel, out_shape=[jax.ShapeDtypeStruct(s, f32) for s...  2.2 us
  transfers between devices with their start and end apart: 6, of which 0 were waited for; matrix products, arithmetic and copies ran while one was open for 0% of the time, Pallas kernels for 45%

profile of v1, /device:TPU:1, one launch (start us, length us, event | category | flops | bytes accessed | tf_op | source)
XLA Modules:
  0.0 70.7 jit_solution(9470345314660264097)
XLA Ops:
  0.0 5.8 %send.1 = f32[64,8,128]{2,1,0:T(8,128)} custom-call(s32[2,64]{1,0:T(2,128)} %bitcast.16, s32[1,64]{1,0:T(1,128)} %bitcast.18, f32[256,128]{1,0:T(8,128)} %bitcast.15, f32[64,2,2,24,128]{4,3,2,1,0:T(8,128)} %bitcast.13), custom_call_target="tpu_custom_call" | custom-call | flops 3000000000 | bytes 3145728 | tf_op jit(solution)/shard_map/send/pallas_call | solution.py:276
  5.8 15.1 %all-to-all-start = ((f32[64,8,128]{2,1,0:T(8,128)}), f32[64,8,128]{2,1,0:T(8,128)S(1)}, u32[]{:S(2)}, u32[]{:S(2)}) async-start(f32[64,8,128]{2,1,0:T(8,128)} %send.1), calls=%async_computation | async-start | bytes 524288 | tf_op jit(solution)/shard_map/all_to_all | solution.py:355
  20.9 2.2 %pack.1 = (f32[16,24,128]{2,1,0:T(8,128)}, f32[4,24,128]{2,1,0:T(8,128)}, f32[4,24,128]{2,1,0:T(8,128)}) custom-call(f32[2,8,16,128]{3,2,1,0:T(8,128)} %refs_4_.1, f32[3,16,128]{2,1,0:T(8,128)} %pos_ref, f32[3,16,128]{2,1,0:T(8,128)} %nrm_ref.1, f32[16,128]{1,0:T(8,128)} %area_ref.1), custom_call_target="tpu_custom_call" | custom-call | flops 100000000 | bytes 1000000 | tf_op jit(solution)/shard_map/pack/pallas_call | solution.py:252
  23.1 1.0 %collective-permute-start = (f32[4,24,128]{2,1,0:T(8,128)}, f32[4,24,128]{2,1,0:T(8,128)S(1)}, u32[]{:S(2)}, u32[]{:S(2)}) collective-permute-start(f32[4,24,128]{2,1,0:T(8,128)} %get-tuple-element.26), channel_id=1, source_target_pairs={{0,4},{4,8},{8,12},{12,16},{16,20},{20,24},{24,28},{28,32},{32,36}... | collective-permute-start | bytes 147464 | tf_op jit(solution)/shard_map/ppermute | solution.py:359
  24.1 6.2 %collective-permute-start.1 = (f32[4,24,128]{2,1,0:T(8,128)}, f32[4,24,128]{2,1,0:T(8,128)S(1)}, u32[]{:S(2)}, u32[]{:S(2)}) collective-permute-start(f32[4,24,128]{2,1,0:T(8,128)} %get-tuple-element.27), channel_id=1, source_target_pairs={{4,0},{8,4},{12,8},{16,12},{20,16},{24,20},{28,24},{32,28},{36,32}... | collective-permute-start | bytes 147464 | tf_op jit(solution)/shard_map/ppermute | solution.py:360
  30.3 14.3 %near_inner.1.refs_3_ = f32[16,8,128]{2,1,0:T(8,128)} custom-call(f32[16,24,128]{2,1,0:T(8,128)} %get-tuple-element.34.refs_0_.refs_1_), custom_call_target="tpu_custom_call" | custom-call | flops 10000000000 | bytes 1000000 | tf_op jit(solution)/shard_map/near_inner/pallas_call | solution.py:319
  44.6 0.0 collective-permute-done.refs_0_
  44.7 0.0 copy-start.2
  44.7 0.0 collective-permute-done.1.refs_2_
  44.7 0.0 copy-start.3
  44.7 0.0 all-to-all-done.coef_ref
  44.7 0.0 copy-start
  44.7 0.7 copy-done
  45.4 5.8 %receive.1 = (f32[16,16,128]{2,1,0:T(8,128)}, f32[16,16,128]{2,1,0:T(8,128)}, f32[16,16,128]{2,1,0:T(8,128)}, f32[16,16,128]{2,1,0:T(8,128)}) custom-call(s32[2,64]{1,0:T(2,128)} %bitcast.17, s32[1]{0:T(128)} %bitcast.7.me_ref, f32[64,8,128]{2,1,0:T(8,128)} %copy-done, f32[64,2,2,24,128]{4,3,2,1,0:T(8,128)} %bitcast.14), custom_call_target="tpu_custom_call" | custom-call | flops 3000000000 | bytes 3145728 | tf_op jit(solution)/shard_map/receive/pallas_call | solution.py:294
  51.2 0.0 copy-start.1
  51.2 1.7 %collective-permute-start.2 = (f32[16,16,128]{2,1,0:T(8,128)}, f32[16,16,128]{2,1,0:T(8,128)S(1)}, u32[]{:S(2)}, u32[]{:S(2)}) collective-permute-start(f32[16,16,128]{2,1,0:T(8,128)} %get-tuple-element.38), channel_id=1, source_target_pairs={{0,1},{1,2},{2,3},{3,0},{4,5},{5,6},{6,7},{7,4},{8,9},{9,10},{10,1... | collective-permute-start | bytes 393224 | tf_op jit(solution)/shard_map/ppermute | solution.py:372
  52.9 1.1 %collective-permute-start.3 = (f32[16,16,128]{2,1,0:T(8,128)}, f32[16,16,128]{2,1,0:T(8,128)S(1)}, u32[]{:S(2)}, u32[]{:S(2)}) collective-permute-start(f32[16,16,128]{2,1,0:T(8,128)} %get-tuple-element.39), channel_id=1, source_target_pairs={{0,2},{1,3},{2,0},{3,1},{4,6},{5,7},{6,4},{7,5},{8,10},{9,11},{10,... | collective-permute-start | bytes 393224 | tf_op jit(solution)/shard_map/ppermute | solution.py:372
  54.1 0.0 collective-permute-start.4
  54.1 0.0 copy-done.2
  54.1 0.0 copy-done.3
  54.1 15.0 %near_edge.1 = f32[2,8,16,128]{3,2,1,0:T(8,128)} custom-call(f32[4,24,128]{2,1,0:T(8,128)} %copy-done.2, f32[16,24,128]{2,1,0:T(8,128)} %get-tuple-element.34.refs_0_.refs_1_, f32[4,24,128]{2,1,0:T(8,128)} %copy-done.3, f32[16,8,128]{2,1,0:T(8,128)} %near_inner.1.refs_3_, f32[2,8,16,128]{3,2,1,0:T(8,128)} %refs_4_.1), custom_call_target="tpu_custom_call" | custom-call | flops 10000000000 | bytes 1000000 | tf_op jit(solution)/shard_map/near_edge/pallas_call | solution.py:333
  69.1 0.0 collective-permute-done.2
  69.1 0.0 collective-permute-done.3
  69.1 0.0 collective-permute-done.4
  69.1 0.0 copy-done.1
  69.1 1.6 %add.15 = f32[2,8,16,128]{3,2,1,0:T(8,128)} add(f32[2,8,16,128]{3,2,1,0:T(8,128)} %near_edge.1, f32[2,8,16,128]{3,2,1,0:T(8,128)S(1)} %bitcast.12) | non-fusion elementwise | flops 32768 | bytes 393216 | tf_op jit(solution)/shard_map/add | solution.py:376
  (1 shorter events, 0.0 us)
Async XLA Ops:
  5.8 38.9 %all-to-all-start = ((f32[64,8,128]{2,1,0:T(8,128)}), f32[64,8,128]{2,1,0:T(8,128)S(1)}, u32[]{:S(2)}, u32[]{:S(2)}) async-start(f32[64,8,128]{2,1,0:T(8,128)} %send.1), calls=%async_computation | async-start | bytes 524288 | tf_op jit(solution)/shard_map/all_to_all | solution.py:355
  23.1 21.5 %collective-permute-start = (f32[4,24,128]{2,1,0:T(8,128)}, f32[4,24,128]{2,1,0:T(8,128)S(1)}, u32[]{:S(2)}, u32[]{:S(2)}) collective-permute-start(f32[4,24,128]{2,1,0:T(8,128)} %get-tuple-element.26), channel_id=1, source_target_pairs={{0,4},{4,8},{8,12},{12,16},{16,20},{20,24},{24,28},{28,32},{32,36}... | collective-permute-start | bytes 147464 | tf_op jit(solution)/shard_map/ppermute | solution.py:359
  24.1 20.5 %collective-permute-start.1 = (f32[4,24,128]{2,1,0:T(8,128)}, f32[4,24,128]{2,1,0:T(8,128)S(1)}, u32[]{:S(2)}, u32[]{:S(2)}) collective-permute-start(f32[4,24,128]{2,1,0:T(8,128)} %get-tuple-element.27), channel_id=1, source_target_pairs={{4,0},{8,4},{12,8},{16,12},{20,16},{24,20},{28,24},{32,28},{36,32}... | collective-permute-start | bytes 147464 | tf_op jit(solution)/shard_map/ppermute | solution.py:360
  44.7 9.4 %copy-start.2 = (f32[4,24,128]{2,1,0:T(8,128)}, f32[4,24,128]{2,1,0:T(8,128)S(1)}, u32[]{:S(2)}) copy-start(f32[4,24,128]{2,1,0:T(8,128)S(1)} %collective-permute-done.refs_0_) | copy-start | bytes 147460
  44.7 9.4 %copy-start.3 = (f32[4,24,128]{2,1,0:T(8,128)}, f32[4,24,128]{2,1,0:T(8,128)S(1)}, u32[]{:S(2)}) copy-start(f32[4,24,128]{2,1,0:T(8,128)S(1)} %collective-permute-done.1.refs_2_) | copy-start | bytes 147460
  44.7 0.7 %copy-start = (f32[64,8,128]{2,1,0:T(8,128)}, f32[64,8,128]{2,1,0:T(8,128)S(1)}, u32[]{:S(2)}) copy-start(f32[64,8,128]{2,1,0:T(8,128)S(1)} %all-to-all-done.coef_ref) | copy-start | bytes 786436
  51.2 17.9 %copy-start.1 = (f32[16,16,128]{2,1,0:T(8,128)S(1)}, f32[16,16,128]{2,1,0:T(8,128)}, u32[]{:S(2)}) copy-start(f32[16,16,128]{2,1,0:T(8,128)} %get-tuple-element.37) | copy-start | bytes 393220
  51.2 17.9 %collective-permute-start.2 = (f32[16,16,128]{2,1,0:T(8,128)}, f32[16,16,128]{2,1,0:T(8,128)S(1)}, u32[]{:S(2)}, u32[]{:S(2)}) collective-permute-start(f32[16,16,128]{2,1,0:T(8,128)} %get-tuple-element.38), channel_id=1, source_target_pairs={{0,1},{1,2},{2,3},{3,0},{4,5},{5,6},{6,7},{7,4},{8,9},{9,10},{10,1... | collective-permute-start | bytes 393224 | tf_op jit(solution)/shard_map/ppermute | solution.py:372
  52.9 16.2 %collective-permute-start.3 = (f32[16,16,128]{2,1,0:T(8,128)}, f32[16,16,128]{2,1,0:T(8,128)S(1)}, u32[]{:S(2)}, u32[]{:S(2)}) collective-permute-start(f32[16,16,128]{2,1,0:T(8,128)} %get-tuple-element.39), channel_id=1, source_target_pairs={{0,2},{1,3},{2,0},{3,1},{4,6},{5,7},{6,4},{7,5},{8,10},{9,11},{10,... | collective-permute-start | bytes 393224 | tf_op jit(solution)/shard_map/ppermute | solution.py:372
  54.1 15.0 %collective-permute-start.4 = (f32[16,16,128]{2,1,0:T(8,128)}, f32[16,16,128]{2,1,0:T(8,128)S(1)}, u32[]{:S(2)}, u32[]{:S(2)}) collective-permute-start(f32[16,16,128]{2,1,0:T(8,128)} %get-tuple-element.40), channel_id=1, source_target_pairs={{0,3},{1,0},{2,1},{3,2},{4,7},{5,4},{6,5},{7,6},{8,11},{9,8},{10,9... | collective-permute-start | bytes 393224 | tf_op jit(solution)/shard_map/ppermute | solution.py:372

commit v2 on v1

--- a/solution.py
+++ b/solution.py
@@ -14,13 +14,19 @@
 bf16 = jnp.bfloat16
 
 SEG = 8
-SIN_POLY = (4.44286798, -7.30744541, 3.59480208, -0.78440355)
-COS_POLY = (1.41420408, -6.97764206, 5.71523842, -1.72834866)
+SIN_POLY = (2.2214303951, -0.9131751650, 0.1098397679)
 
 
 def split_two(value):
     high = value.astype(bf16)
     return high, (value - high.astype(f32)).astype(bf16)
+
+
+def split_three(value):
+    high = value.astype(bf16).astype(f32)
+    rest = value - high
+    middle = rest.astype(bf16).astype(f32)
+    return high, middle, rest - middle
 
 
 def dot_nt(left, right):
@@ -42,10 +48,11 @@
     return value
 
 
-def pack_kernel(field_ref, pos_ref, nrm_ref, area_ref, out_ref, low_ref, high_ref):
-    rhs = field_ref.shape[1]
+def pack(field_ref, pos_ref, nrm_ref, area_ref, out_ref, low_ref, high_ref):
+    span_rows, width = area_ref.shape
     weight = area_ref[...] * (wavenumber / (2.0 * math.pi) / (4.0 * math.pi))
-    parts = [field_ref[c, u] * weight for c in range(2) for u in range(rhs)]
+    field = field_ref[...].reshape(field_ref.shape[0] // span_rows, span_rows, width)
+    parts = [field[q] * weight for q in range(field.shape[0])]
     parts += [pos_ref[i] for i in range(3)] + [nrm_ref[i] for i in range(3)]
     packed = segment_swap(jnp.stack(parts, 0))
     blocks = out_ref.shape[0]
@@ -55,7 +62,8 @@
         high_ref[:, q, :] = packed[q, blocks - high_ref.shape[0] :]
 
 
-def send_kernel(chosen_ref, count_ref, field_ref, v_hbm, out_ref, v_ref, table_ref, sems):
+def send_kernel(chosen_ref, count_ref, field_ref, pos_ref, nrm_ref, area_ref, v_hbm, *rest):
+    out_ref, mid_ref, low_ref, high_ref, v_ref, table_ref, sems = rest
     chunks = sems.shape[0]
     peers = out_ref.shape[0] // chunks
     rank = v_ref.shape[3]
@@ -69,6 +77,7 @@
 
     for index in range(chunks):
         fetch(index).start()
+    pack(field_ref, pos_ref, nrm_ref, area_ref, mid_ref, low_ref, high_ref)
 
     half = field_ref.shape[0] // 2
     for row in range(span_rows):
@@ -106,14 +115,15 @@
 
 
 def receive_kernel(target_ref, me_ref, coef_ref, u_ref, *rest):
-    outs, acc_ref = rest[:-1], rest[-1]
+    outs, accs = rest[:-4], rest[-4:]
     span = len(outs)
     count, cap, rank, width = u_ref.shape[0], u_ref.shape[1], u_ref.shape[3], u_ref.shape[4]
     span_rows = outs[0].shape[1]
     used = 2 * rank * cap
-    piece = acc_ref.shape[0] // span
+    piece = accs[0].shape[0] // span
     peers = 8
-    acc_ref[...] = jnp.zeros_like(acc_ref)
+    for acc_ref in accs:
+        acc_ref[...] = jnp.zeros_like(acc_ref)
     me = me_ref[0]
     lane = lax.broadcasted_iota(jnp.int32, (peers * 8, width), 1)
 
@@ -142,20 +152,24 @@
                 w = target_ref[k, peer]
                 place = ((w // span_rows - me + span) % span) * piece + w % span_rows
                 at = pl.ds(place, 16, stride=span_rows)
+                acc_ref = accs[(2 * i + k) % 4]
                 acc_ref[at, :] += total[16 * k : 16 * k + 16]
         return carry
 
     lax.fori_loop(0, count // peers, one_chunk, 0)
     for k in range(span):
-        outs[k][...] = acc_ref[k * piece : (k + 1) * piece, :].reshape(outs[k].shape)
+        at = slice(k * piece, (k + 1) * piece)
+        total = (accs[0][at, :] + accs[1][at, :]) + (accs[2][at, :] + accs[3][at, :])
+        outs[k][...] = total.reshape(outs[k].shape)
 
 
 def near_kernel(begin, count, skip, edge, *refs):
+    scratch = refs[-7:]
+    pos_ref, wide_ref, kern_even, kern_odd, target_ref, source_ref, acc_ref = scratch
     if edge:
-        left_ref, mid_ref, right_ref, done_ref, field_ref = refs[:5]
-        out_ref, pos_ref, wide_ref, kern_ref, acc_ref = refs[5:]
+        left_ref, mid_ref, right_ref, done_ref, field_ref, out_ref = refs[:-7]
     else:
-        mid_ref, acc_ref, pos_ref, wide_ref, kern_ref = refs
+        mid_ref, out_ref = refs[:-7]
     blocks = mid_ref.shape[0]
     halo = blocks // 4
     window = 2 * halo + 1
@@ -170,91 +184,146 @@
         return right_ref.at[index - halo - blocks]
 
     origin = mid_ref[blocks // 2, 16:19, 0:1]
+    row = lax.broadcasted_iota(jnp.int32, (8, width), 0)
     for b in range(0 if edge else halo, blocks + (2 if edge else 1) * halo):
         ref = block_in(b)
-        pos_ref[b, 0:3, :] = (ref[16:19, :] - origin) * turn
-        pos_ref[b, 3:6, :] = ref[19:22, :]
+        pad = jnp.zeros((5, width), f32)
+        pos_ref[b, 0:8, :] = jnp.concatenate([(ref[16:19, :] - origin) * turn, pad], 0)
+        pos_ref[b, 8:16, :] = jnp.concatenate([ref[19:22, :] * wavenumber, pad], 0)
         re, im = ref[0:8, :], ref[8:16, :]
         rows = jnp.concatenate(
             [jnp.concatenate([re, -im], 1), jnp.concatenate([im, re], 1)], 0
         )
         high, low = split_two(rows)
         wide_ref[:, 2 * width * b : 2 * width * (b + 1)] = jnp.concatenate([high, low], 0)
+    sources = window + 1
+    zeros = jnp.zeros((width, 2 * width), bf16)
+    for kern_ref in (kern_even, kern_odd):
+        for part in (0, 2):
+            kern_ref[(part + 1) * width : (part + 2) * width, : 2 * width] = zeros
+            kern_ref[part * width : (part + 1) * width, 2 * width * (sources - 1) :] = zeros
 
     chunk = 16
     sub = lax.broadcasted_iota(jnp.int32, (chunk, width), 0)
     lane = lax.broadcasted_iota(jnp.int32, (chunk, width), 1)
 
-    def one_block(step, carry):
-        tb = jnp.where(step < count, step, step + skip) + begin
-        target = jnp.transpose(pos_ref[tb + halo])
-        for ch in range(width // chunk):
-            rows = slice(ch * chunk, (ch + 1) * chunk)
-            tx, ty, tz = (
-                jnp.broadcast_to(target[rows, i : i + 1], (chunk, width)) for i in range(3)
+    def evaluate(squared, num, at, offset):
+        if offset == 0:
+            self_pair = (sub + at) == lane
+            squared = jnp.where(self_pair, 1.0, squared)
+        inv = lax.rsqrt(squared)
+        turns = squared * inv
+        frac = turns - jnp.round(turns)
+        z = frac * frac
+        s1 = frac * (SIN_POLY[0] + z * (SIN_POLY[1] + z * SIN_POLY[2]))
+        s1_sq = s1 * s1
+        c1_sq = 2.0 - s1_sq
+        s2 = s1 * (c1_sq * lax.rsqrt(c1_sq))
+        c2 = c1_sq - s1_sq
+        sine = s2 * c2
+        cosine = 1.0 - s2 * (s2 + s2)
+        if offset == 0:
+            inv = jnp.where(self_pair, 0.0, inv)
+        if offset == -halo:
+            inv = jnp.where(lane % SEG >= sub % SEG, inv, 0.0)
+        if offset == halo:
+            inv = jnp.where(lane % SEG <= sub % SEG, inv, 0.0)
+        slant = num * inv
+        first = (slant * (turn / wavenumber)) * inv
+        second = slant + coupling
+        pc, ps = inv * cosine, inv * sine
+        return first * pc + second * ps, first * ps - second * pc
+
+    def pair_of(step):
+        return jnp.where(step < count, step, step + skip) + begin
+
+    def prepare(step, carry):
+        tp = pair_of(step)
+        center = pos_ref[2 * tp + halo, 0:8, 8 * SEG - 1 : 8 * SEG]
+
+        def local_of(index):
+            place = pos_ref[2 * tp + index, 0:8, :] - center
+            return place, jnp.sum(place * place, axis=0, keepdims=True)
+
+        for t in range(2):
+            place, norm = local_of(halo + t)
+            high, mid, low = split_three(
+                jnp.where(row < 3, place, jnp.where(row == 3, 1.0, jnp.where(row == 4, norm, 0.0)))
             )
-            for d in range(window):
-                src = pos_ref.at[tb + d]
-                dx, dy, dz = tx - src[0:1, :], ty - src[1:2, :], tz - src[2:3, :]
-                squared = dx * dx + dy * dy + dz * dz
-                if d == halo:
-                    self_pair = (sub + ch * chunk) == lane
-                    squared = jnp.where(self_pair, 1.0, squared)
-                inv = lax.rsqrt(squared)
-                turns = squared * inv
-                frac = turns - jnp.round(turns)
-                z = frac * frac
-                s = frac * (SIN_POLY[0] + z * (SIN_POLY[1] + z * (SIN_POLY[2] + z * SIN_POLY[3])))
-                c = COS_POLY[0] + z * (COS_POLY[1] + z * (COS_POLY[2] + z * COS_POLY[3]))
-                sine = s * c
-                cosine = 1.0 - s * s
-                if d == halo:
-                    inv = jnp.where(self_pair, 0.0, inv)
-                if d == 0:
-                    inv = jnp.where(lane % SEG >= sub % SEG, inv, 0.0)
-                if d == window - 1:
-                    inv = jnp.where(lane % SEG <= sub % SEG, inv, 0.0)
-                slant = (dx * src[3:4, :] + dy * src[4:5, :] + dz * src[5:6, :]) * inv
-                first = (slant * turn) * inv
-                second = wavenumber * slant + coupling
-                pc, ps = inv * cosine, inv * sine
-                k_re = first * pc + second * ps
-                k_im = first * ps - second * pc
-                for kern, at in ((k_re, 0), (k_im, width)):
-                    high, low = split_two(kern)
-                    cols = slice(2 * width * d + at, 2 * width * d + at + width)
-                    kern_ref[ch * chunk : (ch + 1) * chunk, cols] = high
-                    kern_ref[width + ch * chunk : width + (ch + 1) * chunk, cols] = low
-        start = pl.multiple_of(tb * (2 * width), 2 * width)
-        rhs = wide_ref[:, pl.ds(start, 2 * width * window)]
+            rows = jnp.transpose(jnp.concatenate([high, high, mid, high, mid, low], 0))
+            target_ref[step, t * width : (t + 1) * width, :] = rows.astype(bf16)
+        for sb in range(sources):
+            place, norm = local_of(sb)
+            normal = pos_ref[2 * tp + sb, 8:16, :]
+            along = jnp.sum(normal * place, axis=0, keepdims=True)
+            wide = []
+            for rows in (
+                jnp.where(
+                    row < 3, -2.0 * place, jnp.where(row == 3, norm, jnp.where(row == 4, 1.0, 0.0))
+                ),
+                jnp.where(row < 3, normal, jnp.where(row == 3, -along, 0.0)),
+            ):
+                high, mid, low = split_three(rows)
+                wide.append(jnp.concatenate([high, mid, high, low, mid, high], 0))
+            cols = slice(2 * width * sb, 2 * width * (sb + 1))
+            source_ref[step, :, cols] = jnp.concatenate(wide, 1).astype(bf16)
+        return carry
+
+    def pair_kernels(step, kern_ref):
+        for sb in range(sources):
+            start = width if sb == sources - 1 else 0
+            stop = width if sb == 0 else 2 * width
+            gram = jnp.dot(
+                target_ref[step, start:stop, :],
+                source_ref[step, :, 2 * width * sb : 2 * width * (sb + 1)],
+                preferred_element_type=f32,
+            )
+            for at in range(start, stop, chunk):
+                t = at // width
+                part = gram[at - start : at - start + chunk]
+                kern = evaluate(part[:, :width], part[:, width:], at % width, sb - halo - t)
+                for value, shift in zip(kern, (0, width)):
+                    high, low = split_two(value)
+                    cols = slice(2 * width * sb + shift, 2 * width * sb + shift + width)
+                    kern_ref[at : at + chunk, cols] = high
+                    kern_ref[2 * width + at : 2 * width + at + chunk, cols] = low
+
+    def pair_sums(step, slot, kern_ref):
+        start = pl.multiple_of(pair_of(step) * (4 * width), 4 * width)
+        rhs = wide_ref[:, pl.ds(start, 2 * width * sources)]
         prod = dot_nt(kern_ref[...], rhs)
-        prod = prod[:width] + prod[width:]
-        prod = jnp.transpose(prod)
-        at = tb if edge else step
-        acc_ref[:, pl.ds(at, 1), :] = (prod[:16] + prod[16:])[:, None, :]
+        prod = prod[: 2 * width] + prod[2 * width :]
+        for t in range(2):
+            half = jnp.transpose(prod[t * width : (t + 1) * width])
+            acc_ref[:, pl.ds(2 * slot + t, 1), :] = (half[:16] + half[16:])[:, None, :]
+
+    pairs = 2 * count if edge else count
+    spare = acc_ref.shape[1] // 2 - 1
+
+    def slot_of(step):
+        return pair_of(step) if edge else step
+
+    def two_pairs(index, carry):
+        last = jnp.maximum(2 * index - 1, 0)
+        pair_sums(last, jnp.where(index == 0, spare, slot_of(last)), kern_odd)
+        pair_kernels(2 * index, kern_even)
+        pair_sums(2 * index, slot_of(2 * index), kern_even)
+        pair_kernels(2 * index + 1, kern_odd)
         return carry
 
-    lax.fori_loop(0, 2 * count if edge else count, one_block, 0)
+    kern_odd[...] = jnp.zeros_like(kern_odd)
+    lax.fori_loop(0, pairs, prepare, 0)
+    lax.fori_loop(0, pairs // 2, two_pairs, 0)
+    pair_sums(pairs - 1, slot_of(pairs - 1), kern_odd)
     if edge:
-        acc_ref[:, count : count + skip, :] = done_ref[...]
-        swapped = segment_swap(acc_ref[...])
+        acc_ref[:, 2 * count : 2 * (count + skip), :] = done_ref[...]
+        swapped = segment_swap(acc_ref[:, :blocks, :])
         rhs_count = field_ref.shape[1]
         for c in range(2):
             for u in range(rhs_count):
                 out_ref[c, u] = swapped[c * rhs_count + u] + 0.5 * field_ref[c, u]
-
-
-def run_pack(field, positions, normals, areas):
-    rows, width = areas.shape
-    blocks = width // SEG
-    halo = blocks // 4
-    shapes = [(blocks, 24, width), (halo, 24, width), (halo, 24, width)]
-    return pl.pallas_call(
-        pack_kernel,
-        out_shape=[jax.ShapeDtypeStruct(s, f32) for s in shapes],
-        cost_estimate=cost(10**8, 10**6),
-        name="pack",
-    )(field, positions, normals, areas)
+    else:
+        out_ref[...] = acc_ref[:, : 2 * pairs, :]
 
 
 def vmem(count=1):
@@ -269,23 +338,31 @@
     return pl.CostEstimate(flops=flops, bytes_accessed=size, transcendentals=0)
 
 
-def run_send(chosen, counts, field, v):
+def params(megabytes):
+    return pltpu.CompilerParams(vmem_limit_bytes=megabytes * 1024 * 1024)
+
+
+def run_send(chosen, counts, field, positions, normals, areas, v):
     peers, cap, _, rank, width = v.shape
     rhs, span_rows = field.shape[1:3]
     chunks = 8
+    blocks = width // SEG
+    halo = blocks // 4
+    shapes = [(peers, 8, width), (blocks, 24, width), (halo, 24, width), (halo, 24, width)]
     return pl.pallas_call(
         send_kernel,
-        in_specs=smem(2) + vmem(1) + [pl.BlockSpec(memory_space=pl.ANY)],
-        out_specs=vmem()[0],
-        out_shape=jax.ShapeDtypeStruct((peers, 8, width), f32),
+        in_specs=smem(2) + vmem(4) + [pl.BlockSpec(memory_space=pl.ANY)],
+        out_specs=vmem(4),
+        out_shape=[jax.ShapeDtypeStruct(s, f32) for s in shapes],
         scratch_shapes=[
             pltpu.VMEM(v.shape, f32),
             pltpu.VMEM((span_rows, 16, 2 * width), bf16),
             pltpu.SemaphoreType.DMA((chunks,)),
         ],
         cost_estimate=cost(3 * 10**9, 4 * v.size),
+        compiler_params=params(56),
         name="send",
-    )(chosen, counts, field.reshape(2 * rhs * span_rows, width), v)
+    )(chosen, counts, field.reshape(2 * rhs * span_rows, width), positions, normals, areas, v)
 
 
 def run_receive(targets, me, coef, u, span, span_rows):
@@ -296,19 +373,25 @@
         in_specs=smem(2) + vmem(2),
         out_specs=vmem(span),
         out_shape=[jax.ShapeDtypeStruct(shape, f32)] * span,
-        scratch_shapes=[pltpu.VMEM((span * 16 * span_rows, width), f32)],
+        scratch_shapes=[pltpu.VMEM((span * 16 * span_rows, width), f32)] * 4,
         cost_estimate=cost(3 * 10**9, 4 * u.size),
+        compiler_params=params(12),
         name="receive",
     )(targets, me, coef, u)
 
 
-def near_scratch(blocks, width):
+def near_scratch(blocks, width, pairs, slots):
     halo = blocks // 4
     count = blocks + 2 * halo
+    span = 2 * width * (2 * halo + 2)
     return [
-        pltpu.VMEM((count, 8, width), f32),
+        pltpu.VMEM((count, 16, width), f32),
         pltpu.VMEM((32, 2 * width * count), bf16),
-        pltpu.VMEM((2 * width, 2 * width * (2 * halo + 1)), bf16),
+        pltpu.VMEM((4 * width, span), bf16),
+        pltpu.VMEM((4 * width, span), bf16),
+        pltpu.VMEM((pairs, 2 * width, 48), bf16),
+        pltpu.VMEM((pairs, 48, span), bf16),
+        pltpu.VMEM((16, 2 * slots + 2, width), f32),
     ]
 
 
@@ -317,11 +400,12 @@
     halo = blocks // 4
     count = blocks - 2 * halo
     return pl.pallas_call(
-        functools.partial(near_kernel, halo, count, 0, False),
+        functools.partial(near_kernel, halo // 2, count // 2, 0, False),
         in_specs=vmem(1),
         out_specs=vmem()[0],
         out_shape=jax.ShapeDtypeStruct((16, count, width), f32),
-        scratch_shapes=near_scratch(blocks, width),
+        scratch_shapes=near_scratch(blocks, width, count // 2, count // 2),
+        compiler_params=params(20),
         cost_estimate=cost(10**10, 10**6),
         name="near_inner",
     )(mid)
@@ -331,11 +415,12 @@
     blocks, _, width = mid.shape
     halo = left.shape[0]
     return pl.pallas_call(
-        functools.partial(near_kernel, 0, halo, blocks - 2 * halo, True),
+        functools.partial(near_kernel, 0, halo // 2, blocks // 2 - halo, True),
         in_specs=vmem(5),
         out_specs=vmem()[0],
         out_shape=jax.ShapeDtypeStruct(field.shape, f32),
-        scratch_shapes=near_scratch(blocks, width) + [pltpu.VMEM((16, blocks, width), f32)],
+        scratch_shapes=near_scratch(blocks, width, halo, blocks // 2),
+        compiler_params=params(20),
         cost_estimate=cost(10**10, 10**6),
         name="near_edge",
     )(left, mid, right, done, field)
@@ -348,12 +433,16 @@
     span = lax.axis_size("span")
     span_rows = field.shape[2]
     hold = lax.optimization_barrier
-    outgoing = run_send(
-        col_cluster[0, 0].T, block_count[0], field, v_factors.reshape(v_factors.shape[2:])
+    outgoing, mid, low, high = run_send(
+        col_cluster[0, 0].T,
+        block_count[0],
+        field,
+        positions,
+        normals,
+        areas,
+        v_factors.reshape(v_factors.shape[2:]),
     )
-    outgoing, positions = hold((outgoing, positions))
     incoming = lax.all_to_all(outgoing, "azim", split_axis=0, concat_axis=0, tiled=True)
-    mid, low, high = run_pack(field, positions, normals, areas)
     forward = [(i, (i + 1) % azim) for i in range(azim)]
     backward = [(b, a) for a, b in forward]
     left = lax.ppermute(high, "azim", forward)

time: 71 us -> 57.4 us (0.81)
  Pallas kernels: 43.1 us -> 29.5 us
  other arithmetic: 1.62 us -> 0.71 us
  local copies, waits for them, and re-layouts: 0.72 us -> 1.57 us
    pallas_call x4 -> x3, Pallas kernels: 37.3 us -> 26.2 us  [the longest x1 10.4 us: run_near_edge(): pl.pallas_call(functools.partial(near_kernel, 0, halo // 2, blocks // 2 -...]
    pallas_call x1, Pallas kernels: 5.81 us -> 3.25 us  [run_receive(): pl.pallas_call(receive_kernel, in_specs=smem(2) + vmem(2), out_specs=vmem...]
    add x1, other arithmetic: 1.58 us -> 0.67 us  [shards(): return near + total.reshape(near.shape)]
    unnamed x8 -> x14, local copies, waits for them, and re-layouts: 0.72 us -> 1.57 us
  transfers between devices with their start and end apart: 6 -> 6, of which waited for: 0 -> 0; matrix products, arithmetic and copies ran while one was open for 0% -> 0% of each run, Pallas kernels for 45% -> 36%
where the time goes in v2:
time: 57.4 us; the launch traced here: 57.2 us
  Pallas kernels  29.5 us (51%)
  starting transfers between devices  25.3 us (44%)
  local copies, waits for them, and re-layouts  1.57 us (3%)
  other arithmetic  0.71 us (1%)
    all_to_all x1, starting transfers between devices, shards(): lax.all_to_all(outgoing, 'azim', split_axis=0, concat_axis=0, tiled=True)  15.1 us
    pallas_call x1, Pallas kernels, run_near_edge(): pl.pallas_call(functools.partial(near_kernel, 0, halo // 2, blocks // 2 -...  10.4 us
    pallas_call x1, Pallas kernels, run_near_inner(): pl.pallas_call(functools.partial(near_kernel, halo // 2, count // 2, 0, F...  9.97 us
    ppermute x1, starting transfers between devices, shards(): right = lax.ppermute(low, 'azim', backward)  6.18 us
    pallas_call x1, Pallas kernels, run_send(): pl.pallas_call(send_kernel, in_specs=smem(2) + vmem(4) + [pl.BlockSpec(me...  5.83 us
    pallas_call x1, Pallas kernels, run_receive(): pl.pallas_call(receive_kernel, in_specs=smem(2) + vmem(2), out_specs=vmem...  3.25 us
    ppermute x3, starting transfers between devices, shards(): others.append(lax.ppermute(pieces[k], 'span', ring))  2.92 us
    unnamed x14, local copies, waits for them, and re-layouts  1.57 us
  transfers between devices with their start and end apart: 6, of which 0 were waited for; matrix products, arithmetic and copies ran while one was open for 0% of the time, Pallas kernels for 36%

profile of v2, /device:TPU:1, one launch (start us, length us, event | category | flops | bytes accessed | tf_op | source)
XLA Modules:
  0.0 57.2 jit_solution(866966411128330790)
XLA Ops:
  0.0 5.8 %send.1 = (f32[64,8,128]{2,1,0:T(8,128)}, f32[16,24,128]{2,1,0:T(8,128)}, f32[4,24,128]{2,1,0:T(8,128)}, f32[4,24,128]{2,1,0:T(8,128)}) custom-call(s32[2,64]{1,0:T(2,128)} %bitcast.17, s32[1,64]{1,0:T(1,128)} %bitcast.18, f32[256,128]{1,0:T(8,128)} %bitcast.13, f32[3,16,128]{2,1,0:T(8,128)} %pos_ref.1, f32[3,16,128]{2,1,0:T(8,128)} %nrm_ref.1, ...), custom_call_target="tpu_custom_call" | custom-call | flops 3000000000 | bytes 3145728 | tf_op jit(solution)/shard_map/send/pallas_call | solution.py:352
  5.8 15.1 %all-to-all-start = ((f32[64,8,128]{2,1,0:T(8,128)}), f32[64,8,128]{2,1,0:T(8,128)S(1)}, u32[]{:S(2)}, u32[]{:S(2)}) async-start(f32[64,8,128]{2,1,0:T(8,128)} %get-tuple-element.22), calls=%async_computation | async-start | bytes 524288 | tf_op jit(solution)/shard_map/all_to_all | solution.py:445
  21.0 1.1 %collective-permute-start = (f32[4,24,128]{2,1,0:T(8,128)}, f32[4,24,128]{2,1,0:T(8,128)S(1)}, u32[]{:S(2)}, u32[]{:S(2)}) collective-permute-start(f32[4,24,128]{2,1,0:T(8,128)} %get-tuple-element.24), channel_id=1, source_target_pairs={{0,4},{4,8},{8,12},{12,16},{16,20},{20,24},{24,28},{28,32},{32,36}... | collective-permute-start | bytes 147464 | tf_op jit(solution)/shard_map/ppermute | solution.py:448
  22.1 6.2 %collective-permute-start.1 = (f32[4,24,128]{2,1,0:T(8,128)}, f32[4,24,128]{2,1,0:T(8,128)S(1)}, u32[]{:S(2)}, u32[]{:S(2)}) collective-permute-start(f32[4,24,128]{2,1,0:T(8,128)} %get-tuple-element.25), channel_id=1, source_target_pairs={{4,0},{8,4},{12,8},{16,12},{20,16},{24,20},{28,24},{32,28},{36,32}... | collective-permute-start | bytes 147464 | tf_op jit(solution)/shard_map/ppermute | solution.py:449
  28.2 0.0 copy-start.3
  28.3 0.9 %copy-done.3 = f32[16,24,128]{2,1,0:T(8,128)S(1)} copy-done((f32[16,24,128]{2,1,0:T(8,128)S(1)}, f32[16,24,128]{2,1,0:T(8,128)}, u32[]{:S(2)}) %copy-start.3) | copy-done | bytes 196632
  29.2 0.0 copy-start
  29.2 0.0 copy-start.2
  29.2 10.0 %near_inner.1.refs_3_ = f32[16,8,128]{2,1,0:T(8,128)S(1)} custom-call(f32[16,24,128]{2,1,0:T(8,128)S(1)} %copy-done.3), custom_call_target="tpu_custom_call" | custom-call | flops 10000000000 | bytes 1000000 | tf_op jit(solution)/shard_map/near_inner/pallas_call | solution.py:402
  39.2 0.0 copy-start.5
  39.2 0.6 %copy-done.5 = f32[16,8,128]{2,1,0:T(8,128)} copy-done((f32[16,8,128]{2,1,0:T(8,128)}, f32[16,8,128]{2,1,0:T(8,128)S(1)}, u32[]{:S(2)}) %copy-start.5) | copy-done | bytes 65560
  39.8 0.0 collective-permute-done.refs_0_
  39.8 0.0 collective-permute-done.1.refs_2_
  39.8 0.0 all-to-all-done.coef_ref
  39.8 0.0 copy-done
  39.8 0.0 copy-done.2
  39.8 0.0 copy-start.1
  39.8 0.0 copy-start.4
  39.8 0.0 copy-start.6
  39.9 3.3 %receive.1 = (f32[16,16,128]{2,1,0:T(8,128)S(1)}, f32[16,16,128]{2,1,0:T(8,128)S(1)}, f32[16,16,128]{2,1,0:T(8,128)S(1)}, f32[16,16,128]{2,1,0:T(8,128)S(1)}) custom-call(s32[2,64]{1,0:T(2,128)S(1)} %bitcast.14, s32[1]{0:T(128)} %bitcast.7.me_ref, f32[64,8,128]{2,1,0:T(8,128)S(1)} %all-to-all-done.coef_ref, f32[64,2,2,24,128]{4,3,2,1,0:T(8,128)S(1)} %bitcast.12), custom_call_target="tpu_custom_call" | custom-call | flops 3000000000 | bytes 3145728 | tf_op jit(solution)/shard_map/receive/pallas_call | solution.py:371
  43.1 1.8 %collective-permute-start.2 = (f32[16,16,128]{2,1,0:T(8,128)S(1)}, f32[16,16,128]{2,1,0:T(8,128)S(1)}, u32[]{:S(2)}, u32[]{:S(2)}) collective-permute-start(f32[16,16,128]{2,1,0:T(8,128)S(1)} %get-tuple-element.36), channel_id=1, source_target_pairs={{0,1},{1,2},{2,3},{3,0},{4,5},{5,6},{6,7},{7,4},{8,9},{9,10},{10,1... | collective-permute-start | bytes 393224 | tf_op jit(solution)/shard_map/ppermute | solution.py:461
  44.9 1.1 %collective-permute-start.3 = (f32[16,16,128]{2,1,0:T(8,128)S(1)}, f32[16,16,128]{2,1,0:T(8,128)S(1)}, u32[]{:S(2)}, u32[]{:S(2)}) collective-permute-start(f32[16,16,128]{2,1,0:T(8,128)S(1)} %get-tuple-element.37), channel_id=1, source_target_pairs={{0,2},{1,3},{2,0},{3,1},{4,6},{5,7},{6,4},{7,5},{8,10},{9,11},{10,... | collective-permute-start | bytes 393224 | tf_op jit(solution)/shard_map/ppermute | solution.py:461
  46.0 0.0 collective-permute-start.4
  46.0 0.0 copy-done.1
  46.0 0.0 copy-done.4
  46.0 0.0 copy-done.6
  46.1 10.4 %near_edge.1 = f32[2,8,16,128]{3,2,1,0:T(8,128)S(1)} custom-call(f32[4,24,128]{2,1,0:T(8,128)S(1)} %collective-permute-done.refs_0_, f32[16,24,128]{2,1,0:T(8,128)S(1)} %copy-done.4, f32[4,24,128]{2,1,0:T(8,128)S(1)} %collective-permute-done.1.refs_2_, f32[16,8,128]{2,1,0:T(8,128)S(1)} %copy-done.6, f32[2,8,16,128]{3,2,1,0:T(8,128)S(1)} %copy-done.1), custom_call_target="tpu_custom_call" | custom-call | flops 10000000000 | bytes 1000000 | tf_op jit(solution)/shard_map/near_edge/pallas_call | solution.py:417
  56.5 0.0 collective-permute-done.2
  56.5 0.0 collective-permute-done.3
  56.5 0.0 collective-permute-done.4
  56.5 0.7 %add.15 = f32[2,8,16,128]{3,2,1,0:T(8,128)} add(f32[2,8,16,128]{3,2,1,0:T(8,128)S(1)} %near_edge.1, f32[2,8,16,128]{3,2,1,0:T(8,128)S(1)} %bitcast.15) | non-fusion elementwise | flops 32768 | bytes 393216 | tf_op jit(solution)/shard_map/add | solution.py:465
  (1 shorter events, 0.0 us)
Async XLA Ops:
  5.8 34.0 %all-to-all-start = ((f32[64,8,128]{2,1,0:T(8,128)}), f32[64,8,128]{2,1,0:T(8,128)S(1)}, u32[]{:S(2)}, u32[]{:S(2)}) async-start(f32[64,8,128]{2,1,0:T(8,128)} %get-tuple-element.22), calls=%async_computation | async-start | bytes 524288 | tf_op jit(solution)/shard_map/all_to_all | solution.py:445
  21.0 18.8 %collective-permute-start = (f32[4,24,128]{2,1,0:T(8,128)}, f32[4,24,128]{2,1,0:T(8,128)S(1)}, u32[]{:S(2)}, u32[]{:S(2)}) collective-permute-start(f32[4,24,128]{2,1,0:T(8,128)} %get-tuple-element.24), channel_id=1, source_target_pairs={{0,4},{4,8},{8,12},{12,16},{16,20},{20,24},{24,28},{28,32},{32,36}... | collective-permute-start | bytes 147464 | tf_op jit(solution)/shard_map/ppermute | solution.py:448
  22.1 17.7 %collective-permute-start.1 = (f32[4,24,128]{2,1,0:T(8,128)}, f32[4,24,128]{2,1,0:T(8,128)S(1)}, u32[]{:S(2)}, u32[]{:S(2)}) collective-permute-start(f32[4,24,128]{2,1,0:T(8,128)} %get-tuple-element.25), channel_id=1, source_target_pairs={{4,0},{8,4},{12,8},{16,12},{20,16},{24,20},{28,24},{32,28},{36,32}... | collective-permute-start | bytes 147464 | tf_op jit(solution)/shard_map/ppermute | solution.py:449
  28.2 0.9 %copy-start.3 = (f32[16,24,128]{2,1,0:T(8,128)S(1)}, f32[16,24,128]{2,1,0:T(8,128)}, u32[]{:S(2)}) copy-start(f32[16,24,128]{2,1,0:T(8,128)} %get-tuple-element.32.refs_0_.refs_1_) | copy-start | bytes 589828
  29.2 10.6 %copy-start = (f32[1,1,64,2,2,24,128]{6,5,4,3,2,1,0:T(8,128)S(1)}, f32[1,1,64,2,2,24,128]{6,5,4,3,2,1,0:T(8,128)}, u32[]{:S(2)}) copy-start(f32[1,1,64,2,2,24,128]{6,5,4,3,2,1,0:T(8,128)} %param.17) | copy-start | bytes 9437188
  29.2 10.6 %copy-start.2 = (s32[1,1,64,2]{2,3,1,0:T(2,128)S(1)}, s32[1,1,64,2]{2,3,1,0:T(2,128)}, u32[]{:S(2)}) copy-start(s32[1,1,64,2]{2,3,1,0:T(2,128)} %param.15) | copy-start | bytes 1540
  39.2 0.6 %copy-start.5 = (f32[16,8,128]{2,1,0:T(8,128)}, f32[16,8,128]{2,1,0:T(8,128)S(1)}, u32[]{:S(2)}) copy-start(f32[16,8,128]{2,1,0:T(8,128)S(1)} %near_inner.1.refs_3_) | copy-start | bytes 196612
  39.8 6.2 %copy-start.1 = (f32[2,8,16,128]{3,2,1,0:T(8,128)S(1)}, f32[2,8,16,128]{3,2,1,0:T(8,128)}, u32[]{:S(2)}) copy-start(f32[2,8,16,128]{3,2,1,0:T(8,128)} %refs_4_.1) | copy-start | bytes 393220
  39.8 6.2 %copy-start.4 = (f32[16,24,128]{2,1,0:T(8,128)S(1)}, f32[16,24,128]{2,1,0:T(8,128)}, u32[]{:S(2)}) copy-start(f32[16,24,128]{2,1,0:T(8,128)} %get-tuple-element.32.refs_0_.refs_1_) | copy-start | bytes 589828
  39.8 6.2 %copy-start.6 = (f32[16,8,128]{2,1,0:T(8,128)S(1)}, f32[16,8,128]{2,1,0:T(8,128)}, u32[]{:S(2)}) copy-start(f32[16,8,128]{2,1,0:T(8,128)} %copy-done.5) | copy-start | bytes 196612
  43.1 13.4 %collective-permute-start.2 = (f32[16,16,128]{2,1,0:T(8,128)S(1)}, f32[16,16,128]{2,1,0:T(8,128)S(1)}, u32[]{:S(2)}, u32[]{:S(2)}) collective-permute-start(f32[16,16,128]{2,1,0:T(8,128)S(1)} %get-tuple-element.36), channel_id=1, source_target_pairs={{0,1},{1,2},{2,3},{3,0},{4,5},{5,6},{6,7},{7,4},{8,9},{9,10},{10,1... | collective-permute-start | bytes 393224 | tf_op jit(solution)/shard_map/ppermute | solution.py:461
  44.9 11.6 %collective-permute-start.3 = (f32[16,16,128]{2,1,0:T(8,128)S(1)}, f32[16,16,128]{2,1,0:T(8,128)S(1)}, u32[]{:S(2)}, u32[]{:S(2)}) collective-permute-start(f32[16,16,128]{2,1,0:T(8,128)S(1)} %get-tuple-element.37), channel_id=1, source_target_pairs={{0,2},{1,3},{2,0},{3,1},{4,6},{5,7},{6,4},{7,5},{8,10},{9,11},{10,... | collective-permute-start | bytes 393224 | tf_op jit(solution)/shard_map/ppermute | solution.py:461
  46.0 10.5 %collective-permute-start.4 = (f32[16,16,128]{2,1,0:T(8,128)S(1)}, f32[16,16,128]{2,1,0:T(8,128)S(1)}, u32[]{:S(2)}, u32[]{:S(2)}) collective-permute-start(f32[16,16,128]{2,1,0:T(8,128)S(1)} %get-tuple-element.38), channel_id=1, source_target_pairs={{0,3},{1,0},{2,1},{3,2},{4,7},{5,4},{6,5},{7,6},{8,11},{9,8},{10,9... | collective-permute-start | bytes 393224 | tf_op jit(solution)/shard_map/ppermute | solution.py:461

commit v3 on v2

--- a/solution.py
+++ b/solution.py
@@ -120,8 +120,9 @@
     count, cap, rank, width = u_ref.shape[0], u_ref.shape[1], u_ref.shape[3], u_ref.shape[4]
     span_rows = outs[0].shape[1]
     used = 2 * rank * cap
+    row_bits = span_rows.bit_length() - 1
     piece = accs[0].shape[0] // span
-    peers = 8
+    peers = 16
     for acc_ref in accs:
         acc_ref[...] = jnp.zeros_like(acc_ref)
     me = me_ref[0]
@@ -150,7 +151,7 @@
             total = one[:many] + (one[many:] + two)
             for k in range(cap):
                 w = target_ref[k, peer]
-                place = ((w // span_rows - me + span) % span) * piece + w % span_rows
+                place = (((w >> row_bits) - me) & (span - 1)) * piece + (w & (span_rows - 1))
                 at = pl.ds(place, 16, stride=span_rows)
                 acc_ref = accs[(2 * i + k) % 4]
                 acc_ref[at, :] += total[16 * k : 16 * k + 16]
@@ -164,12 +165,12 @@
 
 
 def near_kernel(begin, count, skip, edge, *refs):
-    scratch = refs[-7:]
-    pos_ref, wide_ref, kern_even, kern_odd, target_ref, source_ref, acc_ref = scratch
+    scratch = refs[-8:]
+    pos_ref, wide_ref, kern_even, kern_odd, target_ref, source_ref, part_ref, acc_ref = scratch
     if edge:
-        left_ref, mid_ref, right_ref, done_ref, field_ref, out_ref = refs[:-7]
+        left_ref, mid_ref, right_ref, done_ref, field_ref, out_ref = refs[:-8]
     else:
-        mid_ref, out_ref = refs[:-7]
+        mid_ref, out_ref, token_ref = refs[:-8]
     blocks = mid_ref.shape[0]
     halo = blocks // 4
     window = 2 * halo + 1
@@ -269,8 +270,12 @@
             source_ref[step, :, cols] = jnp.concatenate(wide, 1).astype(bf16)
         return carry
 
-    def pair_kernels(step, kern_ref):
+    def pair_kernels(step, kern_ref, finish):
         for sb in range(sources):
+            if sb == 3:
+                finish()
+            if sb == sources - 2:
+                part_ref[...] = partial_sums(step, kern_ref, 0)
             start = width if sb == sources - 1 else 0
             stop = width if sb == 0 else 2 * width
             gram = jnp.dot(
@@ -288,11 +293,15 @@
                     kern_ref[at : at + chunk, cols] = high
                     kern_ref[2 * width + at : 2 * width + at + chunk, cols] = low
 
+    def partial_sums(step, kern_ref, half):
+        size = width * sources
+        start = pl.multiple_of(pair_of(step) * (4 * width) + half * size, 2 * width)
+        cols = slice(half * size, (half + 1) * size)
+        prod = dot_nt(kern_ref[:, cols], wide_ref[:, pl.ds(start, size)])
+        return prod[: 2 * width] + prod[2 * width :]
+
     def pair_sums(step, slot, kern_ref):
-        start = pl.multiple_of(pair_of(step) * (4 * width), 4 * width)
-        rhs = wide_ref[:, pl.ds(start, 2 * width * sources)]
-        prod = dot_nt(kern_ref[...], rhs)
-        prod = prod[: 2 * width] + prod[2 * width :]
+        prod = part_ref[...] + partial_sums(step, kern_ref, 1)
         for t in range(2):
             half = jnp.transpose(prod[t * width : (t + 1) * width])
             acc_ref[:, pl.ds(2 * slot + t, 1), :] = (half[:16] + half[16:])[:, None, :]
@@ -305,13 +314,13 @@
 
     def two_pairs(index, carry):
         last = jnp.maximum(2 * index - 1, 0)
-        pair_sums(last, jnp.where(index == 0, spare, slot_of(last)), kern_odd)
-        pair_kernels(2 * index, kern_even)
-        pair_sums(2 * index, slot_of(2 * index), kern_even)
-        pair_kernels(2 * index + 1, kern_odd)
+        slot = jnp.where(index == 0, spare, slot_of(last))
+        even = 2 * index
+        pair_kernels(even, kern_even, lambda: pair_sums(last, slot, kern_odd))
+        pair_kernels(even + 1, kern_odd, lambda: pair_sums(even, slot_of(even), kern_even))
         return carry
 
-    kern_odd[...] = jnp.zeros_like(kern_odd)
+    part_ref[...] = jnp.zeros_like(part_ref)
     lax.fori_loop(0, pairs, prepare, 0)
     lax.fori_loop(0, pairs // 2, two_pairs, 0)
     pair_sums(pairs - 1, slot_of(pairs - 1), kern_odd)
@@ -324,6 +333,7 @@
                 out_ref[c, u] = swapped[c * rhs_count + u] + 0.5 * field_ref[c, u]
     else:
         out_ref[...] = acc_ref[:, : 2 * pairs, :]
+        token_ref[...] = jnp.zeros_like(token_ref)
 
 
 def vmem(count=1):
@@ -345,7 +355,7 @@
 def run_send(chosen, counts, field, positions, normals, areas, v):
     peers, cap, _, rank, width = v.shape
     rhs, span_rows = field.shape[1:3]
-    chunks = 8
+    chunks = 4
     blocks = width // SEG
     halo = blocks // 4
     shapes = [(peers, 8, width), (blocks, 24, width), (halo, 24, width), (halo, 24, width)]
@@ -360,7 +370,7 @@
             pltpu.SemaphoreType.DMA((chunks,)),
         ],
         cost_estimate=cost(3 * 10**9, 4 * v.size),
-        compiler_params=params(56),
+        compiler_params=params(58),
         name="send",
     )(chosen, counts, field.reshape(2 * rhs * span_rows, width), positions, normals, areas, v)
 
@@ -391,6 +401,7 @@
         pltpu.VMEM((4 * width, span), bf16),
         pltpu.VMEM((pairs, 2 * width, 48), bf16),
         pltpu.VMEM((pairs, 48, span), bf16),
+        pltpu.VMEM((2 * width, 32), f32),
         pltpu.VMEM((16, 2 * slots + 2, width), f32),
     ]
 
@@ -402,8 +413,11 @@
     return pl.pallas_call(
         functools.partial(near_kernel, halo // 2, count // 2, 0, False),
         in_specs=vmem(1),
-        out_specs=vmem()[0],
-        out_shape=jax.ShapeDtypeStruct((16, count, width), f32),
+        out_specs=vmem(2),
+        out_shape=[
+            jax.ShapeDtypeStruct((16, count, width), f32),
+            jax.ShapeDtypeStruct((8, width), f32),
+        ],
         scratch_shapes=near_scratch(blocks, width, count // 2, count // 2),
         compiler_params=params(20),
         cost_estimate=cost(10**10, 10**6),
@@ -447,8 +461,8 @@
     backward = [(b, a) for a, b in forward]
     left = lax.ppermute(high, "azim", forward)
     right = lax.ppermute(low, "azim", backward)
-    inner = run_near_inner(mid)
-    incoming, inner, left, right = hold((incoming, inner, left, right))
+    inner, token = run_near_inner(mid)
+    incoming, _ = hold((incoming, token))
     me = lax.axis_index("span").astype(jnp.int32).reshape(1)
     pieces = run_receive(
         row_cluster[0, 0].T, me, incoming, u_factors.reshape(u_factors.shape[2:]), span, span_rows

time: 57.4 us -> 55.9 us (0.974)
  Pallas kernels: 29.5 us -> 28 us
    pallas_call x1, Pallas kernels: 3.25 us -> 2.44 us  [run_receive(): pl.pallas_call(receive_kernel, in_specs=smem(2) + vmem(2), out_specs=vmem...]
  transfers between devices with their start and end apart: 6 -> 6, of which waited for: 0 -> 0; matrix products, arithmetic and copies ran while one was open for 0% -> 0% of each run, Pallas kernels for 36% -> 40%
where the time goes in v3:
time: 55.9 us; the launch traced here: 55.8 us
  Pallas kernels  28 us (50%)
  starting transfers between devices  25.3 us (45%)
  local copies, waits for them, and re-layouts  1.58 us (3%)
  other arithmetic  0.71 us (1%)
    all_to_all x1, starting transfers between devices, shards(): lax.all_to_all(outgoing, 'azim', split_axis=0, concat_axis=0, tiled=True)  15.1 us
    pallas_call x1, Pallas kernels, run_near_edge(): pl.pallas_call(functools.partial(near_kernel, 0, halo // 2, blocks // 2 -...  10.2 us
    pallas_call x1, Pallas kernels, run_near_inner(): pl.pallas_call(functools.partial(near_kernel, halo // 2, count // 2, 0, F...  9.9 us
    ppermute x1, starting transfers between devices, shards(): right = lax.ppermute(low, 'azim', backward)  6.18 us
    pallas_call x1, Pallas kernels, run_send(): pl.pallas_call(send_kernel, in_specs=smem(2) + vmem(4) + [pl.BlockSpec(me...  5.46 us
    ppermute x3, starting transfers between devices, shards(): others.append(lax.ppermute(pieces[k], 'span', ring))  2.95 us
    pallas_call x1, Pallas kernels, run_receive(): pl.pallas_call(receive_kernel, in_specs=smem(2) + vmem(2), out_specs=vmem...  2.44 us
    unnamed x14, local copies, waits for them, and re-layouts  1.58 us
  transfers between devices with their start and end apart: 6, of which 0 were waited for; matrix products, arithmetic and copies ran while one was open for 0% of the time, Pallas kernels for 40%

profile of v3, /device:TPU:1, one launch (start us, length us, event | category | flops | bytes accessed | tf_op | source)
XLA Modules:
  0.0 55.8 jit_solution(1360431153337794938)
XLA Ops:
  0.0 5.5 %send.1 = (f32[64,8,128]{2,1,0:T(8,128)}, f32[16,24,128]{2,1,0:T(8,128)}, f32[4,24,128]{2,1,0:T(8,128)}, f32[4,24,128]{2,1,0:T(8,128)}) custom-call(s32[2,64]{1,0:T(2,128)} %bitcast.17, s32[1,64]{1,0:T(1,128)} %bitcast.18, f32[256,128]{1,0:T(8,128)} %bitcast.13, f32[3,16,128]{2,1,0:T(8,128)} %pos_ref.1, f32[3,16,128]{2,1,0:T(8,128)} %nrm_ref.1, ...), custom_call_target="tpu_custom_call" | custom-call | flops 3000000000 | bytes 3145728 | tf_op jit(solution)/shard_map/send/pallas_call | solution.py:362
  5.5 15.1 %all-to-all-start = ((f32[64,8,128]{2,1,0:T(8,128)}), f32[64,8,128]{2,1,0:T(8,128)S(1)}, u32[]{:S(2)}, u32[]{:S(2)}) async-start(f32[64,8,128]{2,1,0:T(8,128)} %get-tuple-element.21), calls=%async_computation | async-start | bytes 524288 | tf_op jit(solution)/shard_map/all_to_all | solution.py:459
  20.6 1.1 %collective-permute-start = (f32[4,24,128]{2,1,0:T(8,128)}, f32[4,24,128]{2,1,0:T(8,128)S(1)}, u32[]{:S(2)}, u32[]{:S(2)}) collective-permute-start(f32[4,24,128]{2,1,0:T(8,128)} %get-tuple-element.19), channel_id=1, source_target_pairs={{0,4},{4,8},{8,12},{12,16},{16,20},{20,24},{24,28},{28,32},{32,36}... | collective-permute-start | bytes 147464 | tf_op jit(solution)/shard_map/ppermute | solution.py:462
  21.7 6.2 %collective-permute-start.1 = (f32[4,24,128]{2,1,0:T(8,128)}, f32[4,24,128]{2,1,0:T(8,128)S(1)}, u32[]{:S(2)}, u32[]{:S(2)}) collective-permute-start(f32[4,24,128]{2,1,0:T(8,128)} %get-tuple-element.27), channel_id=1, source_target_pairs={{4,0},{8,4},{12,8},{16,12},{20,16},{24,20},{28,24},{32,28},{36,32}... | collective-permute-start | bytes 147464 | tf_op jit(solution)/shard_map/ppermute | solution.py:463
  27.9 0.0 copy-start.3
  27.9 0.9 %copy-done.3 = f32[16,24,128]{2,1,0:T(8,128)S(1)} copy-done((f32[16,24,128]{2,1,0:T(8,128)S(1)}, f32[16,24,128]{2,1,0:T(8,128)}, u32[]{:S(2)}) %copy-start.3) | copy-done | bytes 196632
  28.8 0.0 copy-start
  28.8 0.0 copy-start.2
  28.8 9.9 %near_inner.1 = (f32[16,8,128]{2,1,0:T(8,128)S(1)}, f32[8,128]{1,0:T(8,128)}) custom-call(f32[16,24,128]{2,1,0:T(8,128)S(1)} %copy-done.3), custom_call_target="tpu_custom_call" | custom-call | flops 10000000000 | bytes 1000000 | tf_op jit(solution)/shard_map/near_inner/pallas_call | solution.py:413
  38.7 0.0 copy-start.5
  38.7 0.6 %copy-done.5 = f32[16,8,128]{2,1,0:T(8,128)} copy-done((f32[16,8,128]{2,1,0:T(8,128)}, f32[16,8,128]{2,1,0:T(8,128)S(1)}, u32[]{:S(2)}) %copy-start.5) | copy-done | bytes 65560
  39.3 0.0 all-to-all-done.coef_ref
  39.3 0.0 copy-done
  39.3 0.0 copy-done.2
  39.3 0.0 copy-start.1
  39.4 0.0 copy-start.4
  39.4 0.0 copy-start.6
  39.4 2.4 %receive.1 = (f32[16,16,128]{2,1,0:T(8,128)S(1)}, f32[16,16,128]{2,1,0:T(8,128)S(1)}, f32[16,16,128]{2,1,0:T(8,128)S(1)}, f32[16,16,128]{2,1,0:T(8,128)S(1)}) custom-call(s32[2,64]{1,0:T(2,128)S(1)} %bitcast.14, s32[1]{0:T(128)} %bitcast.7.me_ref, f32[64,8,128]{2,1,0:T(8,128)S(1)} %all-to-all-done.coef_ref, f32[64,2,2,24,128]{4,3,2,1,0:T(8,128)S(1)} %bitcast.12), custom_call_target="tpu_custom_call" | custom-call | flops 3000000000 | bytes 3145728 | tf_op jit(solution)/shard_map/receive/pallas_call | solution.py:381
  41.8 1.8 %collective-permute-start.2 = (f32[16,16,128]{2,1,0:T(8,128)S(1)}, f32[16,16,128]{2,1,0:T(8,128)S(1)}, u32[]{:S(2)}, u32[]{:S(2)}) collective-permute-start(f32[16,16,128]{2,1,0:T(8,128)S(1)} %get-tuple-element.30), channel_id=1, source_target_pairs={{0,1},{1,2},{2,3},{3,0},{4,5},{5,6},{6,7},{7,4},{8,9},{9,10},{10,1... | collective-permute-start | bytes 393224 | tf_op jit(solution)/shard_map/ppermute | solution.py:475
  43.6 1.2 %collective-permute-start.3 = (f32[16,16,128]{2,1,0:T(8,128)S(1)}, f32[16,16,128]{2,1,0:T(8,128)S(1)}, u32[]{:S(2)}, u32[]{:S(2)}) collective-permute-start(f32[16,16,128]{2,1,0:T(8,128)S(1)} %get-tuple-element.31), channel_id=1, source_target_pairs={{0,2},{1,3},{2,0},{3,1},{4,6},{5,7},{6,4},{7,5},{8,10},{9,11},{10,... | collective-permute-start | bytes 393224 | tf_op jit(solution)/shard_map/ppermute | solution.py:475
  44.8 0.0 collective-permute-start.4
  44.8 0.0 collective-permute-done.refs_0_
  44.8 0.0 collective-permute-done.1.refs_2_
  44.8 0.0 copy-done.1
  44.8 0.0 copy-done.4
  44.8 0.0 copy-done.6
  44.8 10.2 %near_edge.1 = f32[2,8,16,128]{3,2,1,0:T(8,128)S(1)} custom-call(f32[4,24,128]{2,1,0:T(8,128)S(1)} %collective-permute-done.refs_0_, f32[16,24,128]{2,1,0:T(8,128)S(1)} %copy-done.4, f32[4,24,128]{2,1,0:T(8,128)S(1)} %collective-permute-done.1.refs_2_, f32[16,8,128]{2,1,0:T(8,128)S(1)} %copy-done.6, f32[2,8,16,128]{3,2,1,0:T(8,128)S(1)} %copy-done.1), custom_call_target="tpu_custom_call" | custom-call | flops 10000000000 | bytes 1000000 | tf_op jit(solution)/shard_map/near_edge/pallas_call | solution.py:431
  55.0 0.0 collective-permute-done.2
  55.0 0.0 collective-permute-done.3
  55.0 0.0 collective-permute-done.4
  55.1 0.7 %add.15 = f32[2,8,16,128]{3,2,1,0:T(8,128)} add(f32[2,8,16,128]{3,2,1,0:T(8,128)S(1)} %near_edge.1, f32[2,8,16,128]{3,2,1,0:T(8,128)S(1)} %bitcast.15) | non-fusion elementwise | flops 32768 | bytes 393216 | tf_op jit(solution)/shard_map/add | solution.py:479
  (1 shorter events, 0.0 us)
Async XLA Ops:
  5.5 33.9 %all-to-all-start = ((f32[64,8,128]{2,1,0:T(8,128)}), f32[64,8,128]{2,1,0:T(8,128)S(1)}, u32[]{:S(2)}, u32[]{:S(2)}) async-start(f32[64,8,128]{2,1,0:T(8,128)} %get-tuple-element.21), calls=%async_computation | async-start | bytes 524288 | tf_op jit(solution)/shard_map/all_to_all | solution.py:459
  20.6 24.2 %collective-permute-start = (f32[4,24,128]{2,1,0:T(8,128)}, f32[4,24,128]{2,1,0:T(8,128)S(1)}, u32[]{:S(2)}, u32[]{:S(2)}) collective-permute-start(f32[4,24,128]{2,1,0:T(8,128)} %get-tuple-element.19), channel_id=1, source_target_pairs={{0,4},{4,8},{8,12},{12,16},{16,20},{20,24},{24,28},{28,32},{32,36}... | collective-permute-start | bytes 147464 | tf_op jit(solution)/shard_map/ppermute | solution.py:462
  21.7 23.1 %collective-permute-start.1 = (f32[4,24,128]{2,1,0:T(8,128)}, f32[4,24,128]{2,1,0:T(8,128)S(1)}, u32[]{:S(2)}, u32[]{:S(2)}) collective-permute-start(f32[4,24,128]{2,1,0:T(8,128)} %get-tuple-element.27), channel_id=1, source_target_pairs={{4,0},{8,4},{12,8},{16,12},{20,16},{24,20},{28,24},{32,28},{36,32}... | collective-permute-start | bytes 147464 | tf_op jit(solution)/shard_map/ppermute | solution.py:463
  27.9 0.9 %copy-start.3 = (f32[16,24,128]{2,1,0:T(8,128)S(1)}, f32[16,24,128]{2,1,0:T(8,128)}, u32[]{:S(2)}) copy-start(f32[16,24,128]{2,1,0:T(8,128)} %get-tuple-element.26.refs_0_.refs_1_) | copy-start | bytes 589828
  28.8 10.5 %copy-start = (f32[1,1,64,2,2,24,128]{6,5,4,3,2,1,0:T(8,128)S(1)}, f32[1,1,64,2,2,24,128]{6,5,4,3,2,1,0:T(8,128)}, u32[]{:S(2)}) copy-start(f32[1,1,64,2,2,24,128]{6,5,4,3,2,1,0:T(8,128)} %param.17) | copy-start | bytes 9437188
  28.8 10.5 %copy-start.2 = (s32[1,1,64,2]{2,3,1,0:T(2,128)S(1)}, s32[1,1,64,2]{2,3,1,0:T(2,128)}, u32[]{:S(2)}) copy-start(s32[1,1,64,2]{2,3,1,0:T(2,128)} %param.15) | copy-start | bytes 1540
  38.7 0.6 %copy-start.5 = (f32[16,8,128]{2,1,0:T(8,128)}, f32[16,8,128]{2,1,0:T(8,128)S(1)}, u32[]{:S(2)}) copy-start(f32[16,8,128]{2,1,0:T(8,128)S(1)} %get-tuple-element.28.refs_3_) | copy-start | bytes 196612
  39.3 5.4 %copy-start.1 = (f32[2,8,16,128]{3,2,1,0:T(8,128)S(1)}, f32[2,8,16,128]{3,2,1,0:T(8,128)}, u32[]{:S(2)}) copy-start(f32[2,8,16,128]{3,2,1,0:T(8,128)} %refs_4_.1) | copy-start | bytes 393220
  39.4 5.4 %copy-start.4 = (f32[16,24,128]{2,1,0:T(8,128)S(1)}, f32[16,24,128]{2,1,0:T(8,128)}, u32[]{:S(2)}) copy-start(f32[16,24,128]{2,1,0:T(8,128)} %get-tuple-element.26.refs_0_.refs_1_) | copy-start | bytes 589828
  39.4 5.4 %copy-start.6 = (f32[16,8,128]{2,1,0:T(8,128)S(1)}, f32[16,8,128]{2,1,0:T(8,128)}, u32[]{:S(2)}) copy-start(f32[16,8,128]{2,1,0:T(8,128)} %copy-done.5) | copy-start | bytes 196612
  41.8 13.2 %collective-permute-start.2 = (f32[16,16,128]{2,1,0:T(8,128)S(1)}, f32[16,16,128]{2,1,0:T(8,128)S(1)}, u32[]{:S(2)}, u32[]{:S(2)}) collective-permute-start(f32[16,16,128]{2,1,0:T(8,128)S(1)} %get-tuple-element.30), channel_id=1, source_target_pairs={{0,1},{1,2},{2,3},{3,0},{4,5},{5,6},{6,7},{7,4},{8,9},{9,10},{10,1... | collective-permute-start | bytes 393224 | tf_op jit(solution)/shard_map/ppermute | solution.py:475
  43.6 11.4 %collective-permute-start.3 = (f32[16,16,128]{2,1,0:T(8,128)S(1)}, f32[16,16,128]{2,1,0:T(8,128)S(1)}, u32[]{:S(2)}, u32[]{:S(2)}) collective-permute-start(f32[16,16,128]{2,1,0:T(8,128)S(1)} %get-tuple-element.31), channel_id=1, source_target_pairs={{0,2},{1,3},{2,0},{3,1},{4,6},{5,7},{6,4},{7,5},{8,10},{9,11},{10,... | collective-permute-start | bytes 393224 | tf_op jit(solution)/shard_map/ppermute | solution.py:475
  44.8 10.3 %collective-permute-start.4 = (f32[16,16,128]{2,1,0:T(8,128)S(1)}, f32[16,16,128]{2,1,0:T(8,128)S(1)}, u32[]{:S(2)}, u32[]{:S(2)}) collective-permute-start(f32[16,16,128]{2,1,0:T(8,128)S(1)} %get-tuple-element.32), channel_id=1, source_target_pairs={{0,3},{1,0},{2,1},{3,2},{4,7},{5,4},{6,5},{7,6},{8,11},{9,8},{10,9... | collective-permute-start | bytes 393224 | tf_op jit(solution)/shard_map/ppermute | solution.py:475

commit v4 on v3

--- a/solution.py
+++ b/solution.py
@@ -62,8 +62,9 @@
         high_ref[:, q, :] = packed[q, blocks - high_ref.shape[0] :]
 
 
-def send_kernel(chosen_ref, count_ref, field_ref, pos_ref, nrm_ref, area_ref, v_hbm, *rest):
-    out_ref, mid_ref, low_ref, high_ref, v_ref, table_ref, sems = rest
+def send_kernel(me_ref, chosen_ref, count_ref, field_ref, pos_ref, nrm_ref, area_ref, v_hbm, *rest):
+    outs, (mid_ref, low_ref, high_ref, out_ref, v_ref, table_ref, sems) = rest[:-7], rest[-7:]
+    me = me_ref[0]
     chunks = sems.shape[0]
     peers = out_ref.shape[0] // chunks
     rank = v_ref.shape[3]
@@ -75,8 +76,9 @@
         rows = pl.ds(index * peers, peers)
         return pltpu.make_async_copy(v_hbm.at[rows], v_ref.at[rows], sems.at[index])
 
+    ahead = me // peers
     for index in range(chunks):
-        fetch(index).start()
+        fetch(index ^ ahead).start()
     pack(field_ref, pos_ref, nrm_ref, area_ref, mid_ref, low_ref, high_ref)
 
     half = field_ref.shape[0] // 2
@@ -90,9 +92,10 @@
     lane = lax.broadcasted_iota(jnp.int32, (8, 2 * rank * cap), 1)
 
     def one_chunk(index, carry):
-        fetch(index).wait()
+        fetch(index ^ ahead).wait()
         for i in range(peers):
-            peer = index * peers + i
+            tile = index * peers + i
+            peer = tile ^ me
             wide = []
             for k in range(cap):
                 re, im = v_ref[peer, k, 0], v_ref[peer, k, 1]
@@ -107,15 +110,17 @@
                 part = first[at : at + 8] + (first[at + 8 : at + 16] + second[at : at + 8])
                 here = (lane // (2 * rank) == k) & (k < count_ref[0, peer])
                 total = jnp.where(here, part, total)
-            out_ref[peer, :, : 2 * rank * cap] = total
-            out_ref[peer, :, 2 * rank * cap :] = jnp.zeros((8, width - 2 * rank * cap), f32)
+            out_ref[tile, :, : 2 * rank * cap] = total
+            out_ref[tile, :, 2 * rank * cap :] = jnp.zeros((8, width - 2 * rank * cap), f32)
         return carry
 
     lax.fori_loop(0, chunks, one_chunk, 0)
-
-
-def receive_kernel(target_ref, me_ref, coef_ref, u_ref, *rest):
-    outs, accs = rest[:-4], rest[-4:]
+    for k, ref in enumerate(outs):
+        ref[...] = out_ref[k * peers : (k + 1) * peers]
+
+
+def receive_kernel(target_ref, me_ref, *rest):
+    parts, u_ref, outs, coef_ref, accs = rest[:4], rest[4], rest[5:-5], rest[-5], rest[-4:]
     span = len(outs)
     count, cap, rank, width = u_ref.shape[0], u_ref.shape[1], u_ref.shape[3], u_ref.shape[4]
     span_rows = outs[0].shape[1]
@@ -125,7 +130,9 @@
     peers = 16
     for acc_ref in accs:
         acc_ref[...] = jnp.zeros_like(acc_ref)
-    me = me_ref[0]
+    for k, ref in enumerate(parts):
+        coef_ref[k * peers : (k + 1) * peers] = ref[...]
+    me, sector = me_ref[0], me_ref[1]
     lane = lax.broadcasted_iota(jnp.int32, (peers * 8, width), 1)
 
     def one_chunk(index, carry):
@@ -139,7 +146,7 @@
             here = lane // (2 * rank) == k
             rows += [jnp.where(here, real_row, zero), jnp.where(here, imag_row, zero)]
         for i in range(peers):
-            peer = index * peers + i
+            peer = ((i % 4) * 16 + (i // 4) * 4 + index) ^ sector
             left = jnp.concatenate([r[8 * i : 8 * i + 8, :used] for r in rows], 0)
             left_high, left_low = split_two(left)
             high, low = split_two(u_ref[peer].reshape(used, width))
@@ -164,29 +171,31 @@
         outs[k][...] = total.reshape(outs[k].shape)
 
 
-def near_kernel(begin, count, skip, edge, *refs):
-    scratch = refs[-8:]
-    pos_ref, wide_ref, kern_even, kern_odd, target_ref, source_ref, part_ref, acc_ref = scratch
-    if edge:
-        left_ref, mid_ref, right_ref, done_ref, field_ref, out_ref = refs[:-8]
+def near_kernel(begin, final, *refs):
+    scratch = refs[-7:]
+    pos_ref, wide_ref, kern_ref, target_ref, source_ref, part_ref, acc_ref = scratch
+    if final:
+        left_ref, mid_ref, right_ref, *done, field_ref, out_ref = refs[:-7]
     else:
-        mid_ref, out_ref, token_ref = refs[:-8]
+        left_ref, mid_ref, right_ref, out_ref, token_ref = refs[:-7]
+    pairs = target_ref.shape[0]
     blocks = mid_ref.shape[0]
     halo = blocks // 4
     window = 2 * halo + 1
     width = mid_ref.shape[2]
     turn = wavenumber / (2.0 * math.pi)
 
-    def block_in(index):
-        if index < halo:
-            return left_ref.at[index]
-        if index < halo + blocks:
-            return mid_ref.at[index - halo]
-        return right_ref.at[index - halo - blocks]
+    def block_in(local):
+        index = 2 * begin - halo + local
+        if index < 0:
+            return left_ref.at[index + halo]
+        if index < blocks:
+            return mid_ref.at[index]
+        return right_ref.at[index - blocks]
 
     origin = mid_ref[blocks // 2, 16:19, 0:1]
     row = lax.broadcasted_iota(jnp.int32, (8, width), 0)
-    for b in range(0 if edge else halo, blocks + (2 if edge else 1) * halo):
+    for b in range(pos_ref.shape[0]):
         ref = block_in(b)
         pad = jnp.zeros((5, width), f32)
         pos_ref[b, 0:8, :] = jnp.concatenate([(ref[16:19, :] - origin) * turn, pad], 0)
@@ -199,10 +208,9 @@
         wide_ref[:, 2 * width * b : 2 * width * (b + 1)] = jnp.concatenate([high, low], 0)
     sources = window + 1
     zeros = jnp.zeros((width, 2 * width), bf16)
-    for kern_ref in (kern_even, kern_odd):
-        for part in (0, 2):
-            kern_ref[(part + 1) * width : (part + 2) * width, : 2 * width] = zeros
-            kern_ref[part * width : (part + 1) * width, 2 * width * (sources - 1) :] = zeros
+    for part in (0, 2):
+        kern_ref[(part + 1) * width : (part + 2) * width, : 2 * width] = zeros
+        kern_ref[part * width : (part + 1) * width, 2 * width * (sources - 1) :] = zeros
 
     chunk = 16
     sub = lax.broadcasted_iota(jnp.int32, (chunk, width), 0)
@@ -235,11 +243,8 @@
         pc, ps = inv * cosine, inv * sine
         return first * pc + second * ps, first * ps - second * pc
 
-    def pair_of(step):
-        return jnp.where(step < count, step, step + skip) + begin
-
     def prepare(step, carry):
-        tp = pair_of(step)
+        tp = step
         center = pos_ref[2 * tp + halo, 0:8, 8 * SEG - 1 : 8 * SEG]
 
         def local_of(index):
@@ -270,12 +275,22 @@
             source_ref[step, :, cols] = jnp.concatenate(wide, 1).astype(bf16)
         return carry
 
-    def pair_kernels(step, kern_ref, finish):
+    def sums(step, index):
+        start = pl.multiple_of((2 * step + index) * (2 * width), 2 * width)
+        cols = slice(2 * width * index, 2 * width * (index + 1))
+        return dot_nt(wide_ref[:, pl.ds(start, 2 * width)], kern_ref[:, cols])
+
+    def finish(step, slot):
+        prod = part_ref[...] + sums(step, sources - 1)
+        prod = prod[:, : 2 * width] + prod[:, 2 * width :]
+        prod = prod[:16] + prod[16:]
+        for t in range(2):
+            acc_ref[:, pl.ds(2 * slot + t, 1), :] = prod[:, t * width : (t + 1) * width][:, None, :]
+
+    spare = acc_ref.shape[1] // 2 - 1
+
+    def one_pair(step, carry):
         for sb in range(sources):
-            if sb == 3:
-                finish()
-            if sb == sources - 2:
-                part_ref[...] = partial_sums(step, kern_ref, 0)
             start = width if sb == sources - 1 else 0
             stop = width if sb == 0 else 2 * width
             gram = jnp.dot(
@@ -283,6 +298,13 @@
                 source_ref[step, :, 2 * width * sb : 2 * width * (sb + 1)],
                 preferred_element_type=f32,
             )
+            if sb == 0:
+                last = jnp.maximum(step - 1, 0)
+                finish(last, jnp.where(step == 0, spare, last))
+            elif sb == 1:
+                part_ref[...] = sums(step, 0)
+            else:
+                part_ref[...] += sums(step, sb - 1)
             for at in range(start, stop, chunk):
                 t = at // width
                 part = gram[at - start : at - start + chunk]
@@ -292,40 +314,16 @@
                     cols = slice(2 * width * sb + shift, 2 * width * sb + shift + width)
                     kern_ref[at : at + chunk, cols] = high
                     kern_ref[2 * width + at : 2 * width + at + chunk, cols] = low
-
-    def partial_sums(step, kern_ref, half):
-        size = width * sources
-        start = pl.multiple_of(pair_of(step) * (4 * width) + half * size, 2 * width)
-        cols = slice(half * size, (half + 1) * size)
-        prod = dot_nt(kern_ref[:, cols], wide_ref[:, pl.ds(start, size)])
-        return prod[: 2 * width] + prod[2 * width :]
-
-    def pair_sums(step, slot, kern_ref):
-        prod = part_ref[...] + partial_sums(step, kern_ref, 1)
-        for t in range(2):
-            half = jnp.transpose(prod[t * width : (t + 1) * width])
-            acc_ref[:, pl.ds(2 * slot + t, 1), :] = (half[:16] + half[16:])[:, None, :]
-
-    pairs = 2 * count if edge else count
-    spare = acc_ref.shape[1] // 2 - 1
-
-    def slot_of(step):
-        return pair_of(step) if edge else step
-
-    def two_pairs(index, carry):
-        last = jnp.maximum(2 * index - 1, 0)
-        slot = jnp.where(index == 0, spare, slot_of(last))
-        even = 2 * index
-        pair_kernels(even, kern_even, lambda: pair_sums(last, slot, kern_odd))
-        pair_kernels(even + 1, kern_odd, lambda: pair_sums(even, slot_of(even), kern_even))
         return carry
 
     part_ref[...] = jnp.zeros_like(part_ref)
     lax.fori_loop(0, pairs, prepare, 0)
-    lax.fori_loop(0, pairs // 2, two_pairs, 0)
-    pair_sums(pairs - 1, slot_of(pairs - 1), kern_odd)
-    if edge:
-        acc_ref[:, 2 * count : 2 * (count + skip), :] = done_ref[...]
+    lax.fori_loop(0, pairs, one_pair, 0)
+    finish(pairs - 1, pairs - 1)
+    if final:
+        own = 2 * pairs
+        for k, ref in enumerate(done):
+            acc_ref[:, own * (k + 1) : own * (k + 2), :] = ref[...]
         swapped = segment_swap(acc_ref[:, :blocks, :])
         rhs_count = field_ref.shape[1]
         for c in range(2):
@@ -352,19 +350,21 @@
     return pltpu.CompilerParams(vmem_limit_bytes=megabytes * 1024 * 1024)
 
 
-def run_send(chosen, counts, field, positions, normals, areas, v):
+def run_send(me, chosen, counts, field, positions, normals, areas, v):
     peers, cap, _, rank, width = v.shape
     rhs, span_rows = field.shape[1:3]
     chunks = 4
     blocks = width // SEG
     halo = blocks // 4
-    shapes = [(peers, 8, width), (blocks, 24, width), (halo, 24, width), (halo, 24, width)]
+    shapes = [(peers // chunks, 8, width)] * chunks
+    shapes += [(blocks, 24, width), (halo, 24, width), (halo, 24, width)]
     return pl.pallas_call(
         send_kernel,
-        in_specs=smem(2) + vmem(4) + [pl.BlockSpec(memory_space=pl.ANY)],
-        out_specs=vmem(4),
+        in_specs=smem(3) + vmem(4) + [pl.BlockSpec(memory_space=pl.ANY)],
+        out_specs=vmem(len(shapes)),
         out_shape=[jax.ShapeDtypeStruct(s, f32) for s in shapes],
         scratch_shapes=[
+            pltpu.VMEM((peers, 8, width), f32),
             pltpu.VMEM(v.shape, f32),
             pltpu.VMEM((span_rows, 16, 2 * width), bf16),
             pltpu.SemaphoreType.DMA((chunks,)),
@@ -372,72 +372,59 @@
         cost_estimate=cost(3 * 10**9, 4 * v.size),
         compiler_params=params(58),
         name="send",
-    )(chosen, counts, field.reshape(2 * rhs * span_rows, width), positions, normals, areas, v)
-
-
-def run_receive(targets, me, coef, u, span, span_rows):
+    )(me, chosen, counts, field.reshape(2 * rhs * span_rows, width), positions, normals, areas, v)
+
+
+def run_receive(targets, where, coefs, u, span, span_rows):
     width = u.shape[4]
     shape = (16, span_rows, width)
     return pl.pallas_call(
         receive_kernel,
-        in_specs=smem(2) + vmem(2),
+        in_specs=smem(2) + vmem(5),
         out_specs=vmem(span),
         out_shape=[jax.ShapeDtypeStruct(shape, f32)] * span,
-        scratch_shapes=[pltpu.VMEM((span * 16 * span_rows, width), f32)] * 4,
+        scratch_shapes=[pltpu.VMEM((u.shape[0], 8, width), f32)]
+        + [pltpu.VMEM((span * 16 * span_rows, width), f32)] * 4,
         cost_estimate=cost(3 * 10**9, 4 * u.size),
         compiler_params=params(12),
         name="receive",
-    )(targets, me, coef, u)
-
-
-def near_scratch(blocks, width, pairs, slots):
-    halo = blocks // 4
-    count = blocks + 2 * halo
-    span = 2 * width * (2 * halo + 2)
-    return [
-        pltpu.VMEM((count, 16, width), f32),
-        pltpu.VMEM((32, 2 * width * count), bf16),
-        pltpu.VMEM((4 * width, span), bf16),
-        pltpu.VMEM((4 * width, span), bf16),
-        pltpu.VMEM((pairs, 2 * width, 48), bf16),
-        pltpu.VMEM((pairs, 48, span), bf16),
-        pltpu.VMEM((2 * width, 32), f32),
-        pltpu.VMEM((16, 2 * slots + 2, width), f32),
-    ]
-
-
-def run_near_inner(mid):
+    )(targets, where, *coefs, u)
+
+
+def run_near(part, left, mid, right, done=(), field=None):
     blocks, _, width = mid.shape
     halo = blocks // 4
-    count = blocks - 2 * halo
+    pairs = halo // 2
+    sources = 2 * halo + 2
+    count = 2 * pairs + 2 * halo
+    final = field is not None
+    if final:
+        out_shape = [jax.ShapeDtypeStruct(field.shape, f32)]
+        args = (left, mid, right, *done, field)
+    else:
+        out_shape = [
+            jax.ShapeDtypeStruct((16, 2 * pairs, width), f32),
+            jax.ShapeDtypeStruct((8, width), f32),
+        ]
+        args = (left, mid, right)
     return pl.pallas_call(
-        functools.partial(near_kernel, halo // 2, count // 2, 0, False),
-        in_specs=vmem(1),
-        out_specs=vmem(2),
-        out_shape=[
-            jax.ShapeDtypeStruct((16, count, width), f32),
-            jax.ShapeDtypeStruct((8, width), f32),
+        functools.partial(near_kernel, part * pairs, final),
+        in_specs=vmem(len(args)),
+        out_specs=vmem(len(out_shape)),
+        out_shape=out_shape,
+        scratch_shapes=[
+            pltpu.VMEM((count, 16, width), f32),
+            pltpu.VMEM((32, 2 * width * count), bf16),
+            pltpu.VMEM((4 * width, 2 * width * sources), bf16),
+            pltpu.VMEM((pairs, 2 * width, 48), bf16),
+            pltpu.VMEM((pairs, 48, 2 * width * sources), bf16),
+            pltpu.VMEM((32, 4 * width), f32),
+            pltpu.VMEM((16, (blocks if final else 2 * pairs) + 2, width), f32),
         ],
-        scratch_shapes=near_scratch(blocks, width, count // 2, count // 2),
-        compiler_params=params(20),
-        cost_estimate=cost(10**10, 10**6),
-        name="near_inner",
-    )(mid)
-
-
-def run_near_edge(left, mid, right, done, field):
-    blocks, _, width = mid.shape
-    halo = left.shape[0]
-    return pl.pallas_call(
-        functools.partial(near_kernel, 0, halo // 2, blocks // 2 - halo, True),
-        in_specs=vmem(5),
-        out_specs=vmem()[0],
-        out_shape=jax.ShapeDtypeStruct(field.shape, f32),
-        scratch_shapes=near_scratch(blocks, width, halo, blocks // 2),
-        compiler_params=params(20),
-        cost_estimate=cost(10**10, 10**6),
-        name="near_edge",
-    )(left, mid, right, done, field)
+        cost_estimate=cost(5 * 10**9, 10**6),
+        compiler_params=params(12),
+        name=f"near_{part}",
+    )(*args)
 
 
 def shards(
@@ -447,7 +434,10 @@
     span = lax.axis_size("span")
     span_rows = field.shape[2]
     hold = lax.optimization_barrier
-    outgoing, mid, low, high = run_send(
+    sector = lax.axis_index("azim").astype(jnp.int32)
+    me = lax.axis_index("span").astype(jnp.int32)
+    *tiles, mid, low, high = run_send(
+        sector.reshape(1),
         col_cluster[0, 0].T,
         block_count[0],
         field,
@@ -456,16 +446,46 @@
         areas,
         v_factors.reshape(v_factors.shape[2:]),
     )
-    incoming = lax.all_to_all(outgoing, "azim", split_axis=0, concat_axis=0, tiled=True)
+
+    def trade(parts, stride):
+        moved = [parts[0]]
+        for k in range(1, 4):
+            pairs = [(i, i ^ (k * stride)) for i in range(azim)]
+            moved.append(lax.ppermute(parts[k], "azim", pairs))
+        return moved
+
+    def regroup(parts):
+        width = parts[0].shape[0] // 4
+        return [
+            jnp.concatenate([p[k * width : (k + 1) * width] for p in parts], 0) for k in range(4)
+        ]
+
+    tiles = trade(tiles, 16)
+    near_1, token = run_near(1, mid, mid, mid)
+    tiles, _ = hold((tiles, token))
+    tiles, mid, low, high = hold((regroup(tiles), mid, low, high))
+    tiles = trade(tiles, 4)
     forward = [(i, (i + 1) % azim) for i in range(azim)]
     backward = [(b, a) for a, b in forward]
     left = lax.ppermute(high, "azim", forward)
     right = lax.ppermute(low, "azim", backward)
-    inner, token = run_near_inner(mid)
-    incoming, _ = hold((incoming, token))
-    me = lax.axis_index("span").astype(jnp.int32).reshape(1)
+    near_2, token = run_near(2, mid, mid, mid)
+    tiles, left, right, _ = hold((tiles, left, right, token))
+    tiles = [
+        jnp.stack([p.reshape(4, 4, *p.shape[1:])[:, k] for p in tiles], 0).reshape(tiles[0].shape)
+        for k in range(4)
+    ]
+    tiles, mid = hold((tiles, mid))
+    tiles = trade(tiles, 1)
+    near_3, token = run_near(3, left, mid, right)
+    tiles, _ = hold((tiles, token))
     pieces = run_receive(
-        row_cluster[0, 0].T, me, incoming, u_factors.reshape(u_factors.shape[2:]), span, span_rows
+        row_cluster[0, 0].T,
+        jnp.stack([me, sector]),
+        tiles,
+        u_factors.reshape(u_factors.shape[2:]),
+        span,
+        span_rows,
     )
     mid, *pieces = hold((mid, *pieces))
     total = pieces[0]
@@ -473,7 +493,7 @@
     for k in range(1, span):
         ring = [(i, (i + k) % span) for i in range(span)]
         others.append(lax.ppermute(pieces[k], "span", ring))
-    near = run_near_edge(left, mid, right, inner, field)
+    (near,) = run_near(0, left, mid, right, (near_1, near_2, near_3), field)
     for other in others:
         total = total + other
     return near + total.reshape(near.shape)

time: 55.9 us -> 63 us (1.13)
  starting transfers between devices: 25.3 us -> 30.6 us
  Pallas kernels: 28 us -> 30.1 us
    ppermute x0 -> x9, starting transfers between devices: none -> 17.2 us  [trade(): moved.append(lax.ppermute(parts[k], 'azim', pairs))]
    all_to_all x1 -> x0, starting transfers between devices: 15.1 us -> none  [shards(): lax.all_to_all(outgoing, 'azim', split_axis=0, concat_axis=0, tiled=True)]
    ppermute x3, starting transfers between devices: 2.95 us -> 5.29 us  [shards(): others.append(lax.ppermute(pieces[k], 'span', ring))]
    pallas_call x4 -> x6, Pallas kernels: 28 us -> 30.1 us  [the longest x4 21.8 us: run_near(): pl.pallas_call(functools.partial(near_kernel, part * pairs, final), in_sp...]
    ppermute x1, starting transfers between devices: 6.18 us -> 6.82 us  [shards(): right = lax.ppermute(low, 'azim', backward)]
  transfers between devices with their start and end apart: 6 -> 14, of which waited for: 0 -> 0; matrix products, arithmetic and copies ran while one was open for 0% -> 0% of each run, Pallas kernels for 40% -> 35%
where the time goes in v4:
time: 63 us; the launch traced here: 62.8 us
  starting transfers between devices  30.6 us (49%)
  Pallas kernels  30.1 us (48%)
  local copies, waits for them, and re-layouts  1.01 us (2%)
  other arithmetic  0.85 us (1%)
    pallas_call x4, Pallas kernels, run_near(): pl.pallas_call(functools.partial(near_kernel, part * pairs, final), in_sp...  21.8 us
    ppermute x9, starting transfers between devices, trade(): moved.append(lax.ppermute(parts[k], 'azim', pairs))  17.2 us
    ppermute x1, starting transfers between devices, shards(): right = lax.ppermute(low, 'azim', backward)  6.82 us
    pallas_call x1, Pallas kernels, run_send(): pl.pallas_call(send_kernel, in_specs=smem(3) + vmem(4) + [pl.BlockSpec(me...  5.81 us
    ppermute x3, starting transfers between devices, shards(): others.append(lax.ppermute(pieces[k], 'span', ring))  5.29 us
    pallas_call x1, Pallas kernels, run_receive(): pl.pallas_call(receive_kernel, in_specs=smem(2) + vmem(5), out_specs=vmem...  2.49 us
    ppermute x1, starting transfers between devices, shards(): left = lax.ppermute(high, 'azim', forward)  1.29 us
  transfers between devices with their start and end apart: 14, of which 0 were waited for; matrix products, arithmetic and copies ran while one was open for 0% of the time, Pallas kernels for 35%

profile of v4, /device:TPU:1, one launch (start us, length us, event | category | flops | bytes accessed | tf_op | source)
XLA Modules:
  0.0 62.8 jit_solution(16295155459702442929)
XLA Ops:
  0.0 5.8 %send.1 = (f32[16,8,128]{2,1,0:T(8,128)}, f32[16,8,128]{2,1,0:T(8,128)}, f32[16,8,128]{2,1,0:T(8,128)}, f32[16,8,128]{2,1,0:T(8,128)}, f32[16,24,128]{2,1,0:T(8,...) custom-call(s32[1]{0:T(128)} %bitcast.me_ref, s32[2,64]{1,0:T(2,128)} %bitcast.98, s32[1,64]{1,0:T(1,128)} %bitcast.99, ...), custom_call_target="tpu_custom_call" | custom-call | flops 3000000000 | bytes 3145728 | tf_op jit(solution)/shard_map/send/pallas_call | solution.py:361
  5.8 3.9 %collective-permute-start = (f32[16,8,128]{2,1,0:T(8,128)}, f32[16,8,128]{2,1,0:T(8,128)S(1)}, u32[]{:S(2)}, u32[]{:S(2)}) collective-permute-start(f32[16,8,128]{2,1,0:T(8,128)} %get-tuple-element.51), channel_id=1, source_target_pairs={{0,64},{4,68},{8,72},{12,76},{16,80},{20,84},{24,88},{28,92},{32,9... | collective-permute-start | bytes 196616 | tf_op jit(solution)/shard_map/ppermute | solution.py:454
  9.7 5.1 %collective-permute-start.1 = (f32[16,8,128]{2,1,0:T(8,128)}, f32[16,8,128]{2,1,0:T(8,128)S(1)}, u32[]{:S(2)}, u32[]{:S(2)}) collective-permute-start(f32[16,8,128]{2,1,0:T(8,128)} %get-tuple-element.52), channel_id=1, source_target_pairs={{0,128},{4,132},{8,136},{12,140},{16,144},{20,148},{24,152},{28,15... | collective-permute-start | bytes 196616 | tf_op jit(solution)/shard_map/ppermute | solution.py:454
  14.8 0.0 collective-permute-start.2
  14.8 0.0 copy-start.3
  14.8 0.9 %copy-done.3 = f32[16,24,128]{2,1,0:T(8,128)S(1)} copy-done((f32[16,24,128]{2,1,0:T(8,128)S(1)}, f32[16,24,128]{2,1,0:T(8,128)}, u32[]{:S(2)}) %copy-start.3) | copy-done | bytes 196632
  15.8 0.0 copy-start.4
  15.8 5.5 %near_1.1 = (f32[16,4,128]{2,1,0:T(4,128)S(1)}, f32[8,128]{1,0:T(8,128)}) custom-call(f32[16,24,128]{2,1,0:T(8,128)S(1)} %copy-done.3, f32[16,24,128]{2,1,0:T(8,128)S(1)} %copy-done.3, f32[16,24,128]{2,1,0:T(8,128)S(1)} %copy-done.3), custom_call_target="tpu_custom_call" | custom-call | flops 5000000000 | bytes 1000000 | tf_op jit(solution)/shard_map/near_1/pallas_call | solution.py:410
  21.2 0.1 pad_add_fusion.me_ref
  21.3 0.0 collective-permute-done
  21.3 0.0 collective-permute-done.1
  21.3 0.0 collective-permute-done.2
  21.3 0.0 copy-done.4
  21.4 2.8 %collective-permute-start.3 = (f32[16,8,128]{2,1,0:T(8,128)S(1)}, f32[16,8,128]{2,1,0:T(8,128)S(1)}, u32[]{:S(2)}, u32[]{:S(2)}) collective-permute-start(f32[16,8,128]{2,1,0:T(8,128)S(1)} %pad_maximum_fusion.1), channel_id=1, source_target_pairs={{0,16},{4,20},{8,24},{12,28},{16,0},{20,4},{24,8},{28,12},{32,48},... | collective-permute-start | bytes 196616 | tf_op jit(solution)/shard_map/ppermute | solution.py:454
  24.3 0.7 %collective-permute-start.4 = (f32[16,8,128]{2,1,0:T(8,128)S(1)}, f32[16,8,128]{2,1,0:T(8,128)S(1)}, u32[]{:S(2)}, u32[]{:S(2)}) collective-permute-start(f32[16,8,128]{2,1,0:T(8,128)S(1)} %pad_maximum_fusion.2), channel_id=1, source_target_pairs={{0,32},{4,36},{8,40},{12,44},{16,48},{20,52},{24,56},{28,60},{32,0... | collective-permute-start | bytes 196616 | tf_op jit(solution)/shard_map/ppermute | solution.py:454
  25.0 0.7 %collective-permute-start.5 = (f32[16,8,128]{2,1,0:T(8,128)S(1)}, f32[16,8,128]{2,1,0:T(8,128)S(1)}, u32[]{:S(2)}, u32[]{:S(2)}) collective-permute-start(f32[16,8,128]{2,1,0:T(8,128)S(1)} %pad_maximum_fusion.3), channel_id=1, source_target_pairs={{0,48},{4,52},{8,56},{12,60},{16,32},{20,36},{24,40},{28,44},{32,1... | collective-permute-start | bytes 196616 | tf_op jit(solution)/shard_map/ppermute | solution.py:454
  25.7 0.0 copy-done.6
  25.7 1.3 %collective-permute-start.6 = (f32[4,24,128]{2,1,0:T(8,128)S(1)}, f32[4,24,128]{2,1,0:T(8,128)S(1)}, u32[]{:S(2)}, u32[]{:S(2)}) collective-permute-start(f32[4,24,128]{2,1,0:T(8,128)S(1)} %copy-done.6), channel_id=1, source_target_pairs={{0,4},{4,8},{8,12},{12,16},{16,20},{20,24},{24,28},{28,32},{32,36}... | collective-permute-start | bytes 147464 | tf_op jit(solution)/shard_map/ppermute | solution.py:470
  27.0 0.0 copy-done.5
  27.0 6.8 %collective-permute-start.7 = (f32[4,24,128]{2,1,0:T(8,128)S(1)}, f32[4,24,128]{2,1,0:T(8,128)S(1)}, u32[]{:S(2)}, u32[]{:S(2)}) collective-permute-start(f32[4,24,128]{2,1,0:T(8,128)S(1)} %copy-done.5), channel_id=1, source_target_pairs={{4,0},{8,4},{12,8},{16,12},{20,16},{24,20},{28,24},{32,28},{36,32}... | collective-permute-start | bytes 147464 | tf_op jit(solution)/shard_map/ppermute | solution.py:471
  33.8 5.5 %near_2.1 = (f32[16,4,128]{2,1,0:T(4,128)S(1)}, f32[8,128]{1,0:T(8,128)}) custom-call(f32[16,24,128]{2,1,0:T(8,128)S(1)} %copy-done.3, f32[16,24,128]{2,1,0:T(8,128)S(1)} %copy-done.3, f32[16,24,128]{2,1,0:T(8,128)S(1)} %copy-done.3), custom_call_target="tpu_custom_call" | custom-call | flops 5000000000 | bytes 1000000 | tf_op jit(solution)/shard_map/near_2/pallas_call | solution.py:410
  39.2 0.0 collective-permute-done.6.refs_0_
  39.3 0.0 collective-permute-done.7.refs_2_
  39.3 0.0 collective-permute-done.3
  39.3 0.0 collective-permute-done.4
  39.3 0.0 collective-permute-done.5
  39.4 0.0 copy-start
  39.4 0.0 copy-start.2
  39.4 0.1 collective-permute-start.8
  39.5 0.1 collective-permute-start.9
  39.6 3.7 %collective-permute-start.10 = (f32[16,8,128]{2,1,0:T(8,128)S(1)}, f32[16,8,128]{2,1,0:T(8,128)S(1)}, u32[]{:S(2)}, u32[]{:S(2)}) collective-permute-start(f32[16,8,128]{2,1,0:T(8,128)S(1)} %bitcast.96), channel_id=1, source_target_pairs={{0,12},{4,8},{8,4},{12,0},{16,28},{20,24},{24,20},{28,16},{32,44},... | collective-permute-start | bytes 196616 | tf_op jit(solution)/shard_map/ppermute | solution.py:454
  43.4 5.5 %near_3.1 = (f32[16,4,128]{2,1,0:T(4,128)S(1)}, f32[8,128]{1,0:T(8,128)}) custom-call(f32[4,24,128]{2,1,0:T(8,128)S(1)} %collective-permute-done.6.refs_0_, f32[16,24,128]{2,1,0:T(8,128)S(1)} %copy-done.3, f32[4,24,128]{2,1,0:T(8,128)S(1)} %collective-permute-done.7.refs_2_), custom_call_target="tpu_custom_call" | custom-call | flops 5000000000 | bytes 1000000 | tf_op jit(solution)/shard_map/near_3/pallas_call | solution.py:410
  48.8 0.0 collective-permute-done.8.rest_1_
  48.8 0.0 collective-permute-done.9.rest_2_
  48.8 0.0 collective-permute-done.10.rest_3_
  48.8 0.0 copy-done
  48.9 0.0 copy-done.2
  48.9 0.0 copy-start.1
  48.9 2.5 %receive.1 = (f32[16,16,128]{2,1,0:T(8,128)S(1)}, f32[16,16,128]{2,1,0:T(8,128)S(1)}, f32[16,16,128]{2,1,0:T(8,128)S(1)}, f32[16,16,128]{2,1,0:T(8,128)S(1)}) custom-call(s32[2,64]{1,0:T(2,128)S(1)} %bitcast.88, s32[2]{0:T(128)S(1)} %pad_add_fusion.me_ref, f32[16,8,128]{2,1,0:T(8,128)S(1)} %bitcast.85, f32[16,8,128]{2,1,0:T(8,128)S(1)} %collective-permute-done.8.rest_1_, ...), custom_call_target="tpu_custom_call" | custom-call | flops 3000000000 | bytes 3145728 | tf_op jit(solution)/shard_map/receive/pallas_call | solution.py:381
  51.4 3.6 %collective-permute-start.13 = (f32[16,16,128]{2,1,0:T(8,128)S(1)}, f32[16,16,128]{2,1,0:T(8,128)S(1)}, u32[]{:S(2)}, u32[]{:S(2)}) collective-permute-start(f32[16,16,128]{2,1,0:T(8,128)S(1)} %get-tuple-element.94), channel_id=1, source_target_pairs={{0,3},{1,0},{2,1},{3,2},{4,7},{5,4},{6,5},{7,6},{8,11},{9,8},{10,9... | collective-permute-start | bytes 393224 | tf_op jit(solution)/shard_map/ppermute | solution.py:495
  54.9 0.4 collective-permute-start.12
  55.3 1.3 %collective-permute-start.11 = (f32[16,16,128]{2,1,0:T(8,128)S(1)}, f32[16,16,128]{2,1,0:T(8,128)S(1)}, u32[]{:S(2)}, u32[]{:S(2)}) collective-permute-start(f32[16,16,128]{2,1,0:T(8,128)S(1)} %get-tuple-element.92), channel_id=1, source_target_pairs={{0,1},{1,2},{2,3},{3,0},{4,5},{5,6},{6,7},{7,4},{8,9},{9,10},{10,1... | collective-permute-start | bytes 393224 | tf_op jit(solution)/shard_map/ppermute | solution.py:495
  56.7 0.0 copy-done.1
  56.7 5.4 %near_0.1 = f32[2,8,16,128]{3,2,1,0:T(8,128)S(1)} custom-call(f32[4,24,128]{2,1,0:T(8,128)S(1)} %collective-permute-done.6.refs_0_, f32[16,24,128]{2,1,0:T(8,128)S(1)} %copy-done.3, f32[4,24,128]{2,1,0:T(8,128)S(1)} %collective-permute-done.7.refs_2_, f32[16,4,128]{2,1,0:T(4,128)S(1)} %get-tuple-element.88.refs_3_, ...), custom_call_target="tpu_custom_call" | custom-call | flops 5000000000 | bytes 1000000 | tf_op jit(solution)/shard_map/near_0/pallas_call | solution.py:410
  62.1 0.0 collective-permute-done.13
  62.1 0.0 collective-permute-done.12
  62.1 0.0 collective-permute-done.11
  62.2 0.7 %add.15 = f32[2,8,16,128]{3,2,1,0:T(8,128)} add(f32[2,8,16,128]{3,2,1,0:T(8,128)S(1)} %near_0.1, f32[2,8,16,128]{3,2,1,0:T(8,128)S(1)} %bitcast.89) | non-fusion elementwise | flops 32768 | bytes 393216 | tf_op jit(solution)/shard_map/add | solution.py:499
  (17 shorter events, 0.2 us)
Async XLA Ops:
  5.8 15.5 %collective-permute-start = (f32[16,8,128]{2,1,0:T(8,128)}, f32[16,8,128]{2,1,0:T(8,128)S(1)}, u32[]{:S(2)}, u32[]{:S(2)}) collective-permute-start(f32[16,8,128]{2,1,0:T(8,128)} %get-tuple-element.51), channel_id=1, source_target_pairs={{0,64},{4,68},{8,72},{12,76},{16,80},{20,84},{24,88},{28,92},{32,9... | collective-permute-start | bytes 196616 | tf_op jit(solution)/shard_map/ppermute | solution.py:454
  9.7 11.6 %collective-permute-start.1 = (f32[16,8,128]{2,1,0:T(8,128)}, f32[16,8,128]{2,1,0:T(8,128)S(1)}, u32[]{:S(2)}, u32[]{:S(2)}) collective-permute-start(f32[16,8,128]{2,1,0:T(8,128)} %get-tuple-element.52), channel_id=1, source_target_pairs={{0,128},{4,132},{8,136},{12,140},{16,144},{20,148},{24,152},{28,15... | collective-permute-start | bytes 196616 | tf_op jit(solution)/shard_map/ppermute | solution.py:454
  14.8 6.5 %collective-permute-start.2 = (f32[16,8,128]{2,1,0:T(8,128)}, f32[16,8,128]{2,1,0:T(8,128)S(1)}, u32[]{:S(2)}, u32[]{:S(2)}) collective-permute-start(f32[16,8,128]{2,1,0:T(8,128)} %get-tuple-element.53), channel_id=1, source_target_pairs={{0,192},{4,196},{8,200},{12,204},{16,208},{20,212},{24,216},{28,22... | collective-permute-start | bytes 196616 | tf_op jit(solution)/shard_map/ppermute | solution.py:454
  14.8 0.9 %copy-start.3 = (f32[16,24,128]{2,1,0:T(8,128)S(1)}, f32[16,24,128]{2,1,0:T(8,128)}, u32[]{:S(2)}) copy-start(f32[16,24,128]{2,1,0:T(8,128)} %get-tuple-element.86.refs_0_.refs_1_.refs_2_) | copy-start | bytes 589828
  15.8 5.6 %copy-start.4 = (f32[16,8,128]{2,1,0:T(8,128)S(1)}, f32[16,8,128]{2,1,0:T(8,128)}, u32[]{:S(2)}) copy-start(f32[16,8,128]{2,1,0:T(8,128)} %get-tuple-element.54) | copy-start | bytes 196612
  15.8 9.9 %copy-start.6 = (f32[4,24,128]{2,1,0:T(8,128)S(1)}, f32[4,24,128]{2,1,0:T(8,128)}, u32[]{:S(2)}) copy-start(f32[4,24,128]{2,1,0:T(8,128)} %get-tuple-element.65) | copy-start | bytes 147460
  15.8 11.2 %copy-start.5 = (f32[4,24,128]{2,1,0:T(8,128)S(1)}, f32[4,24,128]{2,1,0:T(8,128)}, u32[]{:S(2)}) copy-start(f32[4,24,128]{2,1,0:T(8,128)} %get-tuple-element.66) | copy-start | bytes 147460
  21.4 17.8 %collective-permute-start.3 = (f32[16,8,128]{2,1,0:T(8,128)S(1)}, f32[16,8,128]{2,1,0:T(8,128)S(1)}, u32[]{:S(2)}, u32[]{:S(2)}) collective-permute-start(f32[16,8,128]{2,1,0:T(8,128)S(1)} %pad_maximum_fusion.1), channel_id=1, source_target_pairs={{0,16},{4,20},{8,24},{12,28},{16,0},{20,4},{24,8},{28,12},{32,48},... | collective-permute-start | bytes 196616 | tf_op jit(solution)/shard_map/ppermute | solution.py:454
  24.3 15.0 %collective-permute-start.4 = (f32[16,8,128]{2,1,0:T(8,128)S(1)}, f32[16,8,128]{2,1,0:T(8,128)S(1)}, u32[]{:S(2)}, u32[]{:S(2)}) collective-permute-start(f32[16,8,128]{2,1,0:T(8,128)S(1)} %pad_maximum_fusion.2), channel_id=1, source_target_pairs={{0,32},{4,36},{8,40},{12,44},{16,48},{20,52},{24,56},{28,60},{32,0... | collective-permute-start | bytes 196616 | tf_op jit(solution)/shard_map/ppermute | solution.py:454
  25.0 14.3 %collective-permute-start.5 = (f32[16,8,128]{2,1,0:T(8,128)S(1)}, f32[16,8,128]{2,1,0:T(8,128)S(1)}, u32[]{:S(2)}, u32[]{:S(2)}) collective-permute-start(f32[16,8,128]{2,1,0:T(8,128)S(1)} %pad_maximum_fusion.3), channel_id=1, source_target_pairs={{0,48},{4,52},{8,56},{12,60},{16,32},{20,36},{24,40},{28,44},{32,1... | collective-permute-start | bytes 196616 | tf_op jit(solution)/shard_map/ppermute | solution.py:454
  25.7 13.6 %collective-permute-start.6 = (f32[4,24,128]{2,1,0:T(8,128)S(1)}, f32[4,24,128]{2,1,0:T(8,128)S(1)}, u32[]{:S(2)}, u32[]{:S(2)}) collective-permute-start(f32[4,24,128]{2,1,0:T(8,128)S(1)} %copy-done.6), channel_id=1, source_target_pairs={{0,4},{4,8},{8,12},{12,16},{16,20},{20,24},{24,28},{28,32},{32,36}... | collective-permute-start | bytes 147464 | tf_op jit(solution)/shard_map/ppermute | solution.py:470
  27.0 12.3 %collective-permute-start.7 = (f32[4,24,128]{2,1,0:T(8,128)S(1)}, f32[4,24,128]{2,1,0:T(8,128)S(1)}, u32[]{:S(2)}, u32[]{:S(2)}) collective-permute-start(f32[4,24,128]{2,1,0:T(8,128)S(1)} %copy-done.5), channel_id=1, source_target_pairs={{4,0},{8,4},{12,8},{16,12},{20,16},{24,20},{28,24},{32,28},{36,32}... | collective-permute-start | bytes 147464 | tf_op jit(solution)/shard_map/ppermute | solution.py:471
  39.4 9.4 %copy-start = (f32[1,1,64,2,2,24,128]{6,5,4,3,2,1,0:T(8,128)S(1)}, f32[1,1,64,2,2,24,128]{6,5,4,3,2,1,0:T(8,128)}, u32[]{:S(2)}) copy-start(f32[1,1,64,2,2,24,128]{6,5,4,3,2,1,0:T(8,128)} %param.17) | copy-start | bytes 9437188
  39.4 9.4 %copy-start.2 = (s32[1,1,64,2]{2,3,1,0:T(2,128)S(1)}, s32[1,1,64,2]{2,3,1,0:T(2,128)}, u32[]{:S(2)}) copy-start(s32[1,1,64,2]{2,3,1,0:T(2,128)} %param.15) | copy-start | bytes 1540
  39.4 9.4 %collective-permute-start.8 = (f32[16,8,128]{2,1,0:T(8,128)S(1)}, f32[16,8,128]{2,1,0:T(8,128)S(1)}, u32[]{:S(2)}, u32[]{:S(2)}) collective-permute-start(f32[16,8,128]{2,1,0:T(8,128)S(1)} %bitcast.94), channel_id=1, source_target_pairs={{0,4},{4,0},{8,12},{12,8},{16,20},{20,16},{24,28},{28,24},{32,36},... | collective-permute-start | bytes 196616 | tf_op jit(solution)/shard_map/ppermute | solution.py:454
  39.5 9.3 %collective-permute-start.9 = (f32[16,8,128]{2,1,0:T(8,128)S(1)}, f32[16,8,128]{2,1,0:T(8,128)S(1)}, u32[]{:S(2)}, u32[]{:S(2)}) collective-permute-start(f32[16,8,128]{2,1,0:T(8,128)S(1)} %bitcast.95), channel_id=1, source_target_pairs={{0,8},{4,12},{8,0},{12,4},{16,24},{20,28},{24,16},{28,20},{32,40},... | collective-permute-start | bytes 196616 | tf_op jit(solution)/shard_map/ppermute | solution.py:454
  39.6 9.2 %collective-permute-start.10 = (f32[16,8,128]{2,1,0:T(8,128)S(1)}, f32[16,8,128]{2,1,0:T(8,128)S(1)}, u32[]{:S(2)}, u32[]{:S(2)}) collective-permute-start(f32[16,8,128]{2,1,0:T(8,128)S(1)} %bitcast.96), channel_id=1, source_target_pairs={{0,12},{4,8},{8,4},{12,0},{16,28},{20,24},{24,20},{28,16},{32,44},... | collective-permute-start | bytes 196616 | tf_op jit(solution)/shard_map/ppermute | solution.py:454
  48.9 7.8 %copy-start.1 = (f32[2,8,16,128]{3,2,1,0:T(8,128)S(1)}, f32[2,8,16,128]{3,2,1,0:T(8,128)}, u32[]{:S(2)}) copy-start(f32[2,8,16,128]{3,2,1,0:T(8,128)} %refs_6_.1) | copy-start | bytes 393220
  51.4 10.7 %collective-permute-start.13 = (f32[16,16,128]{2,1,0:T(8,128)S(1)}, f32[16,16,128]{2,1,0:T(8,128)S(1)}, u32[]{:S(2)}, u32[]{:S(2)}) collective-permute-start(f32[16,16,128]{2,1,0:T(8,128)S(1)} %get-tuple-element.94), channel_id=1, source_target_pairs={{0,3},{1,0},{2,1},{3,2},{4,7},{5,4},{6,5},{7,6},{8,11},{9,8},{10,9... | collective-permute-start | bytes 393224 | tf_op jit(solution)/shard_map/ppermute | solution.py:495
  54.9 7.2 %collective-permute-start.12 = (f32[16,16,128]{2,1,0:T(8,128)S(1)}, f32[16,16,128]{2,1,0:T(8,128)S(1)}, u32[]{:S(2)}, u32[]{:S(2)}) collective-permute-start(f32[16,16,128]{2,1,0:T(8,128)S(1)} %get-tuple-element.93), channel_id=1, source_target_pairs={{0,2},{1,3},{2,0},{3,1},{4,6},{5,7},{6,4},{7,5},{8,10},{9,11},{10,... | collective-permute-start | bytes 393224 | tf_op jit(solution)/shard_map/ppermute | solution.py:495
  55.3 6.8 %collective-permute-start.11 = (f32[16,16,128]{2,1,0:T(8,128)S(1)}, f32[16,16,128]{2,1,0:T(8,128)S(1)}, u32[]{:S(2)}, u32[]{:S(2)}) collective-permute-start(f32[16,16,128]{2,1,0:T(8,128)S(1)} %get-tuple-element.92), channel_id=1, source_target_pairs={{0,1},{1,2},{2,3},{3,0},{4,5},{5,6},{6,7},{7,4},{8,9},{9,10},{10,1... | collective-permute-start | bytes 393224 | tf_op jit(solution)/shard_map/ppermute | solution.py:495

commit v5 on v3

--- a/solution.py
+++ b/solution.py
@@ -165,12 +165,12 @@
 
 
 def near_kernel(begin, count, skip, edge, *refs):
-    scratch = refs[-8:]
-    pos_ref, wide_ref, kern_even, kern_odd, target_ref, source_ref, part_ref, acc_ref = scratch
+    scratch = refs[-7:]
+    pos_ref, wide_ref, kern_ref, target_ref, source_ref, part_ref, acc_ref = scratch
     if edge:
-        left_ref, mid_ref, right_ref, done_ref, field_ref, out_ref = refs[:-8]
+        left_ref, mid_ref, right_ref, done_ref, field_ref, out_ref = refs[:-7]
     else:
-        mid_ref, out_ref, token_ref = refs[:-8]
+        mid_ref, out_ref, token_ref = refs[:-7]
     blocks = mid_ref.shape[0]
     halo = blocks // 4
     window = 2 * halo + 1
@@ -196,13 +196,12 @@
             [jnp.concatenate([re, -im], 1), jnp.concatenate([im, re], 1)], 0
         )
         high, low = split_two(rows)
-        wide_ref[:, 2 * width * b : 2 * width * (b + 1)] = jnp.concatenate([high, low], 0)
+        wide_ref[:, 2 * width * b : 2 * width * (b + 1)] = jnp.concatenate([high, low], 0).astype(f32)
     sources = window + 1
-    zeros = jnp.zeros((width, 2 * width), bf16)
-    for kern_ref in (kern_even, kern_odd):
-        for part in (0, 2):
-            kern_ref[(part + 1) * width : (part + 2) * width, : 2 * width] = zeros
-            kern_ref[part * width : (part + 1) * width, 2 * width * (sources - 1) :] = zeros
+    zeros = jnp.zeros((width, 2 * width), f32)
+    for part in (0, 2):
+        kern_ref[(part + 1) * width : (part + 2) * width, : 2 * width] = zeros
+        kern_ref[part * width : (part + 1) * width, 2 * width * (sources - 1) :] = zeros
 
     chunk = 16
     sub = lax.broadcasted_iota(jnp.int32, (chunk, width), 0)
@@ -270,60 +269,68 @@
             source_ref[step, :, cols] = jnp.concatenate(wide, 1).astype(bf16)
         return carry
 
-    def pair_kernels(step, kern_ref, finish):
+    batch = 2
+
+    def sums(step, index):
+        size = 2 * width * batch
+        start = pl.multiple_of(pair_of(step) * (4 * width) + size * index, 2 * width)
+        prod = dot_nt(
+            kern_ref[:, size * index : size * (index + 1)], wide_ref[:, pl.ds(start, size)]
+        )
+        return prod[: 2 * width] + prod[2 * width :]
+
+    def finish(step, slot):
+        prod = part_ref[...] + sums(step, sources // batch - 1)
+        for t in range(2):
+            half = jnp.transpose(prod[t * width : (t + 1) * width])
+            acc_ref[:, pl.ds(2 * slot + t, 1), :] = (half[:16] + half[16:])[:, None, :]
+
+    pairs = 2 * count if edge else count
+    spare = acc_ref.shape[1] // 2 - 1
+
+    def slot_of(step):
+        return pair_of(step) if edge else step
+
+    def rows_of(sb):
+        return (width if sb == sources - 1 else 0), (width if sb == 0 else 2 * width)
+
+    def gram_of(step, sb):
+        start, stop = rows_of(sb)
+        return jnp.dot(
+            target_ref[step, start:stop, :],
+            source_ref[step, :, 2 * width * sb : 2 * width * (sb + 1)],
+            preferred_element_type=f32,
+        )
+
+    def one_pair(step, carry):
         for sb in range(sources):
-            if sb == 3:
-                finish()
-            if sb == sources - 2:
-                part_ref[...] = partial_sums(step, kern_ref, 0)
-            start = width if sb == sources - 1 else 0
-            stop = width if sb == 0 else 2 * width
-            gram = jnp.dot(
-                target_ref[step, start:stop, :],
-                source_ref[step, :, 2 * width * sb : 2 * width * (sb + 1)],
-                preferred_element_type=f32,
-            )
+            start, stop = rows_of(sb)
+            gram = gram_of(step, sb)
+            done = sb - 1 if sb % batch == 1 % batch else -1
+            if sb == 1:
+                last = jnp.maximum(step - 1, 0)
+                finish(last, jnp.where(step == 0, spare, slot_of(last)))
+            elif sb > batch and done >= 0:
+                index = done // batch - 1
+                if index == 0:
+                    part_ref[...] = sums(step, 0)
+                else:
+                    part_ref[...] += sums(step, index)
             for at in range(start, stop, chunk):
                 t = at // width
                 part = gram[at - start : at - start + chunk]
                 kern = evaluate(part[:, :width], part[:, width:], at % width, sb - halo - t)
                 for value, shift in zip(kern, (0, width)):
-                    high, low = split_two(value)
+                    high, low = value, value - value.astype(bf16).astype(f32)
                     cols = slice(2 * width * sb + shift, 2 * width * sb + shift + width)
                     kern_ref[at : at + chunk, cols] = high
                     kern_ref[2 * width + at : 2 * width + at + chunk, cols] = low
-
-    def partial_sums(step, kern_ref, half):
-        size = width * sources
-        start = pl.multiple_of(pair_of(step) * (4 * width) + half * size, 2 * width)
-        cols = slice(half * size, (half + 1) * size)
-        prod = dot_nt(kern_ref[:, cols], wide_ref[:, pl.ds(start, size)])
-        return prod[: 2 * width] + prod[2 * width :]
-
-    def pair_sums(step, slot, kern_ref):
-        prod = part_ref[...] + partial_sums(step, kern_ref, 1)
-        for t in range(2):
-            half = jnp.transpose(prod[t * width : (t + 1) * width])
-            acc_ref[:, pl.ds(2 * slot + t, 1), :] = (half[:16] + half[16:])[:, None, :]
-
-    pairs = 2 * count if edge else count
-    spare = acc_ref.shape[1] // 2 - 1
-
-    def slot_of(step):
-        return pair_of(step) if edge else step
-
-    def two_pairs(index, carry):
-        last = jnp.maximum(2 * index - 1, 0)
-        slot = jnp.where(index == 0, spare, slot_of(last))
-        even = 2 * index
-        pair_kernels(even, kern_even, lambda: pair_sums(last, slot, kern_odd))
-        pair_kernels(even + 1, kern_odd, lambda: pair_sums(even, slot_of(even), kern_even))
         return carry
 
     part_ref[...] = jnp.zeros_like(part_ref)
     lax.fori_loop(0, pairs, prepare, 0)
-    lax.fori_loop(0, pairs // 2, two_pairs, 0)
-    pair_sums(pairs - 1, slot_of(pairs - 1), kern_odd)
+    lax.fori_loop(0, pairs, one_pair, 0)
+    finish(pairs - 1, slot_of(pairs - 1))
     if edge:
         acc_ref[:, 2 * count : 2 * (count + skip), :] = done_ref[...]
         swapped = segment_swap(acc_ref[:, :blocks, :])
@@ -396,9 +403,8 @@
     span = 2 * width * (2 * halo + 2)
     return [
         pltpu.VMEM((count, 16, width), f32),
-        pltpu.VMEM((32, 2 * width * count), bf16),
-        pltpu.VMEM((4 * width, span), bf16),
-        pltpu.VMEM((4 * width, span), bf16),
+        pltpu.VMEM((32, 2 * width * count), f32),
+        pltpu.VMEM((4 * width, span), f32),
         pltpu.VMEM((pairs, 2 * width, 48), bf16),
         pltpu.VMEM((pairs, 48, span), bf16),
         pltpu.VMEM((2 * width, 32), f32),

time: 55.9 us -> 53.8 us (0.962)
  Pallas kernels: 28 us -> 25.8 us
    pallas_call x1, Pallas kernels: 10.2 us -> 9 us  [run_near_edge(): pl.pallas_call(functools.partial(near_kernel, 0, halo // 2, blocks // 2 -...]
    pallas_call x1, Pallas kernels: 9.9 us -> 8.9 us  [run_near_inner(): pl.pallas_call(functools.partial(near_kernel, halo // 2, count // 2, 0, F...]
  transfers between devices with their start and end apart: 6 -> 6, of which waited for: 0 -> 0; matrix products, arithmetic and copies ran while one was open for 0% -> 0% of each run, Pallas kernels for 40% -> 38%
where the time goes in v5:
time: 53.8 us; the launch traced here: 53.6 us
  Pallas kernels  25.8 us (48%)
  starting transfers between devices  25.4 us (47%)
  local copies, waits for them, and re-layouts  1.58 us (3%)
  other arithmetic  0.71 us (1%)
    all_to_all x1, starting transfers between devices, shards(): lax.all_to_all(outgoing, 'azim', split_axis=0, concat_axis=0, tiled=True)  15.1 us
    pallas_call x1, Pallas kernels, run_near_edge(): pl.pallas_call(functools.partial(near_kernel, 0, halo // 2, blocks // 2 -...  9 us
    pallas_call x1, Pallas kernels, run_near_inner(): pl.pallas_call(functools.partial(near_kernel, halo // 2, count // 2, 0, F...  8.9 us
    ppermute x1, starting transfers between devices, shards(): right = lax.ppermute(low, 'azim', backward)  6.18 us
    pallas_call x1, Pallas kernels, run_send(): pl.pallas_call(send_kernel, in_specs=smem(2) + vmem(4) + [pl.BlockSpec(me...  5.46 us
    ppermute x3, starting transfers between devices, shards(): others.append(lax.ppermute(pieces[k], 'span', ring))  2.96 us
    pallas_call x1, Pallas kernels, run_receive(): pl.pallas_call(receive_kernel, in_specs=smem(2) + vmem(2), out_specs=vmem...  2.44 us
    unnamed x14, local copies, waits for them, and re-layouts  1.58 us
  transfers between devices with their start and end apart: 6, of which 0 were waited for; matrix products, arithmetic and copies ran while one was open for 0% of the time, Pallas kernels for 38%

profile of v5, /device:TPU:1, one launch (start us, length us, event | category | flops | bytes accessed | tf_op | source)
XLA Modules:
  0.0 53.6 jit_solution(13642609089651738063)
XLA Ops:
  0.0 5.5 %send.1 = (f32[64,8,128]{2,1,0:T(8,128)}, f32[16,24,128]{2,1,0:T(8,128)}, f32[4,24,128]{2,1,0:T(8,128)}, f32[4,24,128]{2,1,0:T(8,128)}) custom-call(s32[2,64]{1,0:T(2,128)} %bitcast.17, s32[1,64]{1,0:T(1,128)} %bitcast.18, f32[256,128]{1,0:T(8,128)} %bitcast.13, f32[3,16,128]{2,1,0:T(8,128)} %pos_ref.1, f32[3,16,128]{2,1,0:T(8,128)} %nrm_ref.1, ...), custom_call_target="tpu_custom_call" | custom-call | flops 3000000000 | bytes 3145728 | tf_op jit(solution)/shard_map/send/pallas_call | solution.py:369
  5.5 15.1 %all-to-all-start = ((f32[64,8,128]{2,1,0:T(8,128)}), f32[64,8,128]{2,1,0:T(8,128)S(1)}, u32[]{:S(2)}, u32[]{:S(2)}) async-start(f32[64,8,128]{2,1,0:T(8,128)} %get-tuple-element.21), calls=%async_computation | async-start | bytes 524288 | tf_op jit(solution)/shard_map/all_to_all | solution.py:465
  20.6 1.1 %collective-permute-start = (f32[4,24,128]{2,1,0:T(8,128)}, f32[4,24,128]{2,1,0:T(8,128)S(1)}, u32[]{:S(2)}, u32[]{:S(2)}) collective-permute-start(f32[4,24,128]{2,1,0:T(8,128)} %get-tuple-element.19), channel_id=1, source_target_pairs={{0,4},{4,8},{8,12},{12,16},{16,20},{20,24},{24,28},{28,32},{32,36}... | collective-permute-start | bytes 147464 | tf_op jit(solution)/shard_map/ppermute | solution.py:468
  21.7 6.2 %collective-permute-start.1 = (f32[4,24,128]{2,1,0:T(8,128)}, f32[4,24,128]{2,1,0:T(8,128)S(1)}, u32[]{:S(2)}, u32[]{:S(2)}) collective-permute-start(f32[4,24,128]{2,1,0:T(8,128)} %get-tuple-element.27), channel_id=1, source_target_pairs={{4,0},{8,4},{12,8},{16,12},{20,16},{24,20},{28,24},{32,28},{36,32}... | collective-permute-start | bytes 147464 | tf_op jit(solution)/shard_map/ppermute | solution.py:469
  27.9 0.0 copy-start.3
  27.9 0.9 %copy-done.3 = f32[16,24,128]{2,1,0:T(8,128)S(1)} copy-done((f32[16,24,128]{2,1,0:T(8,128)S(1)}, f32[16,24,128]{2,1,0:T(8,128)}, u32[]{:S(2)}) %copy-start.3) | copy-done | bytes 196632
  28.8 0.0 copy-start
  28.8 0.0 copy-start.2
  28.8 8.9 %near_inner.1 = (f32[16,8,128]{2,1,0:T(8,128)S(1)}, f32[8,128]{1,0:T(8,128)}) custom-call(f32[16,24,128]{2,1,0:T(8,128)S(1)} %copy-done.3), custom_call_target="tpu_custom_call" | custom-call | flops 10000000000 | bytes 1000000 | tf_op jit(solution)/shard_map/near_inner/pallas_call | solution.py:419
  37.7 0.0 copy-start.5
  37.7 0.6 %copy-done.5 = f32[16,8,128]{2,1,0:T(8,128)} copy-done((f32[16,8,128]{2,1,0:T(8,128)}, f32[16,8,128]{2,1,0:T(8,128)S(1)}, u32[]{:S(2)}) %copy-start.5) | copy-done | bytes 65560
  38.3 0.0 all-to-all-done.coef_ref
  38.3 0.0 copy-done
  38.3 0.0 copy-done.2
  38.3 0.0 copy-start.1
  38.4 0.0 copy-start.4
  38.4 0.0 copy-start.6
  38.4 2.4 %receive.1 = (f32[16,16,128]{2,1,0:T(8,128)S(1)}, f32[16,16,128]{2,1,0:T(8,128)S(1)}, f32[16,16,128]{2,1,0:T(8,128)S(1)}, f32[16,16,128]{2,1,0:T(8,128)S(1)}) custom-call(s32[2,64]{1,0:T(2,128)S(1)} %bitcast.14, s32[1]{0:T(128)} %bitcast.7.me_ref, f32[64,8,128]{2,1,0:T(8,128)S(1)} %all-to-all-done.coef_ref, f32[64,2,2,24,128]{4,3,2,1,0:T(8,128)S(1)} %bitcast.12), custom_call_target="tpu_custom_call" | custom-call | flops 3000000000 | bytes 3145728 | tf_op jit(solution)/shard_map/receive/pallas_call | solution.py:388
  40.8 1.8 %collective-permute-start.2 = (f32[16,16,128]{2,1,0:T(8,128)S(1)}, f32[16,16,128]{2,1,0:T(8,128)S(1)}, u32[]{:S(2)}, u32[]{:S(2)}) collective-permute-start(f32[16,16,128]{2,1,0:T(8,128)S(1)} %get-tuple-element.30), channel_id=1, source_target_pairs={{0,1},{1,2},{2,3},{3,0},{4,5},{5,6},{6,7},{7,4},{8,9},{9,10},{10,1... | collective-permute-start | bytes 393224 | tf_op jit(solution)/shard_map/ppermute | solution.py:481
  42.6 1.2 %collective-permute-start.3 = (f32[16,16,128]{2,1,0:T(8,128)S(1)}, f32[16,16,128]{2,1,0:T(8,128)S(1)}, u32[]{:S(2)}, u32[]{:S(2)}) collective-permute-start(f32[16,16,128]{2,1,0:T(8,128)S(1)} %get-tuple-element.31), channel_id=1, source_target_pairs={{0,2},{1,3},{2,0},{3,1},{4,6},{5,7},{6,4},{7,5},{8,10},{9,11},{10,... | collective-permute-start | bytes 393224 | tf_op jit(solution)/shard_map/ppermute | solution.py:481
  43.8 0.0 collective-permute-start.4
  43.8 0.0 collective-permute-done.refs_0_
  43.8 0.0 collective-permute-done.1.refs_2_
  43.8 0.0 copy-done.1
  43.8 0.0 copy-done.4
  43.8 0.0 copy-done.6
  43.8 9.0 %near_edge.1 = f32[2,8,16,128]{3,2,1,0:T(8,128)S(1)} custom-call(f32[4,24,128]{2,1,0:T(8,128)S(1)} %collective-permute-done.refs_0_, f32[16,24,128]{2,1,0:T(8,128)S(1)} %copy-done.4, f32[4,24,128]{2,1,0:T(8,128)S(1)} %collective-permute-done.1.refs_2_, f32[16,8,128]{2,1,0:T(8,128)S(1)} %copy-done.6, f32[2,8,16,128]{3,2,1,0:T(8,128)S(1)} %copy-done.1), custom_call_target="tpu_custom_call" | custom-call | flops 10000000000 | bytes 1000000 | tf_op jit(solution)/shard_map/near_edge/pallas_call | solution.py:437
  52.8 0.0 collective-permute-done.2
  52.8 0.0 collective-permute-done.3
  52.9 0.0 collective-permute-done.4
  52.9 0.7 %add.15 = f32[2,8,16,128]{3,2,1,0:T(8,128)} add(f32[2,8,16,128]{3,2,1,0:T(8,128)S(1)} %near_edge.1, f32[2,8,16,128]{3,2,1,0:T(8,128)S(1)} %bitcast.15) | non-fusion elementwise | flops 32768 | bytes 393216 | tf_op jit(solution)/shard_map/add | solution.py:485
  (1 shorter events, 0.0 us)
Async XLA Ops:
  5.5 32.9 %all-to-all-start = ((f32[64,8,128]{2,1,0:T(8,128)}), f32[64,8,128]{2,1,0:T(8,128)S(1)}, u32[]{:S(2)}, u32[]{:S(2)}) async-start(f32[64,8,128]{2,1,0:T(8,128)} %get-tuple-element.21), calls=%async_computation | async-start | bytes 524288 | tf_op jit(solution)/shard_map/all_to_all | solution.py:465
  20.6 23.2 %collective-permute-start = (f32[4,24,128]{2,1,0:T(8,128)}, f32[4,24,128]{2,1,0:T(8,128)S(1)}, u32[]{:S(2)}, u32[]{:S(2)}) collective-permute-start(f32[4,24,128]{2,1,0:T(8,128)} %get-tuple-element.19), channel_id=1, source_target_pairs={{0,4},{4,8},{8,12},{12,16},{16,20},{20,24},{24,28},{28,32},{32,36}... | collective-permute-start | bytes 147464 | tf_op jit(solution)/shard_map/ppermute | solution.py:468
  21.7 22.1 %collective-permute-start.1 = (f32[4,24,128]{2,1,0:T(8,128)}, f32[4,24,128]{2,1,0:T(8,128)S(1)}, u32[]{:S(2)}, u32[]{:S(2)}) collective-permute-start(f32[4,24,128]{2,1,0:T(8,128)} %get-tuple-element.27), channel_id=1, source_target_pairs={{4,0},{8,4},{12,8},{16,12},{20,16},{24,20},{28,24},{32,28},{36,32}... | collective-permute-start | bytes 147464 | tf_op jit(solution)/shard_map/ppermute | solution.py:469
  27.9 0.9 %copy-start.3 = (f32[16,24,128]{2,1,0:T(8,128)S(1)}, f32[16,24,128]{2,1,0:T(8,128)}, u32[]{:S(2)}) copy-start(f32[16,24,128]{2,1,0:T(8,128)} %get-tuple-element.26.refs_0_.refs_1_) | copy-start | bytes 589828
  28.8 9.5 %copy-start = (f32[1,1,64,2,2,24,128]{6,5,4,3,2,1,0:T(8,128)S(1)}, f32[1,1,64,2,2,24,128]{6,5,4,3,2,1,0:T(8,128)}, u32[]{:S(2)}) copy-start(f32[1,1,64,2,2,24,128]{6,5,4,3,2,1,0:T(8,128)} %param.17) | copy-start | bytes 9437188
  28.8 9.5 %copy-start.2 = (s32[1,1,64,2]{2,3,1,0:T(2,128)S(1)}, s32[1,1,64,2]{2,3,1,0:T(2,128)}, u32[]{:S(2)}) copy-start(s32[1,1,64,2]{2,3,1,0:T(2,128)} %param.15) | copy-start | bytes 1540
  37.7 0.6 %copy-start.5 = (f32[16,8,128]{2,1,0:T(8,128)}, f32[16,8,128]{2,1,0:T(8,128)S(1)}, u32[]{:S(2)}) copy-start(f32[16,8,128]{2,1,0:T(8,128)S(1)} %get-tuple-element.28.refs_3_) | copy-start | bytes 196612
  38.3 5.5 %copy-start.1 = (f32[2,8,16,128]{3,2,1,0:T(8,128)S(1)}, f32[2,8,16,128]{3,2,1,0:T(8,128)}, u32[]{:S(2)}) copy-start(f32[2,8,16,128]{3,2,1,0:T(8,128)} %refs_4_.1) | copy-start | bytes 393220
  38.4 5.5 %copy-start.4 = (f32[16,24,128]{2,1,0:T(8,128)S(1)}, f32[16,24,128]{2,1,0:T(8,128)}, u32[]{:S(2)}) copy-start(f32[16,24,128]{2,1,0:T(8,128)} %get-tuple-element.26.refs_0_.refs_1_) | copy-start | bytes 589828
  38.4 5.5 %copy-start.6 = (f32[16,8,128]{2,1,0:T(8,128)S(1)}, f32[16,8,128]{2,1,0:T(8,128)}, u32[]{:S(2)}) copy-start(f32[16,8,128]{2,1,0:T(8,128)} %copy-done.5) | copy-start | bytes 196612
  40.8 12.0 %collective-permute-start.2 = (f32[16,16,128]{2,1,0:T(8,128)S(1)}, f32[16,16,128]{2,1,0:T(8,128)S(1)}, u32[]{:S(2)}, u32[]{:S(2)}) collective-permute-start(f32[16,16,128]{2,1,0:T(8,128)S(1)} %get-tuple-element.30), channel_id=1, source_target_pairs={{0,1},{1,2},{2,3},{3,0},{4,5},{5,6},{6,7},{7,4},{8,9},{9,10},{10,1... | collective-permute-start | bytes 393224 | tf_op jit(solution)/shard_map/ppermute | solution.py:481
  42.6 10.2 %collective-permute-start.3 = (f32[16,16,128]{2,1,0:T(8,128)S(1)}, f32[16,16,128]{2,1,0:T(8,128)S(1)}, u32[]{:S(2)}, u32[]{:S(2)}) collective-permute-start(f32[16,16,128]{2,1,0:T(8,128)S(1)} %get-tuple-element.31), channel_id=1, source_target_pairs={{0,2},{1,3},{2,0},{3,1},{4,6},{5,7},{6,4},{7,5},{8,10},{9,11},{10,... | collective-permute-start | bytes 393224 | tf_op jit(solution)/shard_map/ppermute | solution.py:481
  43.8 9.1 %collective-permute-start.4 = (f32[16,16,128]{2,1,0:T(8,128)S(1)}, f32[16,16,128]{2,1,0:T(8,128)S(1)}, u32[]{:S(2)}, u32[]{:S(2)}) collective-permute-start(f32[16,16,128]{2,1,0:T(8,128)S(1)} %get-tuple-element.32), channel_id=1, source_target_pairs={{0,3},{1,0},{2,1},{3,2},{4,7},{5,4},{6,5},{7,6},{8,11},{9,8},{10,9... | collective-permute-start | bytes 393224 | tf_op jit(solution)/shard_map/ppermute | solution.py:481

commit v6 on v5

--- a/solution.py
+++ b/solution.py
@@ -81,34 +81,35 @@
 
     half = field_ref.shape[0] // 2
     for row in range(span_rows):
-        pair = jnp.concatenate(
-            [field_ref[pl.ds(c * half + row, 8, stride=span_rows), :] for c in range(2)], 1
+        re, im = (field_ref[pl.ds(c * half + row, 8, stride=span_rows), :] for c in range(2))
+        high, low = split_two(
+            jnp.concatenate(
+                [jnp.concatenate([re, -im], 1), jnp.concatenate([im, re], 1)], 0
+            )
         )
-        high, low = split_two(pair)
-        table_ref[row] = jnp.concatenate([high.astype(f32), low.astype(f32)], 0).astype(bf16)
-
-    lane = lax.broadcasted_iota(jnp.int32, (8, 2 * rank * cap), 1)
+        table_ref[row] = jnp.concatenate([high, low], 0)
 
     def one_chunk(index, carry):
         fetch(index).wait()
         for i in range(peers):
             peer = index * peers + i
-            wide = []
+            right = jnp.concatenate(
+                [jnp.concatenate([v_ref[peer, k, 0], v_ref[peer, k, 1]], 1) for k in range(cap)], 0
+            )
+            high, low = split_two(right)
+            rows = [table_ref[chosen_ref[k, peer]] for k in range(cap)]
+            first = dot_nt(jnp.concatenate(rows, 0), high)
+            second = dot_nt(jnp.concatenate([r[:16] for r in rows], 0), low)
+            tile = []
             for k in range(cap):
-                re, im = v_ref[peer, k, 0], v_ref[peer, k, 1]
-                wide += [jnp.concatenate([re, -im], 1), jnp.concatenate([im, re], 1)]
-            high, low = split_two(jnp.concatenate(wide, 0))
-            left = jnp.concatenate([table_ref[chosen_ref[k, peer]] for k in range(cap)], 0)
-            first = dot_nt(left, high)
-            second = dot_nt(left, low)
-            total = jnp.zeros((8, 2 * rank * cap), f32)
-            for k in range(cap):
-                at = 16 * k
-                part = first[at : at + 8] + (first[at + 8 : at + 16] + second[at : at + 8])
-                here = (lane // (2 * rank) == k) & (k < count_ref[0, peer])
-                total = jnp.where(here, part, total)
-            out_ref[peer, :, : 2 * rank * cap] = total
-            out_ref[peer, :, 2 * rank * cap :] = jnp.zeros((8, width - 2 * rank * cap), f32)
+                both = first[32 * k : 32 * k + 16] + (
+                    first[32 * k + 16 : 32 * k + 32] + second[16 * k : 16 * k + 16]
+                )
+                both = jnp.where(k < count_ref[0, peer], both, 0.0)
+                cols = slice(k * rank, (k + 1) * rank)
+                tile += [both[:8, cols], both[8:, cols]]
+            tile.append(jnp.zeros((8, width - 2 * rank * cap), f32))
+            out_ref[peer] = jnp.concatenate(tile, 1)
         return carry
 
     lax.fori_loop(0, chunks, one_chunk, 0)
@@ -373,7 +374,7 @@
         out_shape=[jax.ShapeDtypeStruct(s, f32) for s in shapes],
         scratch_shapes=[
             pltpu.VMEM(v.shape, f32),
-            pltpu.VMEM((span_rows, 16, 2 * width), bf16),
+            pltpu.VMEM((span_rows, 32, 2 * width), bf16),
             pltpu.SemaphoreType.DMA((chunks,)),
         ],
         cost_estimate=cost(3 * 10**9, 4 * v.size),

time: 53.8 us -> 53.1 us (0.987)
  Pallas kernels: 25.8 us -> 25.1 us
    pallas_call x1, Pallas kernels: 5.46 us -> 4.79 us  [run_send(): pl.pallas_call(send_kernel, in_specs=smem(2) + vmem(4) + [pl.BlockSpec(me...]
where the time goes in v6:
time: 53.1 us; the launch traced here: 52.9 us
  starting transfers between devices  25.3 us (48%)
  Pallas kernels  25.1 us (47%)
  local copies, waits for them, and re-layouts  1.58 us (3%)
  other arithmetic  0.71 us (1%)
    all_to_all x1, starting transfers between devices, shards(): lax.all_to_all(outgoing, 'azim', split_axis=0, concat_axis=0, tiled=True)  15.1 us
    pallas_call x1, Pallas kernels, run_near_edge(): pl.pallas_call(functools.partial(near_kernel, 0, halo // 2, blocks // 2 -...  9 us
    pallas_call x1, Pallas kernels, run_near_inner(): pl.pallas_call(functools.partial(near_kernel, halo // 2, count // 2, 0, F...  8.92 us
    ppermute x1, starting transfers between devices, shards(): right = lax.ppermute(low, 'azim', backward)  6.18 us
    pallas_call x1, Pallas kernels, run_send(): pl.pallas_call(send_kernel, in_specs=smem(2) + vmem(4) + [pl.BlockSpec(me...  4.79 us
    ppermute x3, starting transfers between devices, shards(): others.append(lax.ppermute(pieces[k], 'span', ring))  2.93 us
    pallas_call x1, Pallas kernels, run_receive(): pl.pallas_call(receive_kernel, in_specs=smem(2) + vmem(2), out_specs=vmem...  2.44 us
    unnamed x14, local copies, waits for them, and re-layouts  1.58 us
  transfers between devices with their start and end apart: 6, of which 0 were waited for; matrix products, arithmetic and copies ran while one was open for 0% of the time, Pallas kernels for 38%

profile of v6, /device:TPU:1, one launch (start us, length us, event | category | flops | bytes accessed | tf_op | source)
XLA Modules:
  0.0 52.9 jit_solution(11375647147772452449)
XLA Ops:
  0.0 4.8 %send.1 = (f32[64,8,128]{2,1,0:T(8,128)}, f32[16,24,128]{2,1,0:T(8,128)}, f32[4,24,128]{2,1,0:T(8,128)}, f32[4,24,128]{2,1,0:T(8,128)}) custom-call(s32[2,64]{1,0:T(2,128)} %bitcast.17, s32[1,64]{1,0:T(1,128)} %bitcast.18, f32[256,128]{1,0:T(8,128)} %bitcast.13, f32[3,16,128]{2,1,0:T(8,128)} %pos_ref.1, f32[3,16,128]{2,1,0:T(8,128)} %nrm_ref.1, ...), custom_call_target="tpu_custom_call" | custom-call | flops 3000000000 | bytes 3145728 | tf_op jit(solution)/shard_map/send/pallas_call | solution.py:370
  4.8 15.1 %all-to-all-start = ((f32[64,8,128]{2,1,0:T(8,128)}), f32[64,8,128]{2,1,0:T(8,128)S(1)}, u32[]{:S(2)}, u32[]{:S(2)}) async-start(f32[64,8,128]{2,1,0:T(8,128)} %get-tuple-element.21), calls=%async_computation | async-start | bytes 524288 | tf_op jit(solution)/shard_map/all_to_all | solution.py:466
  19.9 1.1 %collective-permute-start = (f32[4,24,128]{2,1,0:T(8,128)}, f32[4,24,128]{2,1,0:T(8,128)S(1)}, u32[]{:S(2)}, u32[]{:S(2)}) collective-permute-start(f32[4,24,128]{2,1,0:T(8,128)} %get-tuple-element.19), channel_id=1, source_target_pairs={{0,4},{4,8},{8,12},{12,16},{16,20},{20,24},{24,28},{28,32},{32,36}... | collective-permute-start | bytes 147464 | tf_op jit(solution)/shard_map/ppermute | solution.py:469
  21.0 6.2 %collective-permute-start.1 = (f32[4,24,128]{2,1,0:T(8,128)}, f32[4,24,128]{2,1,0:T(8,128)S(1)}, u32[]{:S(2)}, u32[]{:S(2)}) collective-permute-start(f32[4,24,128]{2,1,0:T(8,128)} %get-tuple-element.27), channel_id=1, source_target_pairs={{4,0},{8,4},{12,8},{16,12},{20,16},{24,20},{28,24},{32,28},{36,32}... | collective-permute-start | bytes 147464 | tf_op jit(solution)/shard_map/ppermute | solution.py:470
  27.2 0.0 copy-start.3
  27.2 0.9 %copy-done.3 = f32[16,24,128]{2,1,0:T(8,128)S(1)} copy-done((f32[16,24,128]{2,1,0:T(8,128)S(1)}, f32[16,24,128]{2,1,0:T(8,128)}, u32[]{:S(2)}) %copy-start.3) | copy-done | bytes 196632
  28.1 0.0 copy-start
  28.1 0.0 copy-start.2
  28.1 8.9 %near_inner.1 = (f32[16,8,128]{2,1,0:T(8,128)S(1)}, f32[8,128]{1,0:T(8,128)}) custom-call(f32[16,24,128]{2,1,0:T(8,128)S(1)} %copy-done.3), custom_call_target="tpu_custom_call" | custom-call | flops 10000000000 | bytes 1000000 | tf_op jit(solution)/shard_map/near_inner/pallas_call | solution.py:420
  37.1 0.0 copy-start.5
  37.1 0.6 %copy-done.5 = f32[16,8,128]{2,1,0:T(8,128)} copy-done((f32[16,8,128]{2,1,0:T(8,128)}, f32[16,8,128]{2,1,0:T(8,128)S(1)}, u32[]{:S(2)}) %copy-start.5) | copy-done | bytes 65560
  37.7 0.0 all-to-all-done.coef_ref
  37.7 0.0 copy-done
  37.7 0.0 copy-done.2
  37.7 0.0 copy-start.1
  37.7 0.0 copy-start.4
  37.7 0.0 copy-start.6
  37.7 2.4 %receive.1 = (f32[16,16,128]{2,1,0:T(8,128)S(1)}, f32[16,16,128]{2,1,0:T(8,128)S(1)}, f32[16,16,128]{2,1,0:T(8,128)S(1)}, f32[16,16,128]{2,1,0:T(8,128)S(1)}) custom-call(s32[2,64]{1,0:T(2,128)S(1)} %bitcast.14, s32[1]{0:T(128)} %bitcast.7.me_ref, f32[64,8,128]{2,1,0:T(8,128)S(1)} %all-to-all-done.coef_ref, f32[64,2,2,24,128]{4,3,2,1,0:T(8,128)S(1)} %bitcast.12), custom_call_target="tpu_custom_call" | custom-call | flops 3000000000 | bytes 3145728 | tf_op jit(solution)/shard_map/receive/pallas_call | solution.py:389
  40.2 1.8 %collective-permute-start.2 = (f32[16,16,128]{2,1,0:T(8,128)S(1)}, f32[16,16,128]{2,1,0:T(8,128)S(1)}, u32[]{:S(2)}, u32[]{:S(2)}) collective-permute-start(f32[16,16,128]{2,1,0:T(8,128)S(1)} %get-tuple-element.30), channel_id=1, source_target_pairs={{0,1},{1,2},{2,3},{3,0},{4,5},{5,6},{6,7},{7,4},{8,9},{9,10},{10,1... | collective-permute-start | bytes 393224 | tf_op jit(solution)/shard_map/ppermute | solution.py:482
  42.0 1.1 %collective-permute-start.3 = (f32[16,16,128]{2,1,0:T(8,128)S(1)}, f32[16,16,128]{2,1,0:T(8,128)S(1)}, u32[]{:S(2)}, u32[]{:S(2)}) collective-permute-start(f32[16,16,128]{2,1,0:T(8,128)S(1)} %get-tuple-element.31), channel_id=1, source_target_pairs={{0,2},{1,3},{2,0},{3,1},{4,6},{5,7},{6,4},{7,5},{8,10},{9,11},{10,... | collective-permute-start | bytes 393224 | tf_op jit(solution)/shard_map/ppermute | solution.py:482
  43.1 0.0 collective-permute-start.4
  43.1 0.0 collective-permute-done.refs_0_
  43.1 0.0 collective-permute-done.1.refs_2_
  43.1 0.0 copy-done.1
  43.1 0.0 copy-done.4
  43.1 0.0 copy-done.6
  43.1 9.0 %near_edge.1 = f32[2,8,16,128]{3,2,1,0:T(8,128)S(1)} custom-call(f32[4,24,128]{2,1,0:T(8,128)S(1)} %collective-permute-done.refs_0_, f32[16,24,128]{2,1,0:T(8,128)S(1)} %copy-done.4, f32[4,24,128]{2,1,0:T(8,128)S(1)} %collective-permute-done.1.refs_2_, f32[16,8,128]{2,1,0:T(8,128)S(1)} %copy-done.6, f32[2,8,16,128]{3,2,1,0:T(8,128)S(1)} %copy-done.1), custom_call_target="tpu_custom_call" | custom-call | flops 10000000000 | bytes 1000000 | tf_op jit(solution)/shard_map/near_edge/pallas_call | solution.py:438
  52.1 0.0 collective-permute-done.2
  52.2 0.0 collective-permute-done.3
  52.2 0.0 collective-permute-done.4
  52.2 0.7 %add.15 = f32[2,8,16,128]{3,2,1,0:T(8,128)} add(f32[2,8,16,128]{3,2,1,0:T(8,128)S(1)} %near_edge.1, f32[2,8,16,128]{3,2,1,0:T(8,128)S(1)} %bitcast.15) | non-fusion elementwise | flops 32768 | bytes 393216 | tf_op jit(solution)/shard_map/add | solution.py:486
  (1 shorter events, 0.0 us)
Async XLA Ops:
  4.8 32.9 %all-to-all-start = ((f32[64,8,128]{2,1,0:T(8,128)}), f32[64,8,128]{2,1,0:T(8,128)S(1)}, u32[]{:S(2)}, u32[]{:S(2)}) async-start(f32[64,8,128]{2,1,0:T(8,128)} %get-tuple-element.21), calls=%async_computation | async-start | bytes 524288 | tf_op jit(solution)/shard_map/all_to_all | solution.py:466
  19.9 23.2 %collective-permute-start = (f32[4,24,128]{2,1,0:T(8,128)}, f32[4,24,128]{2,1,0:T(8,128)S(1)}, u32[]{:S(2)}, u32[]{:S(2)}) collective-permute-start(f32[4,24,128]{2,1,0:T(8,128)} %get-tuple-element.19), channel_id=1, source_target_pairs={{0,4},{4,8},{8,12},{12,16},{16,20},{20,24},{24,28},{28,32},{32,36}... | collective-permute-start | bytes 147464 | tf_op jit(solution)/shard_map/ppermute | solution.py:469
  21.0 22.1 %collective-permute-start.1 = (f32[4,24,128]{2,1,0:T(8,128)}, f32[4,24,128]{2,1,0:T(8,128)S(1)}, u32[]{:S(2)}, u32[]{:S(2)}) collective-permute-start(f32[4,24,128]{2,1,0:T(8,128)} %get-tuple-element.27), channel_id=1, source_target_pairs={{4,0},{8,4},{12,8},{16,12},{20,16},{24,20},{28,24},{32,28},{36,32}... | collective-permute-start | bytes 147464 | tf_op jit(solution)/shard_map/ppermute | solution.py:470
  27.2 0.9 %copy-start.3 = (f32[16,24,128]{2,1,0:T(8,128)S(1)}, f32[16,24,128]{2,1,0:T(8,128)}, u32[]{:S(2)}) copy-start(f32[16,24,128]{2,1,0:T(8,128)} %get-tuple-element.26.refs_0_.refs_1_) | copy-start | bytes 589828
  28.1 9.6 %copy-start = (f32[1,1,64,2,2,24,128]{6,5,4,3,2,1,0:T(8,128)S(1)}, f32[1,1,64,2,2,24,128]{6,5,4,3,2,1,0:T(8,128)}, u32[]{:S(2)}) copy-start(f32[1,1,64,2,2,24,128]{6,5,4,3,2,1,0:T(8,128)} %param.17) | copy-start | bytes 9437188
  28.1 9.6 %copy-start.2 = (s32[1,1,64,2]{2,3,1,0:T(2,128)S(1)}, s32[1,1,64,2]{2,3,1,0:T(2,128)}, u32[]{:S(2)}) copy-start(s32[1,1,64,2]{2,3,1,0:T(2,128)} %param.15) | copy-start | bytes 1540
  37.1 0.6 %copy-start.5 = (f32[16,8,128]{2,1,0:T(8,128)}, f32[16,8,128]{2,1,0:T(8,128)S(1)}, u32[]{:S(2)}) copy-start(f32[16,8,128]{2,1,0:T(8,128)S(1)} %get-tuple-element.28.refs_3_) | copy-start | bytes 196612
  37.7 5.4 %copy-start.1 = (f32[2,8,16,128]{3,2,1,0:T(8,128)S(1)}, f32[2,8,16,128]{3,2,1,0:T(8,128)}, u32[]{:S(2)}) copy-start(f32[2,8,16,128]{3,2,1,0:T(8,128)} %refs_4_.1) | copy-start | bytes 393220
  37.7 5.4 %copy-start.4 = (f32[16,24,128]{2,1,0:T(8,128)S(1)}, f32[16,24,128]{2,1,0:T(8,128)}, u32[]{:S(2)}) copy-start(f32[16,24,128]{2,1,0:T(8,128)} %get-tuple-element.26.refs_0_.refs_1_) | copy-start | bytes 589828
  37.7 5.4 %copy-start.6 = (f32[16,8,128]{2,1,0:T(8,128)S(1)}, f32[16,8,128]{2,1,0:T(8,128)}, u32[]{:S(2)}) copy-start(f32[16,8,128]{2,1,0:T(8,128)} %copy-done.5) | copy-start | bytes 196612
  40.2 12.0 %collective-permute-start.2 = (f32[16,16,128]{2,1,0:T(8,128)S(1)}, f32[16,16,128]{2,1,0:T(8,128)S(1)}, u32[]{:S(2)}, u32[]{:S(2)}) collective-permute-start(f32[16,16,128]{2,1,0:T(8,128)S(1)} %get-tuple-element.30), channel_id=1, source_target_pairs={{0,1},{1,2},{2,3},{3,0},{4,5},{5,6},{6,7},{7,4},{8,9},{9,10},{10,1... | collective-permute-start | bytes 393224 | tf_op jit(solution)/shard_map/ppermute | solution.py:482
  42.0 10.2 %collective-permute-start.3 = (f32[16,16,128]{2,1,0:T(8,128)S(1)}, f32[16,16,128]{2,1,0:T(8,128)S(1)}, u32[]{:S(2)}, u32[]{:S(2)}) collective-permute-start(f32[16,16,128]{2,1,0:T(8,128)S(1)} %get-tuple-element.31), channel_id=1, source_target_pairs={{0,2},{1,3},{2,0},{3,1},{4,6},{5,7},{6,4},{7,5},{8,10},{9,11},{10,... | collective-permute-start | bytes 393224 | tf_op jit(solution)/shard_map/ppermute | solution.py:482
  43.1 9.1 %collective-permute-start.4 = (f32[16,16,128]{2,1,0:T(8,128)S(1)}, f32[16,16,128]{2,1,0:T(8,128)S(1)}, u32[]{:S(2)}, u32[]{:S(2)}) collective-permute-start(f32[16,16,128]{2,1,0:T(8,128)S(1)} %get-tuple-element.32), channel_id=1, source_target_pairs={{0,3},{1,0},{2,1},{3,2},{4,7},{5,4},{6,5},{7,6},{8,11},{9,8},{10,9... | collective-permute-start | bytes 393224 | tf_op jit(solution)/shard_map/ppermute | solution.py:482

commit v7 on v6

--- a/solution.py
+++ b/solution.py
@@ -329,7 +329,7 @@
         return carry
 
     part_ref[...] = jnp.zeros_like(part_ref)
-    lax.fori_loop(0, pairs, prepare, 0)
+    lax.fori_loop(0, pairs, prepare, 0, unroll=True)
     lax.fori_loop(0, pairs, one_pair, 0)
     finish(pairs - 1, slot_of(pairs - 1))
     if edge:

time: 53.1 us -> 52.1 us (0.981)
  Pallas kernels: 25.1 us -> 24.2 us
  transfers between devices with their start and end apart: 6 -> 6, of which waited for: 0 -> 0; matrix products, arithmetic and copies ran while one was open for 0% -> 0% of each run, Pallas kernels for 38% -> 37%
where the time goes in v7:
time: 52.1 us; the launch traced here: 52 us
  starting transfers between devices  25.3 us (49%)
  Pallas kernels  24.2 us (46%)
  local copies, waits for them, and re-layouts  1.58 us (3%)
  other arithmetic  0.71 us (1%)
    all_to_all x1, starting transfers between devices, shards(): lax.all_to_all(outgoing, 'azim', split_axis=0, concat_axis=0, tiled=True)  15.1 us
    pallas_call x1, Pallas kernels, run_near_edge(): pl.pallas_call(functools.partial(near_kernel, 0, halo // 2, blocks // 2 -...  8.52 us
    pallas_call x1, Pallas kernels, run_near_inner(): pl.pallas_call(functools.partial(near_kernel, halo // 2, count // 2, 0, F...  8.45 us
    ppermute x1, starting transfers between devices, shards(): right = lax.ppermute(low, 'azim', backward)  6.18 us
    pallas_call x1, Pallas kernels, run_send(): pl.pallas_call(send_kernel, in_specs=smem(2) + vmem(4) + [pl.BlockSpec(me...  4.79 us
    ppermute x3, starting transfers between devices, shards(): others.append(lax.ppermute(pieces[k], 'span', ring))  2.93 us
    pallas_call x1, Pallas kernels, run_receive(): pl.pallas_call(receive_kernel, in_specs=smem(2) + vmem(2), out_specs=vmem...  2.44 us
    unnamed x14, local copies, waits for them, and re-layouts  1.58 us
  transfers between devices with their start and end apart: 6, of which 0 were waited for; matrix products, arithmetic and copies ran while one was open for 0% of the time, Pallas kernels for 37%

profile of v7, /device:TPU:1, one launch (start us, length us, event | category | flops | bytes accessed | tf_op | source)
XLA Modules:
  0.0 52.0 jit_solution(16386407495960579300)
XLA Ops:
  0.0 4.8 %send.1 = (f32[64,8,128]{2,1,0:T(8,128)}, f32[16,24,128]{2,1,0:T(8,128)}, f32[4,24,128]{2,1,0:T(8,128)}, f32[4,24,128]{2,1,0:T(8,128)}) custom-call(s32[2,64]{1,0:T(2,128)} %bitcast.17, s32[1,64]{1,0:T(1,128)} %bitcast.18, f32[256,128]{1,0:T(8,128)} %bitcast.13, f32[3,16,128]{2,1,0:T(8,128)} %pos_ref.1, f32[3,16,128]{2,1,0:T(8,128)} %nrm_ref.1, ...), custom_call_target="tpu_custom_call" | custom-call | flops 3000000000 | bytes 3145728 | tf_op jit(solution)/shard_map/send/pallas_call | solution.py:370
  4.8 15.1 %all-to-all-start = ((f32[64,8,128]{2,1,0:T(8,128)}), f32[64,8,128]{2,1,0:T(8,128)S(1)}, u32[]{:S(2)}, u32[]{:S(2)}) async-start(f32[64,8,128]{2,1,0:T(8,128)} %get-tuple-element.21), calls=%async_computation | async-start | bytes 524288 | tf_op jit(solution)/shard_map/all_to_all | solution.py:466
  19.9 1.1 %collective-permute-start = (f32[4,24,128]{2,1,0:T(8,128)}, f32[4,24,128]{2,1,0:T(8,128)S(1)}, u32[]{:S(2)}, u32[]{:S(2)}) collective-permute-start(f32[4,24,128]{2,1,0:T(8,128)} %get-tuple-element.19), channel_id=1, source_target_pairs={{0,4},{4,8},{8,12},{12,16},{16,20},{20,24},{24,28},{28,32},{32,36}... | collective-permute-start | bytes 147464 | tf_op jit(solution)/shard_map/ppermute | solution.py:469
  21.0 6.2 %collective-permute-start.1 = (f32[4,24,128]{2,1,0:T(8,128)}, f32[4,24,128]{2,1,0:T(8,128)S(1)}, u32[]{:S(2)}, u32[]{:S(2)}) collective-permute-start(f32[4,24,128]{2,1,0:T(8,128)} %get-tuple-element.27), channel_id=1, source_target_pairs={{4,0},{8,4},{12,8},{16,12},{20,16},{24,20},{28,24},{32,28},{36,32}... | collective-permute-start | bytes 147464 | tf_op jit(solution)/shard_map/ppermute | solution.py:470
  27.2 0.0 copy-start.3
  27.2 0.9 %copy-done.3 = f32[16,24,128]{2,1,0:T(8,128)S(1)} copy-done((f32[16,24,128]{2,1,0:T(8,128)S(1)}, f32[16,24,128]{2,1,0:T(8,128)}, u32[]{:S(2)}) %copy-start.3) | copy-done | bytes 196632
  28.1 0.0 copy-start
  28.1 0.0 copy-start.2
  28.1 8.4 %near_inner.1 = (f32[16,8,128]{2,1,0:T(8,128)S(1)}, f32[8,128]{1,0:T(8,128)}) custom-call(f32[16,24,128]{2,1,0:T(8,128)S(1)} %copy-done.3), custom_call_target="tpu_custom_call" | custom-call | flops 10000000000 | bytes 1000000 | tf_op jit(solution)/shard_map/near_inner/pallas_call | solution.py:420
  36.6 0.0 copy-start.5
  36.6 0.6 %copy-done.5 = f32[16,8,128]{2,1,0:T(8,128)} copy-done((f32[16,8,128]{2,1,0:T(8,128)}, f32[16,8,128]{2,1,0:T(8,128)S(1)}, u32[]{:S(2)}) %copy-start.5) | copy-done | bytes 65560
  37.2 0.0 all-to-all-done.coef_ref
  37.2 0.0 copy-done
  37.2 0.0 copy-done.2
  37.2 0.0 copy-start.1
  37.2 0.0 copy-start.4
  37.2 0.0 copy-start.6
  37.3 2.4 %receive.1 = (f32[16,16,128]{2,1,0:T(8,128)S(1)}, f32[16,16,128]{2,1,0:T(8,128)S(1)}, f32[16,16,128]{2,1,0:T(8,128)S(1)}, f32[16,16,128]{2,1,0:T(8,128)S(1)}) custom-call(s32[2,64]{1,0:T(2,128)S(1)} %bitcast.14, s32[1]{0:T(128)} %bitcast.7.me_ref, f32[64,8,128]{2,1,0:T(8,128)S(1)} %all-to-all-done.coef_ref, f32[64,2,2,24,128]{4,3,2,1,0:T(8,128)S(1)} %bitcast.12), custom_call_target="tpu_custom_call" | custom-call | flops 3000000000 | bytes 3145728 | tf_op jit(solution)/shard_map/receive/pallas_call | solution.py:389
  39.7 1.8 %collective-permute-start.2 = (f32[16,16,128]{2,1,0:T(8,128)S(1)}, f32[16,16,128]{2,1,0:T(8,128)S(1)}, u32[]{:S(2)}, u32[]{:S(2)}) collective-permute-start(f32[16,16,128]{2,1,0:T(8,128)S(1)} %get-tuple-element.30), channel_id=1, source_target_pairs={{0,1},{1,2},{2,3},{3,0},{4,5},{5,6},{6,7},{7,4},{8,9},{9,10},{10,1... | collective-permute-start | bytes 393224 | tf_op jit(solution)/shard_map/ppermute | solution.py:482
  41.5 1.1 %collective-permute-start.3 = (f32[16,16,128]{2,1,0:T(8,128)S(1)}, f32[16,16,128]{2,1,0:T(8,128)S(1)}, u32[]{:S(2)}, u32[]{:S(2)}) collective-permute-start(f32[16,16,128]{2,1,0:T(8,128)S(1)} %get-tuple-element.31), channel_id=1, source_target_pairs={{0,2},{1,3},{2,0},{3,1},{4,6},{5,7},{6,4},{7,5},{8,10},{9,11},{10,... | collective-permute-start | bytes 393224 | tf_op jit(solution)/shard_map/ppermute | solution.py:482
  42.6 0.0 collective-permute-start.4
  42.6 0.0 collective-permute-done.refs_0_
  42.6 0.0 collective-permute-done.1.refs_2_
  42.7 0.0 copy-done.1
  42.7 0.0 copy-done.4
  42.7 0.0 copy-done.6
  42.7 8.5 %near_edge.1 = f32[2,8,16,128]{3,2,1,0:T(8,128)S(1)} custom-call(f32[4,24,128]{2,1,0:T(8,128)S(1)} %collective-permute-done.refs_0_, f32[16,24,128]{2,1,0:T(8,128)S(1)} %copy-done.4, f32[4,24,128]{2,1,0:T(8,128)S(1)} %collective-permute-done.1.refs_2_, f32[16,8,128]{2,1,0:T(8,128)S(1)} %copy-done.6, f32[2,8,16,128]{3,2,1,0:T(8,128)S(1)} %copy-done.1), custom_call_target="tpu_custom_call" | custom-call | flops 10000000000 | bytes 1000000 | tf_op jit(solution)/shard_map/near_edge/pallas_call | solution.py:438
  51.2 0.0 collective-permute-done.2
  51.2 0.0 collective-permute-done.3
  51.2 0.0 collective-permute-done.4
  51.3 0.7 %add.15 = f32[2,8,16,128]{3,2,1,0:T(8,128)} add(f32[2,8,16,128]{3,2,1,0:T(8,128)S(1)} %near_edge.1, f32[2,8,16,128]{3,2,1,0:T(8,128)S(1)} %bitcast.15) | non-fusion elementwise | flops 32768 | bytes 393216 | tf_op jit(solution)/shard_map/add | solution.py:486
  (1 shorter events, 0.0 us)
Async XLA Ops:
  4.8 32.4 %all-to-all-start = ((f32[64,8,128]{2,1,0:T(8,128)}), f32[64,8,128]{2,1,0:T(8,128)S(1)}, u32[]{:S(2)}, u32[]{:S(2)}) async-start(f32[64,8,128]{2,1,0:T(8,128)} %get-tuple-element.21), calls=%async_computation | async-start | bytes 524288 | tf_op jit(solution)/shard_map/all_to_all | solution.py:466
  19.9 22.7 %collective-permute-start = (f32[4,24,128]{2,1,0:T(8,128)}, f32[4,24,128]{2,1,0:T(8,128)S(1)}, u32[]{:S(2)}, u32[]{:S(2)}) collective-permute-start(f32[4,24,128]{2,1,0:T(8,128)} %get-tuple-element.19), channel_id=1, source_target_pairs={{0,4},{4,8},{8,12},{12,16},{16,20},{20,24},{24,28},{28,32},{32,36}... | collective-permute-start | bytes 147464 | tf_op jit(solution)/shard_map/ppermute | solution.py:469
  21.0 21.6 %collective-permute-start.1 = (f32[4,24,128]{2,1,0:T(8,128)}, f32[4,24,128]{2,1,0:T(8,128)S(1)}, u32[]{:S(2)}, u32[]{:S(2)}) collective-permute-start(f32[4,24,128]{2,1,0:T(8,128)} %get-tuple-element.27), channel_id=1, source_target_pairs={{4,0},{8,4},{12,8},{16,12},{20,16},{24,20},{28,24},{32,28},{36,32}... | collective-permute-start | bytes 147464 | tf_op jit(solution)/shard_map/ppermute | solution.py:470
  27.2 0.9 %copy-start.3 = (f32[16,24,128]{2,1,0:T(8,128)S(1)}, f32[16,24,128]{2,1,0:T(8,128)}, u32[]{:S(2)}) copy-start(f32[16,24,128]{2,1,0:T(8,128)} %get-tuple-element.26.refs_0_.refs_1_) | copy-start | bytes 589828
  28.1 9.1 %copy-start = (f32[1,1,64,2,2,24,128]{6,5,4,3,2,1,0:T(8,128)S(1)}, f32[1,1,64,2,2,24,128]{6,5,4,3,2,1,0:T(8,128)}, u32[]{:S(2)}) copy-start(f32[1,1,64,2,2,24,128]{6,5,4,3,2,1,0:T(8,128)} %param.17) | copy-start | bytes 9437188
  28.1 9.1 %copy-start.2 = (s32[1,1,64,2]{2,3,1,0:T(2,128)S(1)}, s32[1,1,64,2]{2,3,1,0:T(2,128)}, u32[]{:S(2)}) copy-start(s32[1,1,64,2]{2,3,1,0:T(2,128)} %param.15) | copy-start | bytes 1540
  36.6 0.6 %copy-start.5 = (f32[16,8,128]{2,1,0:T(8,128)}, f32[16,8,128]{2,1,0:T(8,128)S(1)}, u32[]{:S(2)}) copy-start(f32[16,8,128]{2,1,0:T(8,128)S(1)} %get-tuple-element.28.refs_3_) | copy-start | bytes 196612
  37.2 5.4 %copy-start.1 = (f32[2,8,16,128]{3,2,1,0:T(8,128)S(1)}, f32[2,8,16,128]{3,2,1,0:T(8,128)}, u32[]{:S(2)}) copy-start(f32[2,8,16,128]{3,2,1,0:T(8,128)} %refs_4_.1) | copy-start | bytes 393220
  37.2 5.4 %copy-start.4 = (f32[16,24,128]{2,1,0:T(8,128)S(1)}, f32[16,24,128]{2,1,0:T(8,128)}, u32[]{:S(2)}) copy-start(f32[16,24,128]{2,1,0:T(8,128)} %get-tuple-element.26.refs_0_.refs_1_) | copy-start | bytes 589828
  37.2 5.4 %copy-start.6 = (f32[16,8,128]{2,1,0:T(8,128)S(1)}, f32[16,8,128]{2,1,0:T(8,128)}, u32[]{:S(2)}) copy-start(f32[16,8,128]{2,1,0:T(8,128)} %copy-done.5) | copy-start | bytes 196612
  39.7 11.5 %collective-permute-start.2 = (f32[16,16,128]{2,1,0:T(8,128)S(1)}, f32[16,16,128]{2,1,0:T(8,128)S(1)}, u32[]{:S(2)}, u32[]{:S(2)}) collective-permute-start(f32[16,16,128]{2,1,0:T(8,128)S(1)} %get-tuple-element.30), channel_id=1, source_target_pairs={{0,1},{1,2},{2,3},{3,0},{4,5},{5,6},{6,7},{7,4},{8,9},{9,10},{10,1... | collective-permute-start | bytes 393224 | tf_op jit(solution)/shard_map/ppermute | solution.py:482
  41.5 9.7 %collective-permute-start.3 = (f32[16,16,128]{2,1,0:T(8,128)S(1)}, f32[16,16,128]{2,1,0:T(8,128)S(1)}, u32[]{:S(2)}, u32[]{:S(2)}) collective-permute-start(f32[16,16,128]{2,1,0:T(8,128)S(1)} %get-tuple-element.31), channel_id=1, source_target_pairs={{0,2},{1,3},{2,0},{3,1},{4,6},{5,7},{6,4},{7,5},{8,10},{9,11},{10,... | collective-permute-start | bytes 393224 | tf_op jit(solution)/shard_map/ppermute | solution.py:482
  42.6 8.6 %collective-permute-start.4 = (f32[16,16,128]{2,1,0:T(8,128)S(1)}, f32[16,16,128]{2,1,0:T(8,128)S(1)}, u32[]{:S(2)}, u32[]{:S(2)}) collective-permute-start(f32[16,16,128]{2,1,0:T(8,128)S(1)} %get-tuple-element.32), channel_id=1, source_target_pairs={{0,3},{1,0},{2,1},{3,2},{4,7},{5,4},{6,5},{7,6},{8,11},{9,8},{10,9... | collective-permute-start | bytes 393224 | tf_op jit(solution)/shard_map/ppermute | solution.py:482

commit v8 on v7

--- a/solution.py
+++ b/solution.py
@@ -123,7 +123,7 @@
     used = 2 * rank * cap
     row_bits = span_rows.bit_length() - 1
     piece = accs[0].shape[0] // span
-    peers = 16
+    peers = 32
     for acc_ref in accs:
         acc_ref[...] = jnp.zeros_like(acc_ref)
     me = me_ref[0]
@@ -204,7 +204,7 @@
         kern_ref[(part + 1) * width : (part + 2) * width, : 2 * width] = zeros
         kern_ref[part * width : (part + 1) * width, 2 * width * (sources - 1) :] = zeros
 
-    chunk = 16
+    chunk = 32
     sub = lax.broadcasted_iota(jnp.int32, (chunk, width), 0)
     lane = lax.broadcasted_iota(jnp.int32, (chunk, width), 1)
 

time: 52.1 us -> 51.8 us (level)
  no operation moved by 1% of the time
where the time goes in v8:
time: 51.8 us; the launch traced here: 51.6 us
  starting transfers between devices  25.3 us (49%)
  Pallas kernels  23.9 us (46%)
  local copies, waits for them, and re-layouts  1.58 us (3%)
  other arithmetic  0.71 us (1%)
    all_to_all x1, starting transfers between devices, shards(): lax.all_to_all(outgoing, 'azim', split_axis=0, concat_axis=0, tiled=True)  15.1 us
    pallas_call x1, Pallas kernels, run_near_edge(): pl.pallas_call(functools.partial(near_kernel, 0, halo // 2, blocks // 2 -...  8.52 us
    pallas_call x1, Pallas kernels, run_near_inner(): pl.pallas_call(functools.partial(near_kernel, halo // 2, count // 2, 0, F...  8.45 us
    ppermute x1, starting transfers between devices, shards(): right = lax.ppermute(low, 'azim', backward)  6.18 us
    pallas_call x1, Pallas kernels, run_send(): pl.pallas_call(send_kernel, in_specs=smem(2) + vmem(4) + [pl.BlockSpec(me...  4.79 us
    ppermute x3, starting transfers between devices, shards(): others.append(lax.ppermute(pieces[k], 'span', ring))  2.95 us
    pallas_call x1, Pallas kernels, run_receive(): pl.pallas_call(receive_kernel, in_specs=smem(2) + vmem(2), out_specs=vmem...  2.09 us
    unnamed x14, local copies, waits for them, and re-layouts  1.58 us
  transfers between devices with their start and end apart: 6, of which 0 were waited for; matrix products, arithmetic and copies ran while one was open for 0% of the time, Pallas kernels for 37%

profile of v8, /device:TPU:1, one launch (start us, length us, event | category | flops | bytes accessed | tf_op | source)
XLA Modules:
  0.0 51.6 jit_solution(1294655930340245883)
XLA Ops:
  0.0 4.8 %send.1 = (f32[64,8,128]{2,1,0:T(8,128)}, f32[16,24,128]{2,1,0:T(8,128)}, f32[4,24,128]{2,1,0:T(8,128)}, f32[4,24,128]{2,1,0:T(8,128)}) custom-call(s32[2,64]{1,0:T(2,128)} %bitcast.17, s32[1,64]{1,0:T(1,128)} %bitcast.18, f32[256,128]{1,0:T(8,128)} %bitcast.13, f32[3,16,128]{2,1,0:T(8,128)} %pos_ref.1, f32[3,16,128]{2,1,0:T(8,128)} %nrm_ref.1, ...), custom_call_target="tpu_custom_call" | custom-call | flops 3000000000 | bytes 3145728 | tf_op jit(solution)/shard_map/send/pallas_call | solution.py:370
  4.8 15.1 %all-to-all-start = ((f32[64,8,128]{2,1,0:T(8,128)}), f32[64,8,128]{2,1,0:T(8,128)S(1)}, u32[]{:S(2)}, u32[]{:S(2)}) async-start(f32[64,8,128]{2,1,0:T(8,128)} %get-tuple-element.21), calls=%async_computation | async-start | bytes 524288 | tf_op jit(solution)/shard_map/all_to_all | solution.py:466
  19.9 1.1 %collective-permute-start = (f32[4,24,128]{2,1,0:T(8,128)}, f32[4,24,128]{2,1,0:T(8,128)S(1)}, u32[]{:S(2)}, u32[]{:S(2)}) collective-permute-start(f32[4,24,128]{2,1,0:T(8,128)} %get-tuple-element.19), channel_id=1, source_target_pairs={{0,4},{4,8},{8,12},{12,16},{16,20},{20,24},{24,28},{28,32},{32,36}... | collective-permute-start | bytes 147464 | tf_op jit(solution)/shard_map/ppermute | solution.py:469
  21.0 6.2 %collective-permute-start.1 = (f32[4,24,128]{2,1,0:T(8,128)}, f32[4,24,128]{2,1,0:T(8,128)S(1)}, u32[]{:S(2)}, u32[]{:S(2)}) collective-permute-start(f32[4,24,128]{2,1,0:T(8,128)} %get-tuple-element.27), channel_id=1, source_target_pairs={{4,0},{8,4},{12,8},{16,12},{20,16},{24,20},{28,24},{32,28},{36,32}... | collective-permute-start | bytes 147464 | tf_op jit(solution)/shard_map/ppermute | solution.py:470
  27.2 0.0 copy-start.3
  27.2 0.9 %copy-done.3 = f32[16,24,128]{2,1,0:T(8,128)S(1)} copy-done((f32[16,24,128]{2,1,0:T(8,128)S(1)}, f32[16,24,128]{2,1,0:T(8,128)}, u32[]{:S(2)}) %copy-start.3) | copy-done | bytes 196632
  28.1 0.0 copy-start
  28.1 0.0 copy-start.2
  28.1 8.5 %near_inner.1 = (f32[16,8,128]{2,1,0:T(8,128)S(1)}, f32[8,128]{1,0:T(8,128)}) custom-call(f32[16,24,128]{2,1,0:T(8,128)S(1)} %copy-done.3), custom_call_target="tpu_custom_call" | custom-call | flops 10000000000 | bytes 1000000 | tf_op jit(solution)/shard_map/near_inner/pallas_call | solution.py:420
  36.6 0.0 copy-start.5
  36.6 0.6 %copy-done.5 = f32[16,8,128]{2,1,0:T(8,128)} copy-done((f32[16,8,128]{2,1,0:T(8,128)}, f32[16,8,128]{2,1,0:T(8,128)S(1)}, u32[]{:S(2)}) %copy-start.5) | copy-done | bytes 65560
  37.2 0.0 all-to-all-done.coef_ref
  37.2 0.0 copy-done
  37.2 0.0 copy-done.2
  37.2 0.0 copy-start.1
  37.2 0.0 copy-start.4
  37.2 0.0 copy-start.6
  37.3 2.1 %receive.1 = (f32[16,16,128]{2,1,0:T(8,128)S(1)}, f32[16,16,128]{2,1,0:T(8,128)S(1)}, f32[16,16,128]{2,1,0:T(8,128)S(1)}, f32[16,16,128]{2,1,0:T(8,128)S(1)}) custom-call(s32[2,64]{1,0:T(2,128)S(1)} %bitcast.14, s32[1]{0:T(128)} %bitcast.7.me_ref, f32[64,8,128]{2,1,0:T(8,128)S(1)} %all-to-all-done.coef_ref, f32[64,2,2,24,128]{4,3,2,1,0:T(8,128)S(1)} %bitcast.12), custom_call_target="tpu_custom_call" | custom-call | flops 3000000000 | bytes 3145728 | tf_op jit(solution)/shard_map/receive/pallas_call | solution.py:389
  39.4 1.8 %collective-permute-start.2 = (f32[16,16,128]{2,1,0:T(8,128)S(1)}, f32[16,16,128]{2,1,0:T(8,128)S(1)}, u32[]{:S(2)}, u32[]{:S(2)}) collective-permute-start(f32[16,16,128]{2,1,0:T(8,128)S(1)} %get-tuple-element.30), channel_id=1, source_target_pairs={{0,1},{1,2},{2,3},{3,0},{4,5},{5,6},{6,7},{7,4},{8,9},{9,10},{10,1... | collective-permute-start | bytes 393224 | tf_op jit(solution)/shard_map/ppermute | solution.py:482
  41.2 1.1 %collective-permute-start.3 = (f32[16,16,128]{2,1,0:T(8,128)S(1)}, f32[16,16,128]{2,1,0:T(8,128)S(1)}, u32[]{:S(2)}, u32[]{:S(2)}) collective-permute-start(f32[16,16,128]{2,1,0:T(8,128)S(1)} %get-tuple-element.31), channel_id=1, source_target_pairs={{0,2},{1,3},{2,0},{3,1},{4,6},{5,7},{6,4},{7,5},{8,10},{9,11},{10,... | collective-permute-start | bytes 393224 | tf_op jit(solution)/shard_map/ppermute | solution.py:482
  42.3 0.0 collective-permute-start.4
  42.3 0.0 collective-permute-done.refs_0_
  42.3 0.0 collective-permute-done.1.refs_2_
  42.3 0.0 copy-done.1
  42.3 0.0 copy-done.4
  42.3 0.0 copy-done.6
  42.3 8.5 %near_edge.1 = f32[2,8,16,128]{3,2,1,0:T(8,128)S(1)} custom-call(f32[4,24,128]{2,1,0:T(8,128)S(1)} %collective-permute-done.refs_0_, f32[16,24,128]{2,1,0:T(8,128)S(1)} %copy-done.4, f32[4,24,128]{2,1,0:T(8,128)S(1)} %collective-permute-done.1.refs_2_, f32[16,8,128]{2,1,0:T(8,128)S(1)} %copy-done.6, f32[2,8,16,128]{3,2,1,0:T(8,128)S(1)} %copy-done.1), custom_call_target="tpu_custom_call" | custom-call | flops 10000000000 | bytes 1000000 | tf_op jit(solution)/shard_map/near_edge/pallas_call | solution.py:438
  50.9 0.0 collective-permute-done.2
  50.9 0.0 collective-permute-done.3
  50.9 0.0 collective-permute-done.4
  50.9 0.7 %add.15 = f32[2,8,16,128]{3,2,1,0:T(8,128)} add(f32[2,8,16,128]{3,2,1,0:T(8,128)S(1)} %near_edge.1, f32[2,8,16,128]{3,2,1,0:T(8,128)S(1)} %bitcast.15) | non-fusion elementwise | flops 32768 | bytes 393216 | tf_op jit(solution)/shard_map/add | solution.py:486
  (1 shorter events, 0.0 us)
Async XLA Ops:
  4.8 32.4 %all-to-all-start = ((f32[64,8,128]{2,1,0:T(8,128)}), f32[64,8,128]{2,1,0:T(8,128)S(1)}, u32[]{:S(2)}, u32[]{:S(2)}) async-start(f32[64,8,128]{2,1,0:T(8,128)} %get-tuple-element.21), calls=%async_computation | async-start | bytes 524288 | tf_op jit(solution)/shard_map/all_to_all | solution.py:466
  19.9 22.4 %collective-permute-start = (f32[4,24,128]{2,1,0:T(8,128)}, f32[4,24,128]{2,1,0:T(8,128)S(1)}, u32[]{:S(2)}, u32[]{:S(2)}) collective-permute-start(f32[4,24,128]{2,1,0:T(8,128)} %get-tuple-element.19), channel_id=1, source_target_pairs={{0,4},{4,8},{8,12},{12,16},{16,20},{20,24},{24,28},{28,32},{32,36}... | collective-permute-start | bytes 147464 | tf_op jit(solution)/shard_map/ppermute | solution.py:469
  21.0 21.3 %collective-permute-start.1 = (f32[4,24,128]{2,1,0:T(8,128)}, f32[4,24,128]{2,1,0:T(8,128)S(1)}, u32[]{:S(2)}, u32[]{:S(2)}) collective-permute-start(f32[4,24,128]{2,1,0:T(8,128)} %get-tuple-element.27), channel_id=1, source_target_pairs={{4,0},{8,4},{12,8},{16,12},{20,16},{24,20},{28,24},{32,28},{36,32}... | collective-permute-start | bytes 147464 | tf_op jit(solution)/shard_map/ppermute | solution.py:470
  27.2 0.9 %copy-start.3 = (f32[16,24,128]{2,1,0:T(8,128)S(1)}, f32[16,24,128]{2,1,0:T(8,128)}, u32[]{:S(2)}) copy-start(f32[16,24,128]{2,1,0:T(8,128)} %get-tuple-element.26.refs_0_.refs_1_) | copy-start | bytes 589828
  28.1 9.1 %copy-start = (f32[1,1,64,2,2,24,128]{6,5,4,3,2,1,0:T(8,128)S(1)}, f32[1,1,64,2,2,24,128]{6,5,4,3,2,1,0:T(8,128)}, u32[]{:S(2)}) copy-start(f32[1,1,64,2,2,24,128]{6,5,4,3,2,1,0:T(8,128)} %param.17) | copy-start | bytes 9437188
  28.1 9.1 %copy-start.2 = (s32[1,1,64,2]{2,3,1,0:T(2,128)S(1)}, s32[1,1,64,2]{2,3,1,0:T(2,128)}, u32[]{:S(2)}) copy-start(s32[1,1,64,2]{2,3,1,0:T(2,128)} %param.15) | copy-start | bytes 1540
  36.6 0.6 %copy-start.5 = (f32[16,8,128]{2,1,0:T(8,128)}, f32[16,8,128]{2,1,0:T(8,128)S(1)}, u32[]{:S(2)}) copy-start(f32[16,8,128]{2,1,0:T(8,128)S(1)} %get-tuple-element.28.refs_3_) | copy-start | bytes 196612
  37.2 5.1 %copy-start.1 = (f32[2,8,16,128]{3,2,1,0:T(8,128)S(1)}, f32[2,8,16,128]{3,2,1,0:T(8,128)}, u32[]{:S(2)}) copy-start(f32[2,8,16,128]{3,2,1,0:T(8,128)} %refs_4_.1) | copy-start | bytes 393220
  37.2 5.1 %copy-start.4 = (f32[16,24,128]{2,1,0:T(8,128)S(1)}, f32[16,24,128]{2,1,0:T(8,128)}, u32[]{:S(2)}) copy-start(f32[16,24,128]{2,1,0:T(8,128)} %get-tuple-element.26.refs_0_.refs_1_) | copy-start | bytes 589828
  37.2 5.1 %copy-start.6 = (f32[16,8,128]{2,1,0:T(8,128)S(1)}, f32[16,8,128]{2,1,0:T(8,128)}, u32[]{:S(2)}) copy-start(f32[16,8,128]{2,1,0:T(8,128)} %copy-done.5) | copy-start | bytes 196612
  39.4 11.5 %collective-permute-start.2 = (f32[16,16,128]{2,1,0:T(8,128)S(1)}, f32[16,16,128]{2,1,0:T(8,128)S(1)}, u32[]{:S(2)}, u32[]{:S(2)}) collective-permute-start(f32[16,16,128]{2,1,0:T(8,128)S(1)} %get-tuple-element.30), channel_id=1, source_target_pairs={{0,1},{1,2},{2,3},{3,0},{4,5},{5,6},{6,7},{7,4},{8,9},{9,10},{10,1... | collective-permute-start | bytes 393224 | tf_op jit(solution)/shard_map/ppermute | solution.py:482
  41.2 9.7 %collective-permute-start.3 = (f32[16,16,128]{2,1,0:T(8,128)S(1)}, f32[16,16,128]{2,1,0:T(8,128)S(1)}, u32[]{:S(2)}, u32[]{:S(2)}) collective-permute-start(f32[16,16,128]{2,1,0:T(8,128)S(1)} %get-tuple-element.31), channel_id=1, source_target_pairs={{0,2},{1,3},{2,0},{3,1},{4,6},{5,7},{6,4},{7,5},{8,10},{9,11},{10,... | collective-permute-start | bytes 393224 | tf_op jit(solution)/shard_map/ppermute | solution.py:482
  42.3 8.6 %collective-permute-start.4 = (f32[16,16,128]{2,1,0:T(8,128)S(1)}, f32[16,16,128]{2,1,0:T(8,128)S(1)}, u32[]{:S(2)}, u32[]{:S(2)}) collective-permute-start(f32[16,16,128]{2,1,0:T(8,128)S(1)} %get-tuple-element.32), channel_id=1, source_target_pairs={{0,3},{1,0},{2,1},{3,2},{4,7},{5,4},{6,5},{7,6},{8,11},{9,8},{10,9... | collective-permute-start | bytes 393224 | tf_op jit(solution)/shard_map/ppermute | solution.py:482
